TPU v7x, 32 devices: a whole 2x2x4 slice. The times are simulated.
32 devices in a mesh: dp: 8 (over z, x), tensor: 4 (over y, core).
Axes of the slice: x: 2, y: 2, z: 4, core: 2. Of those that a mesh axis runs over, the one named last changes fastest.
Arguments:
- latent: bfloat16 [8, 16, 1280, 128], P('dp', None, 'tensor'), may hold values from -6 to 6
- clip_flags: int32 [8], P('dp'), may hold values 0 or 1
- cotangent: bfloat16 [8, 16, 1280, 128], P('dp', None, 'tensor'), may hold values from -6 to 6
- norm_gain: float32 [4, 1280], P(None, 'tensor'), may hold values from 0.5 to 1.5
- norm_shift: float32 [4, 1280], P(None, 'tensor'), may hold values from -3 to 3
- channel_bias: float32 [5, 1280], P(None, 'tensor'), may hold values from -3 to 3
- hidden_bias: float32 [5120], P('tensor'), may hold values from -3 to 3
- weight_in: bfloat16 [1280, 1280], P('dp', 'tensor'), may hold values from -0.15625 to 0.15625
- weight_qkv: bfloat16 [2, 1280, 3, 1280], P(None, 'dp', None, 'tensor'), may hold values from -0.15625 to 0.15625
- weight_out: bfloat16 [2, 1280, 1280], P(None, 'tensor', 'dp'), may hold values from -0.5 to 0.5
- weight_up: bfloat16 [1280, 5120], P('dp', 'tensor'), may hold values from -0.15625 to 0.15625
- weight_down: bfloat16 [5120, 1280], P('tensor', 'dp'), may hold values from -0.078125 to 0.078125
- weight_proj: bfloat16 [1280, 1280], P('dp', 'tensor'), may hold values from -0.15625 to 0.15625
Outputs:
- output: bfloat16 [8, 16, 1280, 128], P('dp', None, 'tensor')
- latent_grad: float32 [8, 16, 1280, 128], P('dp', None, 'tensor')
- gain_grad: float32 [4, 1280], P(None, 'tensor')
- shift_grad: float32 [4, 1280], P(None, 'tensor')
- channel_bias_grad: float32 [5, 1280], P(None, 'tensor')
- hidden_bias_grad: float32 [5120], P('tensor')
- weight_in_grad: float32 [1280, 1280], P('dp', 'tensor')
- weight_qkv_grad: float32 [2, 1280, 3, 1280], P(None, 'dp', None, 'tensor')
- weight_out_grad: float32 [2, 1280, 1280], P(None, 'tensor', 'dp')
- weight_up_grad: float32 [1280, 5120], P('dp', 'tensor')
- weight_down_grad: float32 [5120, 1280], P('tensor', 'dp')
- weight_proj_grad: float32 [1280, 1280], P('dp', 'tensor')
Inputs may be any that keep to these rules, and one draw needn't show every extreme that they name: `clip_flags`: 1 marks a slot holding one clip of 16 frames, 0 a slot of 16 unrelated still images that bypass the module.
All inputs are finite; a program needn't handle non-finite values. No bound on the sum of `clip_flags` on one device may be relied on, other than what follows from the above.
Results may differ from a plain program's by a relative error of at most 0.025.
Values may be sent and summed in bfloat16 or wider, within the bound.
A program may use at most 256 MiB of HBM per device.

v0:
```python
from functools import partial
import math

import jax
import jax.numpy as jnp
from jax import lax
from jax.sharding import PartitionSpec as P

C = 1280
GROUPS = 32
FRAMES = 16
HEAD = 160


def product(left_side, right_side):
    return jnp.dot(left_side, right_side, preferred_element_type=jnp.float32)


def inner(left_side, right_side):
    return lax.dot_general(
        left_side, right_side, (((0,), (0,)), ((), ())), preferred_element_type=jnp.float32
    )


def contract_last(left_side, right_side):
    return lax.dot_general(
        left_side, right_side, (((1,), (1,)), ((), ())), preferred_element_type=jnp.float32
    )


def to_rows(values):
    slot_count, frame_count, local_width, pixel_count = values.shape
    return jnp.transpose(values, (0, 1, 3, 2)).reshape(
        slot_count * frame_count * pixel_count, local_width
    )


def from_rows(values, slot_count, pixel_count):
    local_width = values.shape[1]
    return jnp.transpose(values.reshape(slot_count, FRAMES, pixel_count, local_width), (0, 1, 3, 2))


def gather_columns(values):
    return lax.all_gather(values, "tensor", axis=1, tiled=True)


def scatter_forward(partial_terms):
    return lax.psum_scatter(
        partial_terms.astype(jnp.bfloat16), "tensor", scatter_dimension=1, tiled=True
    ).astype(jnp.float32)


def gather_gradient(values):
    return lax.all_gather(values, "tensor", axis=1, tiled=True)


def scatter_backward(partial_terms):
    return lax.psum_scatter(
        partial_terms.astype(jnp.bfloat16), "tensor", scatter_dimension=1, tiled=True
    ).astype(jnp.float32)


def make_positions(channel_ids):
    pair_rate = jnp.exp((channel_ids // 2).astype(jnp.float32) * (-2.0 * math.log(10000.0) / C))
    angles = jnp.arange(FRAMES).astype(jnp.float32)[:, None] * pair_rate[None, :]
    return jnp.where(channel_ids[None, :] % 2 == 0, jnp.sin(angles), jnp.cos(angles))


def layer_stats(stream):
    centre = lax.psum(jnp.sum(stream, 1), "tensor") / C
    offset = stream - centre[:, None]
    spread = lax.psum(jnp.sum(offset * offset, 1), "tensor") / C
    inverse = lax.rsqrt(spread + 1e-05)
    return ((stream - centre[:, None]) * inverse[:, None], inverse)


def layer_back(grad_out, normal_part, inverse, gain):
    scaled = grad_out * gain
    first, second = lax.psum((jnp.sum(scaled, 1), jnp.sum(scaled * normal_part, 1)), "tensor")
    grad_in = inverse[:, None] * (scaled - first[:, None] / C - normal_part * second[:, None] / C)
    return (grad_in, jnp.sum(grad_out * normal_part, 0), jnp.sum(grad_out, 0))


def group_forward(stream, slot_count):
    rows_all, local_width = stream.shape
    group_width = C // GROUPS
    grouped = stream.reshape(
        slot_count, rows_all // slot_count, local_width // group_width, group_width
    )
    centre = jnp.mean(grouped, axis=(1, 3), keepdims=True)
    offset = grouped - centre
    inverse = lax.rsqrt(jnp.mean(offset * offset, axis=(1, 3), keepdims=True) + 1e-06)
    return (offset * inverse, inverse)


def group_backward(grad_out, normal_part, inverse, gain):
    scaled = (grad_out * gain).reshape(normal_part.shape)
    first = jnp.mean(scaled, axis=(1, 3), keepdims=True)
    second = jnp.mean(scaled * normal_part, axis=(1, 3), keepdims=True)
    grad_in = (inverse * (scaled - first - normal_part * second)).reshape(grad_out.shape)
    flat_hat = normal_part.reshape(grad_out.shape)
    return (grad_in, jnp.sum(grad_out * flat_hat, 0), jnp.sum(grad_out, 0))


def body(
    latent,
    clip_flags,
    cotangent,
    norm_gain,
    norm_shift,
    channel_bias,
    hidden_bias,
    weight_in,
    weight_qkv,
    weight_out,
    weight_up,
    weight_down,
    weight_proj,
):
    slot_count = clip_flags.shape[0]
    pixel_count = latent.shape[3]
    start = to_rows(latent.astype(jnp.float32))
    rows_all, local_width = start.shape
    heads_local = local_width // HEAD
    score_scale = 1.0 / math.sqrt(HEAD)
    sharded = (weight_in, weight_qkv, weight_out, weight_up, weight_down, weight_proj)
    full_in, full_qkv, full_out, full_up, full_down, full_proj = (
        lax.all_gather(sharded[0], "dp", axis=0, tiled=True),
        lax.all_gather(sharded[1], "dp", axis=1, tiled=True),
        lax.all_gather(sharded[2], "dp", axis=2, tiled=True),
        lax.all_gather(sharded[3], "dp", axis=0, tiled=True),
        lax.all_gather(sharded[4], "dp", axis=1, tiled=True),
        lax.all_gather(sharded[5], "dp", axis=0, tiled=True),
    )
    column_start = lax.axis_index("tensor") * local_width

    def to_heads(values):
        return values.reshape(slot_count, FRAMES, pixel_count, heads_local, HEAD)

    group_hat, group_inverse = group_forward(start, slot_count)
    normed = group_hat.reshape(start.shape) * norm_gain[0] + norm_shift[0]
    inputs_in = gather_columns(normed.astype(jnp.bfloat16))
    kept_blocks = []
    stream = product(inputs_in, full_in) + channel_bias[0]
    channel_ids = column_start + jnp.arange(local_width, dtype=jnp.int32)
    position_table = make_positions(channel_ids)
    for sub_block in range(2):
        hat_layer, inverse_layer = layer_stats(stream)
        lifted = hat_layer * norm_gain[1 + sub_block] + norm_shift[1 + sub_block]
        lifted = (
            lifted.reshape(slot_count, FRAMES, pixel_count, local_width)
            + position_table[None, :, None, :]
        ).reshape(rows_all, local_width)
        inputs_qkv = gather_columns(lifted.astype(jnp.bfloat16))
        attend_flat_qkv = full_qkv[sub_block].reshape(full_qkv.shape[1], 3 * local_width)
        projected = (
            product(inputs_qkv, attend_flat_qkv)
            .astype(jnp.bfloat16)
            .reshape(rows_all, 3, local_width)
        )
        query_heads = to_heads(projected[:, 0])
        key_heads = to_heads(projected[:, 1])
        value_heads = to_heads(projected[:, 2])
        scores = (
            jnp.einsum(
                "sfphd,sgphd->sphfg", query_heads, key_heads, preferred_element_type=jnp.float32
            )
            * score_scale
        )
        attention_probs = jax.nn.softmax(scores, axis=-1)
        probs_low = attention_probs.astype(jnp.bfloat16)
        attended = jnp.einsum(
            "sphfg,sgphd->sfphd", probs_low, value_heads, preferred_element_type=jnp.float32
        )
        flat_attended = attended.astype(jnp.bfloat16).reshape(rows_all, local_width)
        query_heads, key_heads, value_heads, attention_probs, probs_low, flat_attended = (
            query_heads,
            key_heads,
            value_heads,
            attention_probs,
            probs_low,
            flat_attended,
        )
        stream = stream + (
            scatter_forward(product(flat_attended, full_out[sub_block]))
            + channel_bias[1 + sub_block]
        )
        kept_blocks.append(
            (
                hat_layer,
                inverse_layer,
                inputs_qkv,
                query_heads,
                key_heads,
                value_heads,
                attention_probs,
                probs_low,
                flat_attended,
            )
        )
    hat_feed, inverse_feed = layer_stats(stream)
    inputs_up = gather_columns((hat_feed * norm_gain[3] + norm_shift[3]).astype(jnp.bfloat16))
    pre_act = product(inputs_up, full_up) + hidden_bias
    hidden = jax.nn.gelu(pre_act, approximate=False).astype(jnp.bfloat16)
    stream = stream + (scatter_forward(product(hidden, full_down)) + channel_bias[3])
    inputs_proj = gather_columns(stream.astype(jnp.bfloat16))
    projected_out = product(inputs_proj, full_proj) + channel_bias[4]
    flag_rows = jnp.broadcast_to(
        (clip_flags > 0)[:, None], (slot_count, FRAMES * pixel_count)
    ).reshape(rows_all, 1)
    output = from_rows(
        jnp.where(flag_rows, start + projected_out, start), slot_count, pixel_count
    ).astype(jnp.bfloat16)
    full_in, full_qkv, full_out, full_up, full_down, full_proj = (
        lax.all_gather(sharded[0], "dp", axis=0, tiled=True),
        lax.all_gather(sharded[1], "dp", axis=1, tiled=True),
        lax.all_gather(sharded[2], "dp", axis=2, tiled=True),
        lax.all_gather(sharded[3], "dp", axis=0, tiled=True),
        lax.all_gather(sharded[4], "dp", axis=1, tiled=True),
        lax.all_gather(sharded[5], "dp", axis=0, tiled=True),
    )
    bias_grads = [None] * 5
    gain_grads = [None] * 4
    shift_grads = [None] * 4
    qkv_grads = [None, None]
    out_grads = [None, None]
    cotangent_float = to_rows(cotangent.astype(jnp.float32))
    grad_moved = jnp.where(flag_rows, cotangent_float, 0.0)
    bias_grads[4] = jnp.sum(grad_moved, 0)
    grad_low = grad_moved.astype(jnp.bfloat16)
    grad_proj = inner(inputs_proj, grad_low)
    grad_stream = scatter_backward(contract_last(grad_low, full_proj))
    bias_grads[3] = jnp.sum(grad_stream, 0)
    grad_full = gather_gradient(grad_stream.astype(jnp.bfloat16))
    grad_down = inner(hidden, grad_full)
    grad_hidden = contract_last(grad_full, full_down)
    unused, gelu_pull = jax.vjp(partial(jax.nn.gelu, approximate=False), pre_act)
    grad_pre = gelu_pull(grad_hidden)[0]
    hidden_bias_grad = jnp.sum(grad_pre, 0)
    grad_pre_low = grad_pre.astype(jnp.bfloat16)
    grad_up = inner(inputs_up, grad_pre_low)
    grad_normed = scatter_backward(contract_last(grad_pre_low, full_up))
    grad_layer, gain_grads[3], shift_grads[3] = layer_back(
        grad_normed, hat_feed, inverse_feed, norm_gain[3]
    )
    grad_stream = grad_stream + grad_layer
    for sub_block in (1, 0):
        (
            hat_layer,
            inverse_layer,
            inputs_qkv,
            query_heads,
            key_heads,
            value_heads,
            attention_probs,
            probs_low,
            flat_attended,
        ) = kept_blocks[sub_block]
        bias_grads[1 + sub_block] = jnp.sum(grad_stream, 0)
        grad_full = gather_gradient(grad_stream.astype(jnp.bfloat16))
        out_grads[sub_block] = inner(flat_attended, grad_full)
        grad_attended = to_heads(contract_last(grad_full, full_out[sub_block]).astype(jnp.bfloat16))
        grad_probs = jnp.einsum(
            "sfphd,sgphd->sphfg", grad_attended, value_heads, preferred_element_type=jnp.float32
        )
        grad_values = jnp.einsum(
            "sphfg,sfphd->sgphd", probs_low, grad_attended, preferred_element_type=jnp.float32
        )
        centred = jnp.sum(attention_probs * grad_probs, -1, keepdims=True)
        grad_raw = (attention_probs * (grad_probs - centred) * score_scale).astype(jnp.bfloat16)
        grad_queries = jnp.einsum(
            "sphfg,sgphd->sfphd", grad_raw, key_heads, preferred_element_type=jnp.float32
        )
        grad_keys = jnp.einsum(
            "sphfg,sfphd->sgphd", grad_raw, query_heads, preferred_element_type=jnp.float32
        )
        stacked = jnp.stack(
            [
                grad_queries.reshape(rows_all, local_width),
                grad_keys.reshape(rows_all, local_width),
                grad_values.reshape(rows_all, local_width),
            ],
            1,
        )
        stacked = stacked.astype(jnp.bfloat16).reshape(rows_all, 3 * local_width)
        qkv_grads[sub_block] = inner(inputs_qkv, stacked).reshape(
            inputs_qkv.shape[1], 3, local_width
        )
        flat_qkv = full_qkv[sub_block].reshape(full_qkv.shape[1], 3 * local_width)
        grad_lifted = scatter_backward(contract_last(stacked, flat_qkv))
        grad_layer, gain_grads[1 + sub_block], shift_grads[1 + sub_block] = layer_back(
            grad_lifted, hat_layer, inverse_layer, norm_gain[1 + sub_block]
        )
        grad_stream = grad_stream + grad_layer
    bias_grads[0] = jnp.sum(grad_stream, 0)
    grad_low = grad_stream.astype(jnp.bfloat16)
    grad_in = inner(inputs_in, grad_low)
    grad_normed = scatter_backward(contract_last(grad_low, full_in))
    grad_group, gain_grads[0], shift_grads[0] = group_backward(
        grad_normed, group_hat, group_inverse, norm_gain[0]
    )
    latent_grad = from_rows(cotangent_float + grad_group, slot_count, pixel_count)
    local_grads = (
        grad_in,
        jnp.stack(qkv_grads, 0),
        jnp.stack(out_grads, 0),
        grad_up,
        grad_down,
        grad_proj,
    )
    (
        weight_in_grad,
        weight_qkv_grad,
        weight_out_grad,
        weight_up_grad,
        weight_down_grad,
        weight_proj_grad,
    ) = (
        lax.psum_scatter(
            local_grads[0].astype(jnp.bfloat16), "dp", scatter_dimension=0, tiled=True
        ).astype(jnp.float32),
        lax.psum_scatter(
            local_grads[1].astype(jnp.bfloat16), "dp", scatter_dimension=1, tiled=True
        ).astype(jnp.float32),
        lax.psum_scatter(
            local_grads[2].astype(jnp.bfloat16), "dp", scatter_dimension=2, tiled=True
        ).astype(jnp.float32),
        lax.psum_scatter(
            local_grads[3].astype(jnp.bfloat16), "dp", scatter_dimension=0, tiled=True
        ).astype(jnp.float32),
        lax.psum_scatter(
            local_grads[4].astype(jnp.bfloat16), "dp", scatter_dimension=1, tiled=True
        ).astype(jnp.float32),
        lax.psum_scatter(
            local_grads[5].astype(jnp.bfloat16), "dp", scatter_dimension=0, tiled=True
        ).astype(jnp.float32),
    )
    gain_grad, shift_grad, channel_bias_grad, hidden_bias_total = lax.psum(
        (
            jnp.stack(gain_grads, 0),
            jnp.stack(shift_grads, 0),
            jnp.stack(bias_grads, 0),
            hidden_bias_grad,
        ),
        "dp",
    )
    return (
        output,
        latent_grad,
        gain_grad,
        shift_grad,
        channel_bias_grad,
        hidden_bias_total,
        weight_in_grad,
        weight_qkv_grad,
        weight_out_grad,
        weight_up_grad,
        weight_down_grad,
        weight_proj_grad,
    )


def solution(mesh):
    placed = (
        P("dp", None, "tensor", None),
        P("dp"),
        P("dp", None, "tensor", None),
        P(None, "tensor"),
        P(None, "tensor"),
        P(None, "tensor"),
        P("tensor"),
        P("dp", "tensor"),
        P(None, "dp", None, "tensor"),
        P(None, "tensor", "dp"),
        P("dp", "tensor"),
        P("tensor", "dp"),
        P("dp", "tensor"),
    )
    return jax.shard_map(
        body,
        mesh=mesh,
        in_specs=placed,
        out_specs=(
            P("dp", None, "tensor", None),
            P("dp", None, "tensor", None),
            P(None, "tensor"),
            P(None, "tensor"),
            P(None, "tensor"),
            P("tensor"),
            P("dp", "tensor"),
            P(None, "dp", None, "tensor"),
            P(None, "tensor", "dp"),
            P("dp", "tensor"),
            P("tensor", "dp"),
            P("dp", "tensor"),
        ),
        check_vma=False,
    )
```

profile of v0, /device:TPU:0, one launch (start us, length us, event | category | flops | bytes accessed | tf_op | source)
XLA Modules:
  0.0 1876.0 jit_solution(12052657378615411589)
XLA Ops:
  23.1 36.4 %all_gather.49 = bf16[1280,320]{1,0:T(8,128)(2,1)} all-gather(bf16[160,320]{1,0:T(8,128)(2,1)S(1)} %copy-done.44), channel_id=1, replica_groups=mesh['dp'=8,'tensor'=4] {'dp'}, dimensions={0}, use_global_device_ids=true | all-gather | bytes 921600 | tf_op jit(solution)/shard_map/all_gather | solution.py:128
  86.0 74.5 %all-gather.17.cloned.1.call-done = bf16[2,1280,3,320]{3,0,2,1:T(2,128)(2,1)} async-done(((bf16[2,160,3,320]{3,0,2,1:T(2,128)(2,1)}), bf16[2,1280,3,320]{3,0,2,1:T(2,128)(2,1)}) %all-gather.17.cloned.1.call-update) | async-done | bytes 4915216 | tf_op jit(solution)/shard_map/all_gather | solution.py:129
  184.9 16.4 all-gather.15.cloned.1.call-done
  257.0 50.6 %reduce-scatter.13.cloned.1.call-done = bf16[2048,320]{0,1:T(8,128)(2,1)} async-done(((bf16[2048,1280]{0,1:T(8,128)(2,1)}), bf16[2048,320]{0,1:T(8,128)(2,1)}) %reduce-scatter.13.cloned.1.call-update) | async-done | bytes 1310736 | tf_op jit(solution)/shard_map/reduce_scatter | solution.py:48
  339.3 29.4 %all-gather.21.cloned.1.call-done = bf16[2048,1280]{0,1:T(8,128)(2,1)} async-done(((bf16[2048,320]{0,1:T(8,128)(2,1)}), bf16[2048,1280]{0,1:T(8,128)(2,1)}) %all-gather.21.cloned.1.call-update) | async-done | bytes 5242896 | tf_op jit(solution)/shard_map/all_gather | solution.py:44
  423.8 33.1 %all_gather.58 = bf16[1280,320]{1,0:T(8,128)(2,1)S(1)} all-gather(bf16[160,320]{1,0:T(8,128)(2,1)S(1)} %copy-done.45), channel_id=1, replica_groups=mesh['dp'=8,'tensor'=4] {'dp'}, dimensions={0}, use_global_device_ids=true | all-gather | bytes 921600 | tf_op jit(solution)/shard_map/all_gather | solution.py:133
  491.4 34.1 %reduce-scatter.19.cloned.1.call-done = bf16[2048,320]{0,1:T(8,128)(2,1)} async-done(((bf16[2048,1280]{0,1:T(8,128)(2,1)}), bf16[2048,320]{0,1:T(8,128)(2,1)}) %reduce-scatter.19.cloned.1.call-update) | async-done | bytes 1310736 | tf_op jit(solution)/shard_map/reduce_scatter | solution.py:58
  525.6 64.3 %all-gather.25.cloned.1.call-done = bf16[1280,1280]{1,0:T(8,128)(2,1)} async-done(((bf16[160,1280]{1,0:T(8,128)(2,1)}), bf16[1280,1280]{1,0:T(8,128)(2,1)}) %all-gather.25.cloned.1.call-update) | async-done | bytes 3276816 | tf_op jit(solution)/shard_map/all_gather | solution.py:131
  590.0 41.1 %all-gather.23.cloned.1.call-done = bf16[2048,1280]{0,1:T(8,128)(2,1)} async-done(((bf16[2048,320]{0,1:T(8,128)(2,1)}), bf16[2048,1280]{0,1:T(8,128)(2,1)}) %all-gather.23.cloned.1.call-update) | async-done | bytes 5242896 | tf_op jit(solution)/shard_map/all_gather | solution.py:44
  643.4 52.1 %all-gather.27.cloned.1.call-done = bf16[1280,1280]{0,1:T(8,128)(2,1)} async-done(((bf16[1280,160]{0,1:T(8,128)(2,1)}), bf16[1280,1280]{0,1:T(8,128)(2,1)}) %all-gather.27.cloned.1.call-update) | async-done | bytes 3276816 | tf_op jit(solution)/shard_map/all_gather | solution.py:132
  695.5 40.5 %all-gather.31.cloned.1.call-done = bf16[2048,1280]{0,1:T(8,128)(2,1)} async-done(((bf16[2048,320]{0,1:T(8,128)(2,1)}), bf16[2048,1280]{0,1:T(8,128)(2,1)}) %all-gather.31.cloned.1.call-update) | async-done | bytes 5242896 | tf_op jit(solution)/shard_map/all_gather | solution.py:54
  736.0 37.7 %fusion.134 = (f32[1280]{0:T(1024)}, bf16[2048,1280]{1,0:T(8,128)(2,1)S(1)}, f32[2048,1280]{1,0:T(8,128)}) fusion(f32[2048,1280]{1,0:T(8,128)} %fusion.151, f32[1280]{0:T(1024)S(1)} %copy-done.56, bf16[2048,1280]{0,1:T(8,128)(2,1)} %all-gather.31.cloned.1.call-done, bf16[1280,1280]{0,1:T(8,128)(2,1)} %all-gather.27.cloned.1.call-done), kind=kOutput, calls=%fused_computation.242 | convolution fusion | flops 6904871936 | bytes 34744320 | tf_op jit(solution)/shard_map/dot_general | solution.py:26
  805.0 31.3 %reduce-scatter.21.cloned.1.call-done = bf16[2048,320]{0,1:T(8,128)(2,1)} async-done(((bf16[2048,1280]{0,1:T(8,128)(2,1)}), bf16[2048,320]{0,1:T(8,128)(2,1)}) %reduce-scatter.21.cloned.1.call-update) | async-done | bytes 1310736 | tf_op jit(solution)/shard_map/reduce_scatter | solution.py:58
  849.6 40.5 %reduce-scatter.17.cloned.1.call-done = bf16[2048,320]{0,1:T(8,128)(2,1)} async-done(((bf16[2048,1280]{0,1:T(8,128)(2,1)}), bf16[2048,320]{0,1:T(8,128)(2,1)}) %reduce-scatter.17.cloned.1.call-update) | async-done | bytes 1310736 | tf_op jit(solution)/shard_map/reduce_scatter | solution.py:48
  898.3 40.5 %all-gather.33.cloned.1.call-done = bf16[2048,1280]{0,1:T(8,128)(2,1)} async-done(((bf16[2048,320]{0,1:T(8,128)(2,1)}), bf16[2048,1280]{0,1:T(8,128)(2,1)}) %all-gather.33.cloned.1.call-update) | async-done | bytes 5242896 | tf_op jit(solution)/shard_map/all_gather | solution.py:54
  994.4 51.3 %reduce-scatter.23.cloned.1.call-done = bf16[2048,320]{0,1:T(8,128)(2,1)} async-done(((bf16[2048,1280]{0,1:T(8,128)(2,1)}), bf16[2048,320]{0,1:T(8,128)(2,1)}) %reduce-scatter.23.cloned.1.call-update) | async-done | bytes 1310736 | tf_op jit(solution)/shard_map/reduce_scatter | solution.py:58
  1065.2 41.0 %all-gather.35.cloned.1.call-done = bf16[2048,1280]{0,1:T(8,128)(2,1)} async-done(((bf16[2048,320]{0,1:T(8,128)(2,1)}), bf16[2048,1280]{0,1:T(8,128)(2,1)}) %all-gather.35.cloned.1.call-update) | async-done | bytes 5242896 | tf_op jit(solution)/shard_map/all_gather | solution.py:54
  1230.0 17.7 copy.234
  1298.6 77.2 %reduce-scatter.33.cloned.1.call-done = bf16[1280,160]{0,1:T(8,128)(2,1)} async-done(((bf16[1280,1280]{0,1:T(8,128)(2,1)}), bf16[1280,160]{0,1:T(8,128)(2,1)}) %reduce-scatter.33.cloned.1.call-update) | async-done | bytes 409616 | tf_op jit(solution)/shard_map/reduce_scatter | solution.py:331
  1384.9 57.6 %reduce-scatter.35.cloned.1.call-done = bf16[160,320]{1,0:T(8,128)(2,1)} async-done(((bf16[1280,320]{1,0:T(8,128)(2,1)}), bf16[160,320]{1,0:T(8,128)(2,1)}) %reduce-scatter.35.cloned.1.call-update) | async-done | bytes 102416 | tf_op jit(solution)/shard_map/reduce_scatter | solution.py:334
  1444.2 257.5 %all-reduce.9.cloned.1.call-done = (bf16[2,1280,3,320]{3,0,2,1:T(2,128)(2,1)}, bf16[2,320,1280]{1,0,2:T(2,128)(2,1)}) async-done(((bf16[2,1280,3,320]{3,0,2,1:T(2,128)(2,1)}, bf16[2,320,1280]{1,0,2:T(2,128)(2,1)}), (bf16[2,1280,3,320]{3,0,2,1:T(2,128)(2,1)}, bf16[2,320,1280]{1,0,2:T(2,128)(2,1)})) %all-reduce.9.cloned.1.call-update) | async-done | bytes 6553616
  1706.5 61.4 %reduce-scatter.29.cloned.1.call-done = bf16[160,320]{1,0:T(8,128)(2,1)} async-done(((bf16[1280,320]{1,0:T(8,128)(2,1)}), bf16[160,320]{1,0:T(8,128)(2,1)}) %reduce-scatter.29.cloned.1.call-update) | async-done | bytes 102416 | tf_op jit(solution)/shard_map/reduce_scatter | solution.py:319
  1769.5 51.5 %reduce-scatter.27.cloned.1.call-done = bf16[2048,320]{0,1:T(8,128)(2,1)} async-done(((bf16[2048,1280]{0,1:T(8,128)(2,1)}), bf16[2048,320]{0,1:T(8,128)(2,1)}) %reduce-scatter.27.cloned.1.call-update) | async-done | bytes 1310736 | tf_op jit(solution)/shard_map/reduce_scatter | solution.py:58
  1831.5 37.7 %all-reduce.2 = (f32[4,320]{1,0:T(4,128)}, f32[4,320]{1,0:T(4,128)}, f32[5,320]{1,0:T(8,128)}, f32[1280]{0:T(1024)}) all-reduce(f32[4,320]{1,0:T(4,128)S(1)} %get-tuple-element.154, f32[4,320]{1,0:T(4,128)S(1)} %get-tuple-element.155, f32[5,320]{1,0:T(8,128)S(1)} %stack.87, ...), channel_id=1, replica_groups=mesh['dp'=8,'tensor'=4] {'dp'}, use_global_device_ids=true, to_apply=%region_50.51 | all-reduce | flops 5440 | bytes 43520 | tf_op jit(solution)/shard_map/psum | solution.py:338
  (394 shorter events, 583.5 us)
Async XLA Ops:
  20.2 140.3 %all-gather.17.cloned.1.call-start = ((), (), s32[]{:S(2)}) async-start(), calls=%async_computation.14 | async-start | bytes 6635520 | tf_op jit(solution)/shard_map/all_gather | solution.py:129
  21.7 179.6 %all-gather.15.cloned.1.call-start = ((), (), s32[]{:S(2)}) async-start(), calls=%async_computation.13 | async-start | bytes 6553600 | tf_op jit(solution)/shard_map/all_gather | solution.py:44
  85.2 165.7 %all-gather.19.cloned.1.call-start = ((), (), s32[]{:S(2)}) async-start(), calls=%async_computation.15 | async-start | bytes 2211840 | tf_op jit(solution)/shard_map/all_gather | solution.py:130
  85.7 221.9 %reduce-scatter.13.cloned.1.call-start = ((), (), s32[]{:S(2)}) async-start(), calls=%async_computation.16 | async-start | bytes 6553600 | tf_op jit(solution)/shard_map/reduce_scatter | solution.py:48
  257.0 111.7 %all-gather.21.cloned.1.call-start = ((), (), s32[]{:S(2)}) async-start(), calls=%async_computation.17 | async-start | bytes 6553600 | tf_op jit(solution)/shard_map/all_gather | solution.py:44
  326.7 144.9 %reduce-scatter.15.cloned.1.call-start = ((), (), s32[]{:S(2)}) async-start(), calls=%async_computation.18 | async-start | bytes 6553600 | tf_op jit(solution)/shard_map/reduce_scatter | solution.py:48
  420.0 105.5 %reduce-scatter.19.cloned.1.call-start = ((), (), s32[]{:S(2)}) async-start(), calls=%async_computation.24 | async-start | bytes 6553600 | tf_op jit(solution)/shard_map/reduce_scatter | solution.py:58
  463.2 126.7 %all-gather.25.cloned.1.call-start = ((), (), s32[]{:S(2)}) async-start(), calls=%async_computation.20 | async-start | bytes 3686400 | tf_op jit(solution)/shard_map/all_gather | solution.py:131
  464.0 167.1 %all-gather.23.cloned.1.call-start = ((), (), s32[]{:S(2)}) async-start(), calls=%async_computation.19 | async-start | bytes 6553600 | tf_op jit(solution)/shard_map/all_gather | solution.py:44
  490.7 204.8 %all-gather.27.cloned.1.call-start = ((), (), s32[]{:S(2)}) async-start(), calls=%async_computation.21 | async-start | bytes 3686400 | tf_op jit(solution)/shard_map/all_gather | solution.py:132
  491.4 244.6 %all-gather.31.cloned.1.call-start = ((), (), s32[]{:S(2)}) async-start(), calls=%async_computation.25 | async-start | bytes 6553600 | tf_op jit(solution)/shard_map/all_gather | solution.py:54
  525.6 310.7 %reduce-scatter.21.cloned.1.call-start = ((), (), s32[]{:S(2)}) async-start(), calls=%async_computation.26 | async-start | bytes 6553600 | tf_op jit(solution)/shard_map/reduce_scatter | solution.py:58
  784.7 105.4 %reduce-scatter.17.cloned.1.call-start = ((), (), s32[]{:S(2)}) async-start(), calls=%async_computation.22 | async-start | bytes 6553600 | tf_op jit(solution)/shard_map/reduce_scatter | solution.py:48
  804.9 134.0 %all-gather.33.cloned.1.call-start = ((), (), s32[]{:S(2)}) async-start(), calls=%async_computation.27 | async-start | bytes 6553600 | tf_op jit(solution)/shard_map/all_gather | solution.py:54
  898.3 147.4 %reduce-scatter.23.cloned.1.call-start = ((), (), s32[]{:S(2)}) async-start(), calls=%async_computation.28 | async-start | bytes 6553600 | tf_op jit(solution)/shard_map/reduce_scatter | solution.py:58
  994.2 112.0 %all-gather.35.cloned.1.call-start = ((), (), s32[]{:S(2)}) async-start(), calls=%async_computation.29 | async-start | bytes 6553600 | tf_op jit(solution)/shard_map/all_gather | solution.py:54
  1064.6 124.1 %all-gather.29.cloned.1.call-start = ((), (), s32[]{:S(2)}) async-start(), calls=%async_computation.23 | async-start | bytes 6553600 | tf_op jit(solution)/shard_map/all_gather | solution.py:44
  1065.2 182.6 %reduce-scatter.25.cloned.1.call-start = ((), (), s32[]{:S(2)}) async-start(), calls=%async_computation.30 | async-start | bytes 6553600 | tf_op jit(solution)/shard_map/reduce_scatter | solution.py:58
  1164.8 131.9 %reduce-scatter.31.cloned.1.call-start = ((), (), s32[]{:S(2)}) async-start(), calls=%async_computation.33 | async-start | bytes 3686400 | tf_op jit(solution)/shard_map/reduce_scatter | solution.py:328
  1176.8 199.0 %reduce-scatter.33.cloned.1.call-start = ((), (), s32[]{:S(2)}) async-start(), calls=%async_computation.34 | async-start | bytes 3686400 | tf_op jit(solution)/shard_map/reduce_scatter | solution.py:331
  1188.6 253.9 %reduce-scatter.35.cloned.1.call-start = ((), (), s32[]{:S(2)}) async-start(), calls=%async_computation.35 | async-start | bytes 1105920 | tf_op jit(solution)/shard_map/reduce_scatter | solution.py:334
  1196.7 504.9 %all-reduce.9.cloned.1.call-start = ((), (), s32[]{:S(2)}) async-start(), calls=%async_computation.36 | async-start | bytes 15728640
  1247.7 520.2 %reduce-scatter.29.cloned.1.call-start = ((), (), s32[]{:S(2)}) async-start(), calls=%async_computation.32 | async-start | bytes 1105920 | tf_op jit(solution)/shard_map/reduce_scatter | solution.py:319
  1274.4 546.7 %reduce-scatter.27.cloned.1.call-start = ((), (), s32[]{:S(2)}) async-start(), calls=%async_computation.31 | async-start | bytes 6553600 | tf_op jit(solution)/shard_map/reduce_scatter | solution.py:58
  (81 other events, 2458.8 us)
Sparse Core Ops, SparseCore 0:
  20.3 43.1 all-gather.12
  66.2 94.2 all-gather.16
  203.3 47.5 all-gather.18
  257.1 50.4 reduce-scatter.12
  326.8 41.8 all-gather.20
  420.1 51.3 reduce-scatter.14
  474.1 51.3 reduce-scatter.18
  528.0 61.9 all-gather.24
  592.0 39.0 all-gather.22
  633.5 61.9 all-gather.26
  697.0 39.0 all-gather.30
  784.8 51.3 reduce-scatter.20
  838.6 51.3 reduce-scatter.16
  898.4 40.4 all-gather.32
  994.3 51.3 reduce-scatter.22
  1064.7 41.4 all-gather.34
  1108.2 40.4 all-gather.28
  1164.9 51.7 reduce-scatter.24
  1220.6 76.0 reduce-scatter.30
  1300.3 75.5 reduce-scatter.32
  1380.1 62.3 reduce-scatter.34
  1446.6 255.0 all-reduce.8
  1705.4 62.4 reduce-scatter.28
  1770.6 50.4 reduce-scatter.26
  (1 shorter events, 38.6 us)
where the time goes:
time: 1890 us; the launch traced here: 1880 us
  waiting for transfers between devices  1160 us (61%)
  matrix products  260 us (14%)
  local copies, waits for them, and re-layouts  186 us (10%)
  blocking collectives  175 us (9%)
  other arithmetic  80.7 us (4%)
    unnamed x26, waiting for transfers between devices  260 us
    reduce_scatter x5, waiting for transfers between devices, scatter_backward(): lax.psum_scatter(partial_terms.astype(jnp.bfloat16), 'tensor', scatter_di...  168 us
    all_gather x3, waiting for transfers between devices, gather_gradient(): return lax.all_gather(values, 'tensor', axis=1, tiled=True)  122 us
    reduce_scatter x3, waiting for transfers between devices, scatter_forward(): lax.psum_scatter(partial_terms.astype(jnp.bfloat16), 'tensor', scatter_di...  98.6 us
    all_gather x5, waiting for transfers between devices, gather_columns(): return lax.all_gather(values, 'tensor', axis=1, tiled=True)  90.8 us
    dot_general x8, matrix products, contract_last(): lax.dot_general(left_side, right_side, (((1,), (1,)), ((), ())), preferre...  81.8 us
    reduce_scatter x1, waiting for transfers between devices, body(): lax.psum_scatter(local_grads[4].astype(jnp.bfloat16), 'dp', scatter_dimen...  77.2 us
    all_gather x1, waiting for transfers between devices, body(): lax.all_gather(sharded[1], 'dp', axis=1, tiled=True)  74.5 us
  transfers between devices with their start and end apart: 25, of which 23 were waited for; matrix products, arithmetic and copies ran while one was open for 16% of the time, Pallas kernels for 0%

commit v1 on v0

v1 whole, which is shorter than its diff:
```python
from functools import partial
import math

import jax
import jax.numpy as jnp
from jax import lax
from jax.experimental import pallas as pl
from jax.experimental.pallas import tpu as pltpu
from jax.sharding import PartitionSpec as P

C = 1280
GROUPS = 32
FRAMES = 16
HEAD = 160
BLOCK = 128
MIXED = ("tensor", "dp")


def spread(rows, weight):
    return jnp.einsum("rk,tkn->trn", rows, weight, preferred_element_type=jnp.float32)


def collapse(parts, weight):
    return jnp.einsum("trn,tkn->rk", parts, weight, preferred_element_type=jnp.float32)


def weight_grad(rows, parts):
    return jnp.einsum("rk,trn->tkn", rows, parts, preferred_element_type=jnp.float32)


def make_positions():
    channel_ids = jnp.arange(C)
    pair_rate = jnp.exp((channel_ids // 2).astype(jnp.float32) * (-2.0 * math.log(10000.0) / C))
    angles = jnp.arange(FRAMES).astype(jnp.float32)[:, None] * pair_rate[None, :]
    return jnp.where(channel_ids[None, :] % 2 == 0, jnp.sin(angles), jnp.cos(angles))


def layer_stats(stream):
    centre = jnp.mean(stream, axis=1, keepdims=True)
    offset = stream - centre
    inverse = lax.rsqrt(jnp.mean(offset * offset, axis=1, keepdims=True) + 1e-05)
    return offset * inverse, inverse


def layer_back(grad_out, normal_part, inverse, gain):
    scaled = grad_out * gain
    first = jnp.mean(scaled, axis=1, keepdims=True)
    second = jnp.mean(scaled * normal_part, axis=1, keepdims=True)
    grad_in = inverse * (scaled - first - normal_part * second)
    return grad_in, jnp.sum(grad_out * normal_part, 0), jnp.sum(grad_out, 0)


def dot_rows(left, right):
    return lax.dot_general(left, right, (((1,), (1,)), ((), ())), preferred_element_type=jnp.float32)


def dot_plain(left, right):
    return lax.dot_general(left, right, (((1,), (0,)), ((), ())), preferred_element_type=jnp.float32)


def dot_first(left, right):
    return lax.dot_general(left, right, (((0,), (0,)), ((), ())), preferred_element_type=jnp.float32)


def same_pixel(block):
    row = lax.broadcasted_iota(jnp.int32, (block, block), 0) // FRAMES
    col = lax.broadcasted_iota(jnp.int32, (block, block), 1) // FRAMES
    return row == col


def head_probs(query, key, same, scale):
    scores = jnp.where(same, dot_rows(query, key) * scale, -1e30)
    top = jnp.max(scores, axis=1, keepdims=True)
    weights = jnp.where(same, jnp.exp(scores - top), 0.0)
    return weights / jnp.sum(weights, axis=1, keepdims=True)


def attend_kernel(scale, qkv_ref, out_ref):
    rows, width = out_ref.shape[1], out_ref.shape[2]
    block = min(BLOCK, rows)
    same = same_pixel(block)
    for start in range(0, rows, block):
        for head in range(width // HEAD):
            low = head * HEAD
            query = qkv_ref[0, start : start + block, low : low + HEAD]
            key = qkv_ref[0, start : start + block, width + low : width + low + HEAD]
            value = qkv_ref[0, start : start + block, 2 * width + low : 2 * width + low + HEAD]
            probs = head_probs(query, key, same, scale).astype(jnp.bfloat16)
            out_ref[0, start : start + block, low : low + HEAD] = dot_plain(probs, value).astype(
                jnp.bfloat16
            )


def attend(qkv):
    parts, rows, wide = qkv.shape
    width = wide // 3
    return pl.pallas_call(
        partial(attend_kernel, 1.0 / math.sqrt(HEAD)),
        grid=(parts,),
        in_specs=[pl.BlockSpec((1, rows, wide), lambda t: (t, 0, 0))],
        out_specs=pl.BlockSpec((1, rows, width), lambda t: (t, 0, 0)),
        out_shape=jax.ShapeDtypeStruct((parts, rows, width), jnp.bfloat16),
        compiler_params=pltpu.CompilerParams(vmem_limit_bytes=32 << 20),
    )(qkv)


def attend_back_kernel(scale, qkv_ref, grad_ref, out_ref):
    rows, width = grad_ref.shape[1], grad_ref.shape[2]
    block = min(BLOCK, rows)
    same = same_pixel(block)
    for start in range(0, rows, block):
        for head in range(width // HEAD):
            low = head * HEAD
            here = slice(start, start + block)
            query = qkv_ref[0, here, low : low + HEAD]
            key = qkv_ref[0, here, width + low : width + low + HEAD]
            value = qkv_ref[0, here, 2 * width + low : 2 * width + low + HEAD]
            grad = grad_ref[0, here, low : low + HEAD]
            probs = head_probs(query, key, same, scale)
            grad_probs = dot_rows(grad, value)
            centred = jnp.sum(probs * grad_probs, axis=1, keepdims=True)
            grad_raw = (probs * (grad_probs - centred) * scale).astype(jnp.bfloat16)
            out_ref[0, here, low : low + HEAD] = dot_plain(grad_raw, key).astype(jnp.bfloat16)
            out_ref[0, here, width + low : width + low + HEAD] = dot_first(grad_raw, query).astype(
                jnp.bfloat16
            )
            out_ref[0, here, 2 * width + low : 2 * width + low + HEAD] = dot_first(
                probs.astype(jnp.bfloat16), grad
            ).astype(jnp.bfloat16)


def attend_back(qkv, grad):
    parts, rows, wide = qkv.shape
    width = wide // 3
    return pl.pallas_call(
        partial(attend_back_kernel, 1.0 / math.sqrt(HEAD)),
        grid=(parts,),
        in_specs=[
            pl.BlockSpec((1, rows, wide), lambda t: (t, 0, 0)),
            pl.BlockSpec((1, rows, width), lambda t: (t, 0, 0)),
        ],
        out_specs=pl.BlockSpec((1, rows, wide), lambda t: (t, 0, 0)),
        out_shape=jax.ShapeDtypeStruct((parts, rows, wide), jnp.bfloat16),
        compiler_params=pltpu.CompilerParams(vmem_limit_bytes=32 << 20),
    )(qkv, grad)


def gather_weight(shard):
    tensor_size = lax.axis_size("tensor")
    whole = lax.all_gather(shard, MIXED, axis=0, tiled=True)
    return whole.reshape(tensor_size, C, shard.shape[1])


def reduce_weight(grad):
    parts, rows, width = grad.shape
    flat = grad.astype(jnp.bfloat16).reshape(parts * rows, width)
    return lax.psum_scatter(flat, MIXED, scatter_dimension=0, tiled=True).astype(jnp.float32)


def to_pixels(values, tensor_size):
    slots, frames, width, pixels = values.shape
    own = pixels // tensor_size
    turned = jnp.transpose(values, (3, 0, 1, 2)).reshape(tensor_size, own * slots * frames, width)
    return lax.all_to_all(turned, "tensor", 0, 0, tiled=True)


def to_channels(values, slots, pixels):
    tensor_size, rows, width = values.shape
    arrived = lax.all_to_all(values, "tensor", 0, 0, tiled=True)
    return jnp.transpose(arrived.reshape(pixels, slots, FRAMES, width), (1, 2, 3, 0))


def body(
    latent,
    clip_flags,
    cotangent,
    norm_gain,
    norm_shift,
    channel_bias,
    hidden_bias,
    weight_in,
    weight_qkv,
    weight_out,
    weight_up,
    weight_down,
    weight_proj,
):
    tensor_size = lax.axis_size("tensor")
    slots, frames, width, pixels = latent.shape
    share = weight_in.shape[0]
    hidden_width = hidden_bias.shape[0]
    flags = (clip_flags > 0)[:, None, None, None]

    full_in = gather_weight(weight_in)
    full_qkv, full_out = [], []
    for block in range(2):
        full_qkv.append(gather_weight(weight_qkv[block].reshape(share, 3 * width)))
        full_out.append(gather_weight(weight_out[block].T))
    full_up = gather_weight(weight_up)
    full_down = gather_weight(weight_down.T)
    full_proj = gather_weight(weight_proj)

    packed = jnp.concatenate([norm_gain, norm_shift, channel_bias], 0)
    packed = lax.all_gather(
        jnp.concatenate([packed.reshape(-1), hidden_bias]), "tensor", axis=0, tiled=False
    )
    channel_params = packed[:, : 13 * width].reshape(tensor_size, 13, width)
    channel_params = jnp.transpose(channel_params, (1, 0, 2)).reshape(13, C)
    gains, shifts, biases = channel_params[:4], channel_params[4:8], channel_params[8:]
    hidden_full = packed[:, 13 * width :]

    start = latent.astype(jnp.float32)
    cot = cotangent.astype(jnp.float32)
    group_width = C // GROUPS
    grouped = start.reshape(slots, frames, width // group_width, group_width, pixels)
    group_centre = jnp.mean(grouped, axis=(1, 3, 4), keepdims=True)
    offset = grouped - group_centre
    group_inverse = lax.rsqrt(jnp.mean(offset * offset, axis=(1, 3, 4), keepdims=True) + 1e-06)
    group_hat = (offset * group_inverse).reshape(start.shape)
    normed = group_hat * norm_gain[0][:, None] + norm_shift[0][:, None]
    arrived = to_pixels(normed.astype(jnp.bfloat16), tensor_size)
    rows = arrived.shape[1]
    inputs_in = jnp.transpose(arrived, (1, 0, 2)).reshape(rows, C)

    grad_moved_local = jnp.where(flags, cot, 0.0)
    bias_moved = jnp.sum(grad_moved_local, axis=(0, 1, 3))
    grad_moved = to_pixels(grad_moved_local.astype(jnp.bfloat16), tensor_size)

    def join(parts):
        return jnp.transpose(parts, (1, 0, 2)).reshape(rows, parts.shape[0] * parts.shape[2])

    stream = join(spread(inputs_in, full_in)) + biases[0]
    position = jnp.tile(make_positions(), (rows // FRAMES, 1))
    kept = []
    for block in range(2):
        hat, inverse = layer_stats(stream)
        lifted = (hat * gains[1 + block] + shifts[1 + block] + position).astype(jnp.bfloat16)
        qkv = spread(lifted, full_qkv[block]).astype(jnp.bfloat16)
        attended = attend(qkv)
        stream = stream + collapse(attended, full_out[block]) + biases[1 + block]
        kept.append((hat, inverse, lifted, qkv, attended))
    hat_feed, inverse_feed = layer_stats(stream)
    inputs_up = (hat_feed * gains[3] + shifts[3]).astype(jnp.bfloat16)
    pre_act = spread(inputs_up, full_up) + hidden_full[:, None, :]
    hidden = jax.nn.gelu(pre_act, approximate=False).astype(jnp.bfloat16)
    stream = stream + collapse(hidden, full_down) + biases[3]
    inputs_proj = stream.astype(jnp.bfloat16)
    moved = spread(inputs_proj, full_proj) + biases[4].reshape(tensor_size, 1, width)
    moved_local = to_channels(moved.astype(jnp.bfloat16), slots, pixels).astype(jnp.float32)
    output = jnp.where(flags, start + moved_local, start).astype(jnp.bfloat16)

    bias_grads = [None] * 4
    gain_grads = [None] * 3
    shift_grads = [None] * 3
    qkv_grads = [None, None]
    out_grads = [None, None]
    proj_grad = reduce_weight(weight_grad(inputs_proj, grad_moved))
    grad_stream = collapse(grad_moved, full_proj)
    bias_grads[3] = jnp.sum(grad_stream, 0)
    grad_low = grad_stream.astype(jnp.bfloat16)
    down_grad = reduce_weight(weight_grad(grad_low, hidden))
    grad_hidden = spread(grad_low, full_down)
    unused, gelu_pull = jax.vjp(partial(jax.nn.gelu, approximate=False), pre_act)
    grad_pre = gelu_pull(grad_hidden)[0]
    hidden_grad = jnp.sum(grad_pre, 1)
    grad_pre_low = grad_pre.astype(jnp.bfloat16)
    up_grad = reduce_weight(weight_grad(inputs_up, grad_pre_low))
    grad_layer, gain_grads[2], shift_grads[2] = layer_back(
        collapse(grad_pre_low, full_up), hat_feed, inverse_feed, gains[3]
    )
    grad_stream = grad_stream + grad_layer
    for block in (1, 0):
        hat, inverse, lifted, qkv, attended = kept[block]
        bias_grads[1 + block] = jnp.sum(grad_stream, 0)
        grad_low = grad_stream.astype(jnp.bfloat16)
        out_grads[block] = reduce_weight(weight_grad(grad_low, attended)).T
        grad_attended = spread(grad_low, full_out[block]).astype(jnp.bfloat16)
        grad_qkv = attend_back(qkv, grad_attended)
        qkv_grads[block] = reduce_weight(weight_grad(lifted, grad_qkv)).reshape(share, 3, width)
        grad_layer, gain_grads[block], shift_grads[block] = layer_back(
            collapse(grad_qkv, full_qkv[block]), hat, inverse, gains[1 + block]
        )
        grad_stream = grad_stream + grad_layer
    bias_grads[0] = jnp.sum(grad_stream, 0)
    grad_low = grad_stream.astype(jnp.bfloat16)
    grad_low_parts = jnp.transpose(grad_low.reshape(rows, tensor_size, width), (1, 0, 2))
    in_grad = reduce_weight(weight_grad(inputs_in, grad_low_parts))
    grad_normed = collapse(grad_low_parts, full_in).astype(jnp.bfloat16)
    grad_normed = jnp.transpose(grad_normed.reshape(rows, tensor_size, width), (1, 0, 2))
    grad_normed = to_channels(grad_normed, slots, pixels).astype(jnp.float32)
    scaled = grad_normed * norm_gain[0][:, None]
    scaled_groups = scaled.reshape(grouped.shape)
    hat_groups = group_hat.reshape(grouped.shape)
    first = jnp.mean(scaled_groups, axis=(1, 3, 4), keepdims=True)
    second = jnp.mean(scaled_groups * hat_groups, axis=(1, 3, 4), keepdims=True)
    grad_group = group_inverse * (scaled_groups - first - hat_groups * second)
    latent_grad = cot + grad_group.reshape(start.shape)
    group_gain_grad = jnp.sum(grad_normed * group_hat, axis=(0, 1, 3))
    group_shift_grad = jnp.sum(grad_normed, axis=(0, 1, 3))

    vectors = jnp.stack(gain_grads + shift_grads + bias_grads, 0)
    vectors = jnp.transpose(vectors.reshape(10, tensor_size, width), (1, 0, 2))
    vectors = jnp.concatenate([vectors.reshape(tensor_size, 10 * width), hidden_grad], 1)
    vectors = lax.psum_scatter(vectors, "tensor", scatter_dimension=0, tiled=False)
    sums = lax.psum(
        jnp.concatenate([vectors, group_gain_grad, group_shift_grad, bias_moved]), "dp"
    )
    channel_sums = sums[: 10 * width].reshape(10, width)
    hidden_bias_grad = sums[10 * width : 10 * width + hidden_width]
    local_sums = sums[10 * width + hidden_width :].reshape(3, width)
    gain_grad = jnp.concatenate([local_sums[0:1], channel_sums[0:3]], 0)
    shift_grad = jnp.concatenate([local_sums[1:2], channel_sums[3:6]], 0)
    channel_bias_grad = jnp.concatenate([channel_sums[6:10], local_sums[2:3]], 0)
    return (
        output,
        latent_grad,
        gain_grad,
        shift_grad,
        channel_bias_grad,
        hidden_bias_grad,
        in_grad,
        jnp.stack(qkv_grads, 0),
        jnp.stack(out_grads, 0),
        up_grad,
        down_grad.T,
        proj_grad,
    )


def solution(mesh):
    placed = (
        P("dp", None, "tensor", None),
        P("dp"),
        P("dp", None, "tensor", None),
        P(None, "tensor"),
        P(None, "tensor"),
        P(None, "tensor"),
        P("tensor"),
        P("dp", "tensor"),
        P(None, "dp", None, "tensor"),
        P(None, "tensor", "dp"),
        P("dp", "tensor"),
        P("tensor", "dp"),
        P("dp", "tensor"),
    )
    return jax.shard_map(
        body,
        mesh=mesh,
        in_specs=placed,
        out_specs=(
            P("dp", None, "tensor", None),
            P("dp", None, "tensor", None),
            P(None, "tensor"),
            P(None, "tensor"),
            P(None, "tensor"),
            P("tensor"),
            P("dp", "tensor"),
            P(None, "dp", None, "tensor"),
            P(None, "tensor", "dp"),
            P("dp", "tensor"),
            P("tensor", "dp"),
            P("dp", "tensor"),
        ),
        check_vma=False,
    )
```

time: 1890 us -> 2260 us (1.20)
  waiting for transfers between devices: 1160 us -> 1710 us
  blocking collectives: 175 us -> 36.1 us
  Pallas kernels: 0 us -> 50 us
  other arithmetic: 80.7 us -> 36.4 us
  local copies, waits for them, and re-layouts: 186 us -> 145 us
    unnamed x26, waiting for transfers between devices: 260 us -> 658 us
    reduce_scatter x12 -> x2, waiting for transfers between devices: 476 us -> 562 us  [reduce_weight(): lax.psum_scatter(flat, MIXED, scatter_dimension=0, tiled=True)]
    all_gather x2 -> x0, blocking collectives: 69.6 us -> none  [the longest x1 36.4 us: body(): lax.all_gather(sharded[0], 'dp', axis=0, tiled=True)]
    psum x10 -> x1, blocking collectives: 105 us -> 36.1 us  [body(): lax.psum(jnp.concatenate([vectors, group_gain_grad, group_shift_grad, bia...]
    pallas_call x0 -> x4, Pallas kernels: none -> 50 us  [the longest x2 34.2 us: attend_back(): pl.pallas_call(partial(attend_back_kernel, 1.0 / math.sqrt(HEAD)), grid=(...]
    all_gather x12 -> x8, waiting for transfers between devices: 420 us -> 467 us  [gather_weight(): whole = lax.all_gather(shard, MIXED, axis=0, tiled=True)]
    another operation x29 -> x13, local copies, waits for them, and re-layouts: 43.8 us -> 3.04 us  [the longest x2 2.13 us: body(): full_qkv.append(gather_weight(weight_qkv[block].reshape(share, 3 * width)))]
    transpose x8 -> x1, local copies, waits for them, and re-layouts: 31.1 us -> 0.71 us  [body(): full_out.append(gather_weight(weight_out[block].T))]
  transfers between devices with their start and end apart: 25 -> 22, of which waited for: 23 -> 18; matrix products, arithmetic and copies ran while one was open for 16% -> 14% of each run, Pallas kernels for 0% -> 1%
where the time goes in v1:
time: 2260 us; the launch traced here: 2250 us
  waiting for transfers between devices  1710 us (76%)
  matrix products  239 us (11%)
  local copies, waits for them, and re-layouts  145 us (6%)
  Pallas kernels  50 us (2%)
  other arithmetic  36.4 us (2%)
  blocking collectives  36.1 us (2%)
    unnamed x26, waiting for transfers between devices  658 us
    reduce_scatter x2, waiting for transfers between devices, reduce_weight(): lax.psum_scatter(flat, MIXED, scatter_dimension=0, tiled=True)  562 us
    all_gather x8, waiting for transfers between devices, gather_weight(): whole = lax.all_gather(shard, MIXED, axis=0, tiled=True)  467 us
    dot_general x8, matrix products, spread(): jnp.einsum('rk,tkn->trn', rows, weight, preferred_element_type=jnp.float32)  96.2 us
    unnamed x148, local copies, waits for them, and re-layouts  94.5 us
    dot_general x8, matrix products, collapse(): jnp.einsum('trn,tkn->rk', parts, weight, preferred_element_type=jnp.float32)  76.6 us
    dot_general x8, matrix products, weight_grad(): jnp.einsum('rk,trn->tkn', rows, parts, preferred_element_type=jnp.float32)  66.4 us
  transfers between devices with their start and end apart: 22, of which 18 were waited for; matrix products, arithmetic and copies ran while one was open for 14% of the time, Pallas kernels for 1%

profile of v1, /device:TPU:0, one launch (start us, length us, event | category | flops | bytes accessed | tf_op | source)
XLA Modules:
  0.0 2253.2 jit_solution(3637085512995367330)
XLA Ops:
  55.9 31.4 %all-gather.10.cloned.1.call-done = bf16[5120,320]{1,0:T(8,128)(2,1)} async-done(((bf16[160,320]{1,0:T(8,128)(2,1)}), bf16[5120,320]{1,0:T(8,128)(2,1)}) %all-gather.10.cloned.1.call-update) | async-done | bytes 3276816 | tf_op jit(solution)/shard_map/all_gather | solution.py:150
  102.4 47.8 %all-gather.24.cloned.1.call-done = bf16[5120,320]{1,0:T(8,128)(2,1)} async-done(((bf16[160,320]{1,0:T(8,128)(2,1)}), bf16[5120,320]{1,0:T(8,128)(2,1)}) %all-gather.24.cloned.1.call-update) | async-done | bytes 3276816 | tf_op jit(solution)/shard_map/all_gather | solution.py:150
  157.4 81.5 %all-gather.12.cloned.1.call-done = bf16[5120,960]{1,0:T(8,128)(2,1)} async-done(((bf16[160,960]{1,0:T(8,128)(2,1)}), bf16[5120,960]{1,0:T(8,128)(2,1)}) %all-gather.12.cloned.1.call-update) | async-done | bytes 9830416 | tf_op jit(solution)/shard_map/all_gather | solution.py:150
  269.0 33.9 %all-gather.14.cloned.1.call-done = bf16[5120,320]{1,0:T(8,128)(2,1)} async-done(((bf16[160,320]{1,0:T(8,128)(2,1)}), bf16[5120,320]{1,0:T(8,128)(2,1)}) %all-gather.14.cloned.1.call-update) | async-done | bytes 3276816 | tf_op jit(solution)/shard_map/all_gather | solution.py:150
  310.4 81.4 %all-gather.16.cloned.1.call-done = bf16[5120,960]{1,0:T(8,128)(2,1)} async-done(((bf16[160,960]{1,0:T(8,128)(2,1)}), bf16[5120,960]{1,0:T(8,128)(2,1)}) %all-gather.16.cloned.1.call-update) | async-done | bytes 9830416 | tf_op jit(solution)/shard_map/all_gather | solution.py:150
  391.7 13.6 convolution_convert_fusion.8
  421.6 34.0 %all-gather.18.cloned.1.call-done = bf16[5120,320]{1,0:T(8,128)(2,1)} async-done(((bf16[160,320]{1,0:T(8,128)(2,1)}), bf16[5120,320]{1,0:T(8,128)(2,1)}) %all-gather.18.cloned.1.call-update) | async-done | bytes 3276816 | tf_op jit(solution)/shard_map/all_gather | solution.py:150
  462.8 93.0 %all-gather.20.cloned.1.call-done = bf16[5120,1280]{1,0:T(8,128)(2,1)} async-done(((bf16[160,1280]{1,0:T(8,128)(2,1)}), bf16[5120,1280]{1,0:T(8,128)(2,1)}) %all-gather.20.cloned.1.call-update) | async-done | bytes 13107216 | tf_op jit(solution)/shard_map/all_gather | solution.py:150
  555.8 35.2 %fusion.8 = (bf16[4,512,1280]{2,1,0:T(8,128)(2,1)}, f32[4,512,1280]{2,1,0:T(8,128)}, f32[512,4,1280]{2,0,1:T(8,128)}) fusion(f32[4,1280]{1,0:T(4,128)S(1)} %slice.205, bf16[4,1280,1280]{2,1,0:T(8,128)(2,1)} %bitcast.330, f32[512,1280]{1,0:T(8,128)} %copy-done.17, f32[1280]{0:T(1024)S(1)} %add.283, f32[1280]{0:T(1024)S(1)} %mul.355, ...), kind=kOutput, calls=%fused_computation.20 | convolution fusion | flops 6887178240 | bytes 41977856 | tf_op jit(solution)/shard_map/rk,tkn->trn/dot_general | solution.py:20
  591.0 64.5 %all-gather.22.cloned.1.call-done = bf16[5120,1280]{1,0:T(8,128)(2,1)} async-done(((bf16[160,1280]{1,0:T(8,128)(2,1)}), bf16[5120,1280]{1,0:T(8,128)(2,1)}) %all-gather.22.cloned.1.call-update) | async-done | bytes 13107216 | tf_op jit(solution)/shard_map/all_gather | solution.py:150
  655.5 19.9 fusion.97
  675.4 14.3 multiply_reduce_fusion.1
  699.6 17.2 shard_map.222
  739.7 17.0 shard_map.223
  756.8 14.2 multiply_reduce_fusion.3
  852.4 14.2 copy.332
  876.7 14.1 copy.333
  980.1 36.1 %psum.7 = f32[5440]{0:T(1024)S(1)} all-reduce(f32[5440]{0:T(1024)S(1)} %concatenate.25), channel_id=1, replica_groups=mesh['dp'=8,'tensor'=4] {'dp'}, use_global_device_ids=true, to_apply=%region_35.36 | all-reduce | flops 5440 | bytes 43520 | tf_op jit(solution)/shard_map/psum | solution.py:305
  1027.6 81.4 %reduce-scatter.35.cloned.1.call-done = bf16[160,320]{1,0:T(8,128)(2,1)} async-done(((bf16[5120,320]{1,0:T(8,128)(2,1)}), bf16[160,320]{1,0:T(8,128)(2,1)}) %reduce-scatter.35.cloned.1.call-update) | async-done | bytes 102416
  1110.9 106.5 %reduce-scatter.25.cloned.1.call-done = bf16[160,320]{1,0:T(8,128)(2,1)} async-done(((bf16[5120,320]{1,0:T(8,128)(2,1)}), bf16[160,320]{1,0:T(8,128)(2,1)}) %reduce-scatter.25.cloned.1.call-update) | async-done | bytes 102416
  1219.2 227.2 %reduce-scatter.27.cloned.1.call-done = bf16[160,960]{1,0:T(8,128)(2,1)} async-done(((bf16[5120,960]{1,0:T(8,128)(2,1)}), bf16[160,960]{1,0:T(8,128)(2,1)}) %reduce-scatter.27.cloned.1.call-update) | async-done | bytes 307216
  1447.9 227.5 %reduce-scatter.29.cloned.1.call-done = bf16[160,960]{1,0:T(8,128)(2,1)} async-done(((bf16[5120,960]{1,0:T(8,128)(2,1)}), bf16[160,960]{1,0:T(8,128)(2,1)}) %reduce-scatter.29.cloned.1.call-update) | async-done | bytes 307216
  1678.8 280.2 %reduce-scatter.21.cloned.1.call-done = bf16[160,1280]{1,0:T(8,128)(2,1)} async-done(((bf16[5120,1280]{1,0:T(8,128)(2,1)}), bf16[160,1280]{1,0:T(8,128)(2,1)}) %reduce-scatter.21.cloned.1.call-update) | async-done | bytes 409616 | tf_op jit(solution)/shard_map/reduce_scatter | solution.py:157
  1961.0 282.2 %reduce-scatter.23.cloned.1.call-done = bf16[160,1280]{1,0:T(8,128)(2,1)} async-done(((bf16[5120,1280]{1,0:T(8,128)(2,1)}), bf16[160,1280]{1,0:T(8,128)(2,1)}) %reduce-scatter.23.cloned.1.call-update) | async-done | bytes 409616 | tf_op jit(solution)/shard_map/reduce_scatter | solution.py:157
  (339 shorter events, 366.3 us)
Async XLA Ops:
  8.0 39.7 %all-reduce.5.cloned.1.call-start = ((), (), s32[]{:S(2)}) async-start(), calls=%async_computation.22 | async-start | bytes 180224
  12.6 74.8 %all-gather.10.cloned.1.call-start = ((), (), s32[]{:S(2)}) async-start(), calls=%async_computation.12 | async-start | bytes 4055040 | tf_op jit(solution)/shard_map/all_gather | solution.py:150
  13.1 137.1 %all-gather.24.cloned.1.call-start = ((), (), s32[]{:S(2)}) async-start(), calls=%async_computation.19 | async-start | bytes 4055040 | tf_op jit(solution)/shard_map/all_gather | solution.py:150
  13.7 225.2 %all-gather.12.cloned.1.call-start = ((), (), s32[]{:S(2)}) async-start(), calls=%async_computation.13 | async-start | bytes 10813440 | tf_op jit(solution)/shard_map/all_gather | solution.py:150
  16.3 286.5 %all-gather.14.cloned.1.call-start = ((), (), s32[]{:S(2)}) async-start(), calls=%async_computation.14 | async-start | bytes 4055040 | tf_op jit(solution)/shard_map/all_gather | solution.py:150
  17.1 374.6 %all-gather.16.cloned.1.call-start = ((), (), s32[]{:S(2)}) async-start(), calls=%async_computation.15 | async-start | bytes 10813440 | tf_op jit(solution)/shard_map/all_gather | solution.py:150
  18.5 437.1 %all-gather.18.cloned.1.call-start = ((), (), s32[]{:S(2)}) async-start(), calls=%async_computation.16 | async-start | bytes 4055040 | tf_op jit(solution)/shard_map/all_gather | solution.py:150
  19.3 536.5 %all-gather.20.cloned.1.call-start = ((), (), s32[]{:S(2)}) async-start(), calls=%async_computation.17 | async-start | bytes 13516800 | tf_op jit(solution)/shard_map/all_gather | solution.py:150
  19.8 635.6 %all-gather.22.cloned.1.call-start = ((), (), s32[]{:S(2)}) async-start(), calls=%async_computation.18 | async-start | bytes 13516800 | tf_op jit(solution)/shard_map/all_gather | solution.py:150
  26.6 24.9 %all-to-all-start = ((bf16[4,512,320]{1,2,0:T(8,128)(2,1)}), bf16[4,512,320]{1,2,0:T(8,128)(2,1)}, u32[]{:S(2)}, u32[]{:S(2)}) async-start(bf16[4,512,320]{1,2,0:T(8,128)(2,1)} %copy.224), calls=%async_computation | async-start | bytes 2621440 | tf_op jit(solution)/shard_map/all_to_all | solution.py:164
  35.2 273.5 %copy-start.30 = (f32[16,1280]{1,0:T(8,128)}, f32[16,1280]{1,0:T(8,128)S(1)}, u32[]{:S(2)}) copy-start(f32[16,1280]{1,0:T(8,128)S(1)} %fusion.73) | copy-start | bytes 245764
  50.6 258.0 %copy-start.40 = (f32[1280]{0:T(1024)}, f32[1280]{0:T(1024)S(1)}, u32[]{:S(2)}) copy-start(f32[1280]{0:T(1024)S(1)} %mul.349) | copy-start | bytes 15364
  51.6 50.8 %all-to-all-start.2 = ((bf16[4,512,320]{1,2,0:T(8,128)(2,1)}), bf16[4,512,320]{1,2,0:T(8,128)(2,1)}, u32[]{:S(2)}, u32[]{:S(2)}) async-start(bf16[4,512,320]{1,2,0:T(8,128)(2,1)} %copy.248), calls=%async_computation.2 | async-start | bytes 2621440 | tf_op jit(solution)/shard_map/all_to_all | solution.py:164
  55.9 895.5 %all-reduce.7.cloned.1.call-start = ((), (), s32[]{:S(2)}) async-start(), calls=%async_computation.29 | async-start | bytes 143360
  777.5 246.9 %reduce-scatter.33.cloned.1.call-start = ((), (), s32[]{:S(2)}) async-start(), calls=%async_computation.27 | async-start | bytes 4055040
  788.9 236.5 %reduce-scatter.31.cloned.1.call-start = ((), (), s32[]{:S(2)}) async-start(), calls=%async_computation.26 | async-start | bytes 4055040
  801.8 307.2 %reduce-scatter.35.cloned.1.call-start = ((), (), s32[]{:S(2)}) async-start(), calls=%async_computation.28 | async-start | bytes 4055040
  828.9 388.5 %reduce-scatter.25.cloned.1.call-start = ((), (), s32[]{:S(2)}) async-start(), calls=%async_computation.23 | async-start | bytes 4055040
  842.6 603.8 %reduce-scatter.27.cloned.1.call-start = ((), (), s32[]{:S(2)}) async-start(), calls=%async_computation.24 | async-start | bytes 10813440
  866.6 808.8 %reduce-scatter.29.cloned.1.call-start = ((), (), s32[]{:S(2)}) async-start(), calls=%async_computation.25 | async-start | bytes 10813440
  890.8 1068.2 %reduce-scatter.21.cloned.1.call-start = ((), (), s32[]{:S(2)}) async-start(), calls=%async_computation.20 | async-start | bytes 13516800 | tf_op jit(solution)/shard_map/reduce_scatter | solution.py:157
  903.6 1339.6 %reduce-scatter.23.cloned.1.call-start = ((), (), s32[]{:S(2)}) async-start(), calls=%async_computation.21 | async-start | bytes 13516800 | tf_op jit(solution)/shard_map/reduce_scatter | solution.py:157
  925.7 21.0 all-to-all-start.3
  946.7 21.9 all-to-all-start.1
  (60 other events, 1105.0 us)
Sparse Core Ops, SparseCore 0:
  12.7 35.0 all-reduce.4
  777.6 27.6 all-reduce.6
Sparse Core Ops, SparseCore 1:
  16.0 71.2 all-gather.9
  90.2 60.0 all-gather.23
  154.0 84.9 all-gather.11
  243.0 59.8 all-gather.13
  306.8 84.9 all-gather.15
  395.8 59.8 all-gather.17
  458.7 97.0 all-gather.19
  558.9 96.5 all-gather.21
  789.0 102.5 reduce-scatter.32
  897.0 103.7 reduce-scatter.30
  1006.0 102.9 reduce-scatter.34
  1114.4 102.9 reduce-scatter.24
  1219.6 226.8 reduce-scatter.26
  1448.7 226.6 reduce-scatter.28
  1677.7 281.2 reduce-scatter.20
  1961.5 281.7 reduce-scatter.22

commit v2 on v1

--- a/solution.py
+++ b/solution.py
@@ -24,10 +24,6 @@
     return jnp.einsum("trn,tkn->rk", parts, weight, preferred_element_type=jnp.float32)
 
 
-def weight_grad(rows, parts):
-    return jnp.einsum("rk,trn->tkn", rows, parts, preferred_element_type=jnp.float32)
-
-
 def make_positions():
     channel_ids = jnp.arange(C)
     pair_rate = jnp.exp((channel_ids // 2).astype(jnp.float32) * (-2.0 * math.log(10000.0) / C))
@@ -75,86 +71,673 @@
     return weights / jnp.sum(weights, axis=1, keepdims=True)
 
 
-def attend_kernel(scale, qkv_ref, out_ref):
+def attend_kernel(scale, qk_ref, v_ref, out_ref):
     rows, width = out_ref.shape[1], out_ref.shape[2]
     block = min(BLOCK, rows)
     same = same_pixel(block)
     for start in range(0, rows, block):
         for head in range(width // HEAD):
-            low = head * HEAD
-            query = qkv_ref[0, start : start + block, low : low + HEAD]
-            key = qkv_ref[0, start : start + block, width + low : width + low + HEAD]
-            value = qkv_ref[0, start : start + block, 2 * width + low : 2 * width + low + HEAD]
+            here, low = slice(start, start + block), head * HEAD
+            query = qk_ref[0, here, low : low + HEAD]
+            key = qk_ref[0, here, width + low : width + low + HEAD]
+            value = v_ref[0, here, low : low + HEAD]
             probs = head_probs(query, key, same, scale).astype(jnp.bfloat16)
-            out_ref[0, start : start + block, low : low + HEAD] = dot_plain(probs, value).astype(
-                jnp.bfloat16
-            )
-
-
-def attend(qkv):
-    parts, rows, wide = qkv.shape
-    width = wide // 3
+            out_ref[0, here, low : low + HEAD] = dot_plain(probs, value).astype(jnp.bfloat16)
+
+
+def part_spec(array):
+    return pl.BlockSpec((1,) + array.shape[1:], lambda t: (t, 0, 0))
+
+
+def attend(qk, values):
     return pl.pallas_call(
         partial(attend_kernel, 1.0 / math.sqrt(HEAD)),
-        grid=(parts,),
-        in_specs=[pl.BlockSpec((1, rows, wide), lambda t: (t, 0, 0))],
-        out_specs=pl.BlockSpec((1, rows, width), lambda t: (t, 0, 0)),
-        out_shape=jax.ShapeDtypeStruct((parts, rows, width), jnp.bfloat16),
+        grid=(qk.shape[0],),
+        in_specs=[part_spec(qk), part_spec(values)],
+        out_specs=part_spec(values),
+        out_shape=jax.ShapeDtypeStruct(values.shape, jnp.bfloat16),
         compiler_params=pltpu.CompilerParams(vmem_limit_bytes=32 << 20),
-    )(qkv)
-
-
-def attend_back_kernel(scale, qkv_ref, grad_ref, out_ref):
+    )(qk, values)
+
+
+def attend_back_kernel(scale, qk_ref, v_ref, grad_ref, dqk_ref, dv_ref):
     rows, width = grad_ref.shape[1], grad_ref.shape[2]
     block = min(BLOCK, rows)
     same = same_pixel(block)
     for start in range(0, rows, block):
         for head in range(width // HEAD):
-            low = head * HEAD
-            here = slice(start, start + block)
-            query = qkv_ref[0, here, low : low + HEAD]
-            key = qkv_ref[0, here, width + low : width + low + HEAD]
-            value = qkv_ref[0, here, 2 * width + low : 2 * width + low + HEAD]
+            here, low = slice(start, start + block), head * HEAD
+            query = qk_ref[0, here, low : low + HEAD]
+            key = qk_ref[0, here, width + low : width + low + HEAD]
+            value = v_ref[0, here, low : low + HEAD]
             grad = grad_ref[0, here, low : low + HEAD]
             probs = head_probs(query, key, same, scale)
             grad_probs = dot_rows(grad, value)
             centred = jnp.sum(probs * grad_probs, axis=1, keepdims=True)
             grad_raw = (probs * (grad_probs - centred) * scale).astype(jnp.bfloat16)
-            out_ref[0, here, low : low + HEAD] = dot_plain(grad_raw, key).astype(jnp.bfloat16)
-            out_ref[0, here, width + low : width + low + HEAD] = dot_first(grad_raw, query).astype(
+            dqk_ref[0, here, low : low + HEAD] = dot_plain(grad_raw, key).astype(jnp.bfloat16)
+            dqk_ref[0, here, width + low : width + low + HEAD] = dot_first(grad_raw, query).astype(
                 jnp.bfloat16
             )
-            out_ref[0, here, 2 * width + low : 2 * width + low + HEAD] = dot_first(
-                probs.astype(jnp.bfloat16), grad
-            ).astype(jnp.bfloat16)
-
-
-def attend_back(qkv, grad):
-    parts, rows, wide = qkv.shape
-    width = wide // 3
+            dv_ref[0, here, low : low + HEAD] = dot_first(probs.astype(jnp.bfloat16), grad).astype(
+                jnp.bfloat16
+            )
+
+
+def attend_back(qk, values, grad):
     return pl.pallas_call(
         partial(attend_back_kernel, 1.0 / math.sqrt(HEAD)),
-        grid=(parts,),
-        in_specs=[
-            pl.BlockSpec((1, rows, wide), lambda t: (t, 0, 0)),
-            pl.BlockSpec((1, rows, width), lambda t: (t, 0, 0)),
+        grid=(qk.shape[0],),
+        in_specs=[part_spec(qk), part_spec(values), part_spec(values)],
+        out_specs=[part_spec(qk), part_spec(values)],
+        out_shape=[
+            jax.ShapeDtypeStruct(qk.shape, jnp.bfloat16),
+            jax.ShapeDtypeStruct(values.shape, jnp.bfloat16),
         ],
-        out_specs=pl.BlockSpec((1, rows, wide), lambda t: (t, 0, 0)),
-        out_shape=jax.ShapeDtypeStruct((parts, rows, wide), jnp.bfloat16),
         compiler_params=pltpu.CompilerParams(vmem_limit_bytes=32 << 20),
-    )(qkv, grad)
-
-
-def gather_weight(shard):
-    tensor_size = lax.axis_size("tensor")
-    whole = lax.all_gather(shard, MIXED, axis=0, tiled=True)
-    return whole.reshape(tensor_size, C, shard.shape[1])
-
-
-def reduce_weight(grad):
-    parts, rows, width = grad.shape
-    flat = grad.astype(jnp.bfloat16).reshape(parts * rows, width)
-    return lax.psum_scatter(flat, MIXED, scatter_dimension=0, tiled=True).astype(jnp.float32)
+    )(qk, values, grad)
+
+
+UNITS = 9
+WIDE = 640
+SLOTS_IN_FLIGHT = 6
+ROWS_A = 96
+MESH_ID = pl.DeviceIdType.MESH
+
+
+class Place:
+    def __init__(self):
+        dp, tn = lax.axis_index("dp"), lax.axis_index("tensor")
+        self.z, self.x = dp // 2, dp % 2
+        self.y, self.c = tn // 2, tn % 2
+        self.far_x, self.far_y = 1 - self.x, 1 - self.y
+        self.to = {
+            "x": (self.z * 2 + self.far_x, tn),
+            "y": (dp, self.far_y * 2 + self.c),
+            "core": (dp, self.y * 2 + 1 - self.c),
+            "up": (dp + 2, tn),
+            "down": (dp - 2, tn),
+        }
+        self.has_up = self.z < 3
+        self.has_down = self.z > 0
+
+    def greet(self):
+        barrier = pltpu.get_barrier_semaphore()
+
+        def hello(name):
+            pl.semaphore_signal(barrier, inc=1, device_id=self.to[name], device_id_type=MESH_ID)
+
+        for name in ("x", "y", "core"):
+            hello(name)
+        pl.when(self.has_up)(lambda: hello("up"))
+        pl.when(self.has_down)(lambda: hello("down"))
+        pl.semaphore_wait(barrier, 3 + (6 - self.z) // 4 + (self.z + 3) // 4)
+
+
+def await_bytes(ref, sem):
+    pltpu.make_async_copy(ref, ref, sem).wait()
+
+
+def gather_kernel(shard_ref, whole_ref, local_sem, send_sem, recv_sem, core_sem):
+    at = Place()
+    z, x, y, c = at.z, at.x, at.y, at.c
+    share = shard_ref.shape[1]
+    cut = (pl.ds(0, ROWS_A), pl.ds(ROWS_A, share - ROWS_A))
+    kinds = {"up": 0, "down": 1, "x": 2, "y": 3, "core": 4}
+    at.greet()
+
+    def send(unit, colour, yy, zz, xx, kind, own=False):
+        place = whole_ref.at[unit, yy, c, zz, xx, cut[colour]]
+        pltpu.make_async_remote_copy(
+            src_ref=shard_ref.at[unit, cut[colour]] if own else place,
+            dst_ref=place,
+            send_sem=send_sem.at[unit, colour, kinds[kind]],
+            recv_sem=recv_sem.at[unit, colour, yy, zz, xx],
+            device_id=at.to[kind],
+            device_id_type=MESH_ID,
+        ).start()
+
+    def arrived(unit, colour, yy, zz, xx):
+        await_bytes(
+            whole_ref.at[unit, yy, c, zz, xx, cut[colour]], recv_sem.at[unit, colour, yy, zz, xx]
+        )
+
+    def own_copy(unit):
+        return pltpu.make_async_copy(
+            shard_ref.at[unit], whole_ref.at[unit, y, c, z, x], local_sem.at[unit]
+        )
+
+    def to_core(unit, part):
+        if part == 2:
+            place = whole_ref.at[unit, :, c, :, :, cut[1]]
+        else:
+            place = whole_ref.at[unit, y if part == 0 else at.far_y, c, :, :, cut[0]]
+        return pltpu.make_async_remote_copy(
+            src_ref=place,
+            dst_ref=place,
+            send_sem=send_sem.at[unit, part // 2, 4],
+            recv_sem=core_sem.at[unit, part],
+            device_id=at.to["core"],
+            device_id_type=MESH_ID,
+        )
+
+    def from_z(unit, colour, step, yy):
+        @pl.when(z >= step)
+        def _():
+            zz = z - step
+            arrived(unit, colour, yy, zz, x)
+            pl.when(at.has_up)(lambda: send(unit, colour, yy, zz, x, "up"))
+            send(unit, colour, yy, zz, x, "x")
+            if colour == 0:
+                send(unit, colour, yy, zz, x, "y")
+
+        @pl.when(z + step <= 3)
+        def _():
+            zz = z + step
+            arrived(unit, colour, yy, zz, x)
+            pl.when(at.has_down)(lambda: send(unit, colour, yy, zz, x, "down"))
+            send(unit, colour, yy, zz, x, "x")
+            if colour == 0:
+                send(unit, colour, yy, zz, x, "y")
+
+    def from_x(unit, step):
+        def one(zz):
+            arrived(unit, 0, y, zz, at.far_x)
+            send(unit, 0, y, zz, at.far_x, "y")
+
+        if step == 0:
+            one(z)
+        else:
+            pl.when(z >= step)(lambda: one(z - step))
+            pl.when(z + step <= 3)(lambda: one(z + step))
+
+    def stage0(unit):
+        own_copy(unit).start()
+        pl.when(at.has_up)(lambda: send(unit, 0, y, z, x, "up", True))
+        pl.when(at.has_down)(lambda: send(unit, 0, y, z, x, "down", True))
+        send(unit, 1, y, z, x, "y", True)
+        send(unit, 0, y, z, x, "x", True)
+        pl.when(at.has_up)(lambda: send(unit, 1, y, z, x, "up", True))
+        pl.when(at.has_down)(lambda: send(unit, 1, y, z, x, "down", True))
+        send(unit, 0, y, z, x, "y", True)
+        send(unit, 1, y, z, x, "x", True)
+
+    def stage1(unit):
+        from_z(unit, 0, 1, y)
+        arrived(unit, 1, at.far_y, z, x)
+        pl.when(at.has_up)(lambda: send(unit, 1, at.far_y, z, x, "up"))
+        pl.when(at.has_down)(lambda: send(unit, 1, at.far_y, z, x, "down"))
+        send(unit, 1, at.far_y, z, x, "x")
+        from_z(unit, 1, 1, y)
+        from_x(unit, 0)
+
+    def stage2(unit):
+        from_z(unit, 0, 2, y)
+        from_z(unit, 1, 1, at.far_y)
+        from_z(unit, 1, 2, y)
+        from_x(unit, 1)
+
+    def stage3(unit):
+        from_z(unit, 0, 3, y)
+        from_z(unit, 1, 2, at.far_y)
+        from_z(unit, 1, 3, y)
+        from_x(unit, 2)
+
+    def stage4(unit):
+        from_z(unit, 1, 3, at.far_y)
+        from_x(unit, 3)
+        own_copy(unit).wait()
+        to_core(unit, 0).start()
+
+    def stage5(unit):
+        for zz in range(4):
+            for xx in range(2):
+                arrived(unit, 0, at.far_y, zz, xx)
+        to_core(unit, 1).start()
+        for zz in range(4):
+            for yy in range(2):
+                arrived(unit, 1, yy, zz, at.far_x)
+        to_core(unit, 2).start()
+
+    def stage6(unit):
+        other = 1 - c
+        await_bytes(whole_ref.at[unit, y, other, :, :, cut[0]], core_sem.at[unit, 0])
+        await_bytes(whole_ref.at[unit, at.far_y, other, :, :, cut[0]], core_sem.at[unit, 1])
+        await_bytes(whole_ref.at[unit, :, other, :, :, cut[1]], core_sem.at[unit, 2])
+        for colour in range(2):
+            rows = cut[colour]
+            await_bytes(whole_ref.at[unit, :, c, :, :, rows], send_sem.at[unit, colour, 4])
+            whole_x = whole_ref.at[unit, 0, c, :, 0, rows] if colour == 0 else None
+            if colour == 0:
+                await_bytes(whole_x, send_sem.at[unit, 0, 2])
+                await_bytes(whole_ref.at[unit, 0, c, :, :, rows], send_sem.at[unit, 0, 3])
+            else:
+                await_bytes(whole_ref.at[unit, 0, c, :, :, rows], send_sem.at[unit, 1, 2])
+                await_bytes(whole_ref.at[unit, 0, c, 0, 0, rows], send_sem.at[unit, 1, 3])
+            for level in range(3):
+
+                def ups(level=level):
+                    if colour == 0:
+                        ref = whole_ref.at[unit, 0, c, pl.ds(0, level + 1), 0, rows]
+                    else:
+                        ref = whole_ref.at[unit, :, c, pl.ds(0, level + 1), 0, rows]
+                    return ref
+
+                pl.when(z == level)(
+                    lambda level=level: await_bytes(ups(level), send_sem.at[unit, colour, 0])
+                )
+                pl.when(z == 3 - level)(
+                    lambda level=level: await_bytes(ups(level), send_sem.at[unit, colour, 1])
+                )
+
+    stages = (stage0, stage1, stage2, stage3, stage4, stage5, stage6)
+
+    def advance(turn, carry):
+        for number in reversed(range(len(stages))):
+            unit = turn - number
+
+            @pl.when((unit >= 0) & (unit < UNITS))
+            def _(number=number, unit=unit):
+                stages[number](unit)
+
+        return carry
+
+    lax.fori_loop(0, UNITS + len(stages) - 1, advance, 0)
+
+
+def gather_all(shards):
+    units, share, wide = shards.shape
+    return pl.pallas_call(
+        gather_kernel,
+        in_specs=[pl.BlockSpec(memory_space=pl.ANY)],
+        out_specs=pl.BlockSpec(memory_space=pl.ANY),
+        out_shape=jax.ShapeDtypeStruct((units, 2, 2, 4, 2, share, wide), jnp.bfloat16),
+        scratch_shapes=[
+            pltpu.SemaphoreType.DMA((units,)),
+            pltpu.SemaphoreType.DMA((units, 2, 5)),
+            pltpu.SemaphoreType.DMA((units, 2, 2, 4, 2)),
+            pltpu.SemaphoreType.DMA((units, 3)),
+        ],
+        compiler_params=pltpu.CompilerParams(
+            collective_id=0, has_side_effects=True, vmem_limit_bytes=16 << 20
+        ),
+    )(shards)
+
+
+def reduce_kernel(
+    pt_ref,
+    q_ref,
+    out_ref,
+    ptx_ref,
+    qx_ref,
+    p_buf,
+    q_buf,
+    dw,
+    rya,
+    rxa,
+    rua,
+    rda,
+    rxb,
+    rub,
+    rdb,
+    ryb,
+    load_sem,
+    give_sem,
+    take_sem,
+    send_sem,
+    recv_sem,
+    credit,
+):
+    at = Place()
+    z, x, y, c = at.z, at.x, at.y, at.c
+    far_x, far_y = at.far_x, at.far_y
+    share = out_ref.shape[1]
+    row_a, row_b = pl.ds(0, ROWS_A), pl.ds(ROWS_A, share - ROWS_A)
+    count_p = pt_ref.shape[0]
+    at.greet()
+
+    def give_p(index):
+        return pltpu.make_async_remote_copy(
+            src_ref=pt_ref.at[index],
+            dst_ref=ptx_ref.at[index],
+            send_sem=give_sem.at[index],
+            recv_sem=take_sem.at[index],
+            device_id=at.to["core"],
+            device_id_type=MESH_ID,
+        )
+
+    def give_q(index):
+        return pltpu.make_async_remote_copy(
+            src_ref=q_ref.at[index, :, 1 - c],
+            dst_ref=qx_ref.at[index],
+            send_sem=give_sem.at[count_p + index],
+            recv_sem=take_sem.at[count_p + index],
+            device_id=at.to["core"],
+            device_id_type=MESH_ID,
+        )
+
+    for index in range(UNITS):
+        if (index + index // 5) % 2 == 0:
+            give_p((index + index // 5) // 2).start()
+        give_q(index).start()
+        if index in (4, 5, 7):
+            extra = (index - 3) // 2
+            give_p(5 + extra).start()
+            give_q(UNITS + extra).start()
+
+    names = ["ya0", "ya1", "xa", "ua0", "ua1", "ua2", "da0", "da1", "da2"]
+    names += ["xb0", "xb1", "ub0", "ub1", "ub2", "db0", "db1", "db2", "yb"]
+    number = {name: index for index, name in enumerate(names)}
+
+    def copy(slot, name, src, dst, kind, shift=0):
+        index = number[name] + shift
+        return pltpu.make_async_remote_copy(
+            src_ref=src,
+            dst_ref=dst,
+            send_sem=send_sem.at[slot, index],
+            recv_sem=recv_sem.at[slot, index],
+            device_id=at.to[kind],
+            device_id_type=MESH_ID,
+        )
+
+    def ya(slot, part):
+        side = far_x if part == 0 else x
+        return copy(
+            slot, f"ya{part}", dw.at[slot, far_y, :, side, row_a], rya.at[slot, part], "y"
+        )
+
+    def xa(slot):
+        return copy(slot, "xa", dw.at[slot, y, :, far_x, row_a], rxa.at[slot], "x")
+
+    def xb(slot, part):
+        return copy(slot, f"xb{part}", dw.at[slot, part, :, far_x, row_b], rxb.at[slot, part], "x")
+
+    def yb(slot):
+        return copy(slot, "yb", dw.at[slot, far_y, z, x, row_b], ryb.at[slot], "y")
+
+    def up(slot, colour, d):
+        if colour == 0:
+            return copy(slot, "ua0", dw.at[slot, y, d, x, row_a], rua.at[slot, d - 1], "up", d - 1)
+        return copy(slot, "ub0", dw.at[slot, :, d, x, row_b], rub.at[slot, d - 1], "up", d - 1)
+
+    def down(slot, colour, d):
+        if colour == 0:
+            return copy(slot, "da0", dw.at[slot, y, d, x, row_a], rda.at[slot, d], "down", d)
+        return copy(slot, "db0", dw.at[slot, :, d, x, row_b], rdb.at[slot, d], "down", d)
+
+    def add(place, got):
+        total = place[...].astype(jnp.float32) + got[...].astype(jnp.float32)
+        place[...] = total.astype(jnp.bfloat16)
+
+    def products(slot, p_index, q_index, more):
+        loads = [
+            pltpu.make_async_copy(pt_ref.at[p_index], p_buf.at[0], load_sem.at[0]),
+            pltpu.make_async_copy(ptx_ref.at[p_index], p_buf.at[1], load_sem.at[1]),
+            pltpu.make_async_copy(q_ref.at[q_index, :, c], q_buf.at[0], load_sem.at[2]),
+            pltpu.make_async_copy(qx_ref.at[q_index], q_buf.at[1], load_sem.at[3]),
+        ]
+        for load in loads:
+            load.start()
+        for load in loads:
+            load.wait()
+
+        def one(step, carry):
+            side, zz = step // 4, step % 4
+            yy = jnp.where(side == 0, far_y, y)
+            rows = pl.ds(pl.multiple_of(zz * 2 * share, 2 * share), 2 * share)
+            total = dot_plain(p_buf[0, rows, :], q_buf[0, yy]) + dot_plain(
+                p_buf[1, rows, :], q_buf[1, yy]
+            )
+            total = total.reshape(2, share, WIDE)
+            if more:
+                total = total + dw[slot, yy, zz].astype(jnp.float32)
+            dw[slot, yy, zz] = total.astype(jnp.bfloat16)
+            return carry
+
+        lax.fori_loop(0, 8, one, 0)
+
+    def stage0(turn):
+        slot = turn % SLOTS_IN_FLIGHT
+        p_index = (turn + turn // 5) // 2
+
+        @pl.when((turn + turn // 5) % 2 == 0)
+        def _():
+            give_p(p_index).wait_recv()
+
+        give_q(turn).wait_recv()
+        products(slot, p_index, turn, False)
+
+        @pl.when((turn == 4) | (turn == 5) | (turn == 7))
+        def _():
+            extra = (turn - 3) // 2
+            give_p(5 + extra).wait_recv()
+            give_q(UNITS + extra).wait_recv()
+            products(slot, 5 + extra, UNITS + extra, True)
+
+        @pl.when(turn >= SLOTS_IN_FLIGHT)
+        def _():
+            pl.semaphore_wait(credit.at[0], 1)
+            pl.semaphore_wait(credit.at[1], 1)
+            pl.when(at.has_up)(lambda: pl.semaphore_wait(credit.at[2], 1))
+            pl.when(at.has_down)(lambda: pl.semaphore_wait(credit.at[3], 1))
+
+        ya(slot, 0).start()
+        xb(slot, 0).start()
+        ya(slot, 1).start()
+        xb(slot, 1).start()
+
+    def z_step(slot, colour, step):
+        @pl.when(z <= step - 1)
+        def _():
+            d = z + 4 - step
+
+            @pl.when(z >= 1)
+            def _():
+                up(slot, colour, d).wait_recv()
+                if colour == 0:
+                    add(dw.at[slot, y, d, x, row_a], rua.at[slot, d - 1])
+                else:
+                    add(dw.at[slot, 0, d, x, row_b], rub.at[slot, d - 1, 0])
+                    add(dw.at[slot, 1, d, x, row_b], rub.at[slot, d - 1, 1])
+
+            up(slot, colour, d).start()
+
+        @pl.when(3 - z <= step - 1)
+        def _():
+            d = z - 4 + step
+
+            @pl.when(z <= 2)
+            def _():
+                down(slot, colour, d).wait_recv()
+                if colour == 0:
+                    add(dw.at[slot, y, d, x, row_a], rda.at[slot, d])
+                else:
+                    add(dw.at[slot, 0, d, x, row_b], rdb.at[slot, d, 0])
+                    add(dw.at[slot, 1, d, x, row_b], rdb.at[slot, d, 1])
+
+            down(slot, colour, d).start()
+
+    def stage1(turn):
+        slot = turn % SLOTS_IN_FLIGHT
+        for part in range(2):
+            xb(slot, part).wait_recv()
+            for zz in range(4):
+                add(dw.at[slot, part, zz, x, row_b], rxb.at[slot, part, zz])
+        z_step(slot, 1, 1)
+        ya(slot, 0).wait_recv()
+        for zz in range(4):
+            add(dw.at[slot, y, zz, far_x, row_a], rya.at[slot, 0, zz])
+        xa(slot).start()
+        ya(slot, 1).wait_recv()
+        for zz in range(4):
+            add(dw.at[slot, y, zz, x, row_a], rya.at[slot, 1, zz])
+
+    def stage2(turn):
+        slot = turn % SLOTS_IN_FLIGHT
+        z_step(slot, 1, 2)
+        xa(slot).wait_recv()
+        for zz in range(4):
+            add(dw.at[slot, y, zz, x, row_a], rxa.at[slot, zz])
+        z_step(slot, 0, 1)
+
+    def stage3(turn):
+        slot = turn % SLOTS_IN_FLIGHT
+        z_step(slot, 1, 3)
+        z_step(slot, 0, 2)
+
+    def stage4(turn):
+        slot = turn % SLOTS_IN_FLIGHT
+        z_step(slot, 0, 3)
+
+        @pl.when(z >= 1)
+        def _():
+            up(slot, 1, z).wait_recv()
+            for yy in range(2):
+                add(dw.at[slot, yy, z, x, row_b], rub.at[slot, z - 1, yy])
+
+        @pl.when(z <= 2)
+        def _():
+            down(slot, 1, z).wait_recv()
+            for yy in range(2):
+                add(dw.at[slot, yy, z, x, row_b], rdb.at[slot, z, yy])
+
+        yb(slot).start()
+
+    def stage5(turn):
+        slot = turn % SLOTS_IN_FLIGHT
+        unit = UNITS - 1 - turn
+        out_ref[unit, row_a, :] = dw[slot, y, z, x, row_a, :].astype(jnp.float32)
+
+        @pl.when(z >= 1)
+        def _():
+            up(slot, 0, z).wait_recv()
+            out_ref[unit, row_a, :] += rua[slot, z - 1].astype(jnp.float32)
+
+        @pl.when(z <= 2)
+        def _():
+            down(slot, 0, z).wait_recv()
+            out_ref[unit, row_a, :] += rda[slot, z].astype(jnp.float32)
+
+        yb(slot).wait_recv()
+        out_ref[unit, row_b, :] = dw[slot, y, z, x, row_b, :].astype(jnp.float32) + ryb[
+            slot
+        ].astype(jnp.float32)
+
+        ya(slot, 0).wait_send()
+        ya(slot, 1).wait_send()
+        xa(slot).wait_send()
+        xb(slot, 0).wait_send()
+        xb(slot, 1).wait_send()
+        yb(slot).wait_send()
+        for colour in range(2):
+            for step in range(1, 4):
+
+                @pl.when(z <= step - 1)
+                def _(colour=colour, step=step):
+                    up(slot, colour, z + 4 - step).wait_send()
+
+                @pl.when(3 - z <= step - 1)
+                def _(colour=colour, step=step):
+                    down(slot, colour, z - 4 + step).wait_send()
+
+        @pl.when(turn + SLOTS_IN_FLIGHT < UNITS)
+        def _():
+            def grant(kind, index):
+                pl.semaphore_signal(
+                    credit.at[index], inc=1, device_id=at.to[kind], device_id_type=MESH_ID
+                )
+
+            grant("x", 0)
+            grant("y", 1)
+            pl.when(at.has_up)(lambda: grant("up", 3))
+            pl.when(at.has_down)(lambda: grant("down", 2))
+
+    stages = (stage0, stage1, stage2, stage3, stage4, stage5)
+
+    def advance(now, carry):
+        for step in range(len(stages)):
+            turn = now - step
+
+            @pl.when((turn >= 0) & (turn < UNITS))
+            def _(step=step, turn=turn):
+                stages[step](turn)
+
+        return carry
+
+    lax.fori_loop(0, UNITS + len(stages) - 1, advance, 0)
+    for index in range(count_p):
+        give_p(index).wait_send()
+    for index in range(q_ref.shape[0]):
+        give_q(index).wait_send()
+
+
+def reduce_all(turned, parts, share):
+    count_p, width, rows = turned.shape
+    count_q = parts.shape[0]
+    low = jnp.bfloat16
+    slots, rest = SLOTS_IN_FLIGHT, share - ROWS_A
+    return pl.pallas_call(
+        reduce_kernel,
+        in_specs=[pl.BlockSpec(memory_space=pl.ANY)] * 2,
+        out_specs=[
+            pl.BlockSpec(memory_space=pltpu.VMEM),
+            pl.BlockSpec(memory_space=pl.ANY),
+            pl.BlockSpec(memory_space=pl.ANY),
+        ],
+        out_shape=[
+            jax.ShapeDtypeStruct((UNITS, share, WIDE), jnp.float32),
+            jax.ShapeDtypeStruct((count_p, width, rows), low),
+            jax.ShapeDtypeStruct((count_q, 2, rows, WIDE), low),
+        ],
+        scratch_shapes=[
+            pltpu.VMEM((2, width, rows), low),
+            pltpu.VMEM((2, 2, rows, WIDE), low),
+            pltpu.VMEM((slots, 2, 4, 2, share, WIDE), low),
+            pltpu.VMEM((slots, 2, 4, ROWS_A, WIDE), low),
+            pltpu.VMEM((slots, 4, ROWS_A, WIDE), low),
+            pltpu.VMEM((slots, 3, ROWS_A, WIDE), low),
+            pltpu.VMEM((slots, 3, ROWS_A, WIDE), low),
+            pltpu.VMEM((slots, 2, 4, rest, WIDE), low),
+            pltpu.VMEM((slots, 3, 2, rest, WIDE), low),
+            pltpu.VMEM((slots, 3, 2, rest, WIDE), low),
+            pltpu.VMEM((slots, rest, WIDE), low),
+            pltpu.SemaphoreType.DMA((4,)),
+            pltpu.SemaphoreType.DMA((count_p + count_q,)),
+            pltpu.SemaphoreType.DMA((count_p + count_q,)),
+            pltpu.SemaphoreType.DMA((slots, 18)),
+            pltpu.SemaphoreType.DMA((slots, 18)),
+            pltpu.SemaphoreType.REGULAR((4,)),
+        ],
+        compiler_params=pltpu.CompilerParams(
+            collective_id=1, has_side_effects=True, vmem_limit_bytes=60 << 20
+        ),
+    )(turned, parts)[0]
+
+
+def gather_plain(shards):
+    units, share, wide = shards.shape
+    whole = lax.all_gather(shards, MIXED, axis=1, tiled=True)
+    return whole.reshape(units, lax.axis_size("tensor"), C, wide)
+
+
+def reduce_plain(turned, parts, share):
+    reduced = []
+    for turn in range(UNITS):
+        whole = jnp.einsum(
+            "kr,trn->tkn", turned[(turn + turn // 5) // 2], parts[turn],
+            preferred_element_type=jnp.float32,
+        )
+        if turn in (4, 5, 7):
+            extra = (turn - 3) // 2
+            whole = whole + jnp.einsum(
+                "kr,trn->tkn", turned[5 + extra], parts[UNITS + extra],
+                preferred_element_type=jnp.float32,
+            )
+        whole = whole.astype(jnp.bfloat16).reshape(-1, whole.shape[2])
+        reduced.append(
+            lax.psum_scatter(whole, MIXED, scatter_dimension=0, tiled=True).astype(jnp.float32)
+        )
+    return jnp.stack(reduced[::-1], 0)
 
 
 def to_pixels(values, tensor_size):
@@ -171,6 +754,7 @@
 
 
 def body(
+    by_kernel,
     latent,
     clip_flags,
     cotangent,
@@ -191,14 +775,30 @@
     hidden_width = hidden_bias.shape[0]
     flags = (clip_flags > 0)[:, None, None, None]
 
-    full_in = gather_weight(weight_in)
-    full_qkv, full_out = [], []
+    wide = 2 * width
+
+    shards = []
+    side = jnp.concatenate
     for block in range(2):
-        full_qkv.append(gather_weight(weight_qkv[block].reshape(share, 3 * width)))
-        full_out.append(gather_weight(weight_out[block].T))
-    full_up = gather_weight(weight_up)
-    full_down = gather_weight(weight_down.T)
-    full_proj = gather_weight(weight_proj)
+        shards.append(weight_qkv[block, :, :2].reshape(share, wide))
+        other = weight_in if block == 0 else weight_out[0].T
+        shards.append(side([weight_qkv[block, :, 2], other], 1))
+    shards.append(side([weight_out[1].T, weight_proj], 1))
+    shards += [weight_up[:, :wide], weight_up[:, wide:]]
+    down_turned = weight_down.T
+    shards += [down_turned[:, :wide], down_turned[:, wide:]]
+    shards = jnp.stack(shards, 0)
+    if by_kernel:
+        whole = gather_all(shards).reshape(UNITS, tensor_size, C, wide)
+    else:
+        whole = gather_plain(shards)
+    full_qk = (whole[0], whole[2])
+    full_v = (whole[1, :, :, :width], whole[3, :, :, :width])
+    full_in = whole[1, :, :, width:]
+    full_out = (whole[3, :, :, width:], whole[4, :, :, :width])
+    full_proj = whole[4, :, :, width:]
+    full_up = (whole[5], whole[6])
+    full_down = (whole[7], whole[8])
 
     packed = jnp.concatenate([norm_gain, norm_shift, channel_bias], 0)
     packed = lax.all_gather(
@@ -235,15 +835,21 @@
     for block in range(2):
         hat, inverse = layer_stats(stream)
         lifted = (hat * gains[1 + block] + shifts[1 + block] + position).astype(jnp.bfloat16)
-        qkv = spread(lifted, full_qkv[block]).astype(jnp.bfloat16)
-        attended = attend(qkv)
+        qk = spread(lifted, full_qk[block]).astype(jnp.bfloat16)
+        values = spread(lifted, full_v[block]).astype(jnp.bfloat16)
+        attended = attend(qk, values)
         stream = stream + collapse(attended, full_out[block]) + biases[1 + block]
-        kept.append((hat, inverse, lifted, qkv, attended))
+        kept.append((hat, inverse, lifted, qk, values, attended))
     hat_feed, inverse_feed = layer_stats(stream)
     inputs_up = (hat_feed * gains[3] + shifts[3]).astype(jnp.bfloat16)
-    pre_act = spread(inputs_up, full_up) + hidden_full[:, None, :]
-    hidden = jax.nn.gelu(pre_act, approximate=False).astype(jnp.bfloat16)
-    stream = stream + collapse(hidden, full_down) + biases[3]
+    pre_act = [
+        spread(inputs_up, full_up[half])
+        + hidden_full[:, None, half * wide : half * wide + wide]
+        for half in range(2)
+    ]
+    hidden = [jax.nn.gelu(pre, approximate=False).astype(jnp.bfloat16) for pre in pre_act]
+    stream = stream + collapse(hidden[0], full_down[0]) + collapse(hidden[1], full_down[1])
+    stream = stream + biases[3]
     inputs_proj = stream.astype(jnp.bfloat16)
     moved = spread(inputs_proj, full_proj) + biases[4].reshape(tensor_size, 1, width)
     moved_local = to_channels(moved.astype(jnp.bfloat16), slots, pixels).astype(jnp.float32)
@@ -252,39 +858,65 @@
     bias_grads = [None] * 4
     gain_grads = [None] * 3
     shift_grads = [None] * 3
-    qkv_grads = [None, None]
-    out_grads = [None, None]
-    proj_grad = reduce_weight(weight_grad(inputs_proj, grad_moved))
+    empty = jnp.zeros((tensor_size, rows, width), jnp.bfloat16)
+    turned, parts = [None] * 8, [None] * 12
+    turned[5] = inputs_proj.T
+    parts[9] = side([empty, grad_moved], 2)
     grad_stream = collapse(grad_moved, full_proj)
     bias_grads[3] = jnp.sum(grad_stream, 0)
     grad_low = grad_stream.astype(jnp.bfloat16)
-    down_grad = reduce_weight(weight_grad(grad_low, hidden))
-    grad_hidden = spread(grad_low, full_down)
-    unused, gelu_pull = jax.vjp(partial(jax.nn.gelu, approximate=False), pre_act)
-    grad_pre = gelu_pull(grad_hidden)[0]
-    hidden_grad = jnp.sum(grad_pre, 1)
-    grad_pre_low = grad_pre.astype(jnp.bfloat16)
-    up_grad = reduce_weight(weight_grad(inputs_up, grad_pre_low))
+    turned[0] = grad_low.T
+    parts[0], parts[1] = hidden[1], hidden[0]
+    turned[1] = inputs_up.T
+    hidden_grads = [None, None]
+    grad_normed = 0.0
+    for half in (1, 0):
+        grad_hidden = spread(grad_low, full_down[half])
+        unused, gelu_pull = jax.vjp(partial(jax.nn.gelu, approximate=False), pre_act[half])
+        grad_pre = gelu_pull(grad_hidden)[0]
+        hidden_grads[half] = jnp.sum(grad_pre, 1)
+        parts[3 - half] = grad_pre.astype(jnp.bfloat16)
+        grad_normed = grad_normed + collapse(parts[3 - half], full_up[half])
+    hidden_grad = side(hidden_grads, 1)
     grad_layer, gain_grads[2], shift_grads[2] = layer_back(
-        collapse(grad_pre_low, full_up), hat_feed, inverse_feed, gains[3]
+        grad_normed, hat_feed, inverse_feed, gains[3]
     )
     grad_stream = grad_stream + grad_layer
     for block in (1, 0):
-        hat, inverse, lifted, qkv, attended = kept[block]
+        hat, inverse, lifted, qk, values, attended = kept[block]
         bias_grads[1 + block] = jnp.sum(grad_stream, 0)
         grad_low = grad_stream.astype(jnp.bfloat16)
-        out_grads[block] = reduce_weight(weight_grad(grad_low, attended)).T
+        turned[2 if block == 1 else 6] = grad_low.T
+        pair = [attended, empty] if block == 1 else [empty, attended]
+        parts[4 if block == 1 else 10] = side(pair, 2)
         grad_attended = spread(grad_low, full_out[block]).astype(jnp.bfloat16)
-        grad_qkv = attend_back(qkv, grad_attended)
-        qkv_grads[block] = reduce_weight(weight_grad(lifted, grad_qkv)).reshape(share, 3, width)
+        grad_qk, grad_values = attend_back(qk, values, grad_attended)
+        turned[3 if block == 1 else 4] = lifted.T
+        parts[5 if block == 1 else 7] = side([grad_values, empty], 2)
+        parts[6 if block == 1 else 8] = grad_qk
+        grad_lifted = collapse(grad_qk, full_qk[block]) + collapse(grad_values, full_v[block])
         grad_layer, gain_grads[block], shift_grads[block] = layer_back(
-            collapse(grad_qkv, full_qkv[block]), hat, inverse, gains[1 + block]
+            grad_lifted, hat, inverse, gains[1 + block]
         )
         grad_stream = grad_stream + grad_layer
     bias_grads[0] = jnp.sum(grad_stream, 0)
     grad_low = grad_stream.astype(jnp.bfloat16)
     grad_low_parts = jnp.transpose(grad_low.reshape(rows, tensor_size, width), (1, 0, 2))
-    in_grad = reduce_weight(weight_grad(inputs_in, grad_low_parts))
+    turned[7] = inputs_in.T
+    parts[11] = side([empty, grad_low_parts], 2)
+    turned, parts = jnp.stack(turned, 0), jnp.stack(parts, 0)
+    if by_kernel:
+        reduced = reduce_all(turned, parts.reshape(12, 2, 2, rows, wide), share)
+    else:
+        reduced = reduce_plain(turned, parts, share)
+    qkv_grads = [
+        side([reduced[2 * block], reduced[2 * block + 1, :, :width]], 1).reshape(share, 3, width)
+        for block in range(2)
+    ]
+    out_grads = [reduced[3, :, width:].T, reduced[4, :, :width].T]
+    in_grad, proj_grad = reduced[1, :, width:], reduced[4, :, width:]
+    up_grad = side([reduced[5], reduced[6]], 1)
+    down_grad = side([reduced[7], reduced[8]], 1)
     grad_normed = collapse(grad_low_parts, full_in).astype(jnp.bfloat16)
     grad_normed = jnp.transpose(grad_normed.reshape(rows, tensor_size, width), (1, 0, 2))
     grad_normed = to_channels(grad_normed, slots, pixels).astype(jnp.float32)
@@ -344,7 +976,7 @@
         P("dp", "tensor"),
     )
     return jax.shard_map(
-        body,
+        partial(body, tuple(mesh.shape[name] for name in ("dp", "tensor")) == (8, 4)),
         mesh=mesh,
         in_specs=placed,
         out_specs=(

time: 2260 us -> 1020 us (0.45)
  waiting for transfers between devices: 1710 us -> 13.7 us
  Pallas kernels: 50 us -> 558 us
  matrix products: 239 us -> 178 us
    unnamed x26 -> x4, waiting for transfers between devices: 658 us -> 8.03 us
    reduce_scatter x2 -> x0, waiting for transfers between devices: 562 us -> none  [reduce_weight(): lax.psum_scatter(flat, MIXED, scatter_dimension=0, tiled=True)]
    pallas_call x2 -> x4, Pallas kernels: 15.8 us -> 524 us  [the longest x1 270 us: reduce_all(): pl.pallas_call(reduce_kernel, in_specs=[pl.BlockSpec(memory_space=pl.ANY)...]
    all_gather x8 -> x0, waiting for transfers between devices: 467 us -> none  [gather_weight(): whole = lax.all_gather(shard, MIXED, axis=0, tiled=True)]
    dot_general x8 -> x0, matrix products: 66.4 us -> none  [weight_grad(): jnp.einsum('rk,trn->tkn', rows, parts, preferred_element_type=jnp.float32)]
    slice x5 -> x7, local copies, waits for them, and re-layouts: 3.02 us -> 33.2 us  [the longest x1 26.4 us: body(): full_down = (whole[7], whole[8])]
    unnamed x148 -> x223, local copies, waits for them, and re-layouts: 94.5 us -> 71.5 us
    dot_general x8 -> x12, matrix products: 96.2 us -> 101 us  [spread(): jnp.einsum('rk,tkn->trn', rows, weight, preferred_element_type=jnp.float32)]
  transfers between devices with their start and end apart: 22 -> 6, of which waited for: 18 -> 3; matrix products, arithmetic and copies ran while one was open for 14% -> 10% of each run, Pallas kernels for 1% -> 23%
where the time goes in v2:
time: 1020 us
  Pallas kernels  558 us (55%)
  matrix products  178 us (17%)
  local copies, waits for them, and re-layouts  159 us (16%)
  other arithmetic  38.2 us (4%)
  blocking collectives  37.5 us (4%)
  starting transfers between devices  17.1 us (2%)
  between operations  17 us (2%)
  waiting for transfers between devices  13.7 us (1%)
    pallas_call x1, Pallas kernels, reduce_all(): pl.pallas_call(reduce_kernel, in_specs=[pl.BlockSpec(memory_space=pl.ANY)...  270 us
    pallas_call x1, Pallas kernels, gather_all(): pl.pallas_call(gather_kernel, in_specs=[pl.BlockSpec(memory_space=pl.ANY)...  238 us
    dot_general x12, matrix products, spread(): jnp.einsum('rk,tkn->trn', rows, weight, preferred_element_type=jnp.float32)  101 us
    dot_general x12, matrix products, collapse(): jnp.einsum('trn,tkn->rk', parts, weight, preferred_element_type=jnp.float32)  77.5 us
    unnamed x223, local copies, waits for them, and re-layouts  71.5 us
    psum x1, blocking collectives, body(): lax.psum(jnp.concatenate([vectors, group_gain_grad, group_shift_grad, bia...  37.5 us
    pallas_call x2, Pallas kernels, attend_back(): pl.pallas_call(partial(attend_back_kernel, 1.0 / math.sqrt(HEAD)), grid=(...  34.6 us
    slice x1, local copies, waits for them, and re-layouts, body(): full_down = (whole[7], whole[8])  26.4 us
  transfers between devices with their start and end apart: 6, of which 3 were waited for; matrix products, arithmetic and copies ran while one was open for 10% of the time, Pallas kernels for 23%

profile of v2, /device:TPU:0, one launch (start us, length us, event | category | flops | bytes accessed | tf_op | source)
XLA Modules:
  0.0 1019.7 jit_solution(6023303775067956543)
XLA Ops:
  24.1 237.7 %shard_map.220 = bf16[9,2,2,4,2,160,640]{6,5,4,3,2,1,0:T(8,128)(2,1)} custom-call(bf16[9,160,640]{2,1,0:T(8,128)(2,1)S(1)} %fusion.112.shard_ref), custom_call_target="tpu_custom_call" | custom-call | tf_op jit(solution)/shard_map/pallas_call | solution.py:350
  264.4 26.4 %fusion.133 = (bf16[1,2,2,4,2,160,640]{6,5,4,3,2,1,0:T(8,128)(2,1)}, bf16[1,2,2,4,2,160,640]{6,5,4,3,2,1,0:T(8,128)(2,1)}, bf16[1,2,2,4,2,160,640]{6,5,4,3,2,1,0...) fusion(bf16[9,2,2,4,2,160,640]{6,5,4,3,2,1,0:T(8,128)(2,1)} %sh, ...), kind=kLoop, calls=%fused_computation.284 | loop fusion | bytes 78643200 | tf_op jit(solution)/shard_map/slice | solution.py:801
  292.0 6.1 slice.331
  317.5 8.1 fusion.145
  353.5 8.0 shard_map.221
  384.2 7.8 shard_map.222
  399.0 20.7 %fusion.15 = (bf16[4,512,640]{2,1,0:T(8,128)(2,1)}, f32[4,512,640]{2,1,0:T(8,128)}, f32[4,640,512]{1,2,0:T(8,128)}) fusion(f32[4,640]{1,0:T(4,128)S(1)} %get-tuple-element.140, bf16[4,1280,640]{2,1,0:T(8,128)(2,1)} %bitcast.571, bf16[512,1280]{0,1:T(8,128)(2,1)S(1)} %get-tuple-element.100), kind=kOutput, calls=%fused_computation.30 | convolution fusion | flops 3441950720 | bytes 20981760 | tf_op jit(solution)/shard_map/rk,tkn->trn/dot_general | solution.py:20
  419.8 10.5 %fusion.135 = (f32[4,640]{1,0:T(4,128)}, bf16[4,512,640]{2,1,0:T(8,128)(2,1)}) fusion(f32[4,512,640]{2,1,0:T(8,128)} %get-tuple-element.104, bf16[4,1280,640]{2,1,0:T(8,128)(2,1)S(1)} %bitcast.555, f32[512,1280]{0,1:T(8,128)S(1)} %copy-done.22, f32[4,640,512]{1,2,0:T(8,128)} %get-tuple-element.157, f32[4,640]{1,0:T(4,128)S(1)} %get-tuple-element.140), kind=kOutput, calls=%fused_computation.286 | convolution fusion | flops 3377067520 | bytes 22302720 | tf_op jit(solution)/shard_map/rk,tkn->trn/dot_general | solution.py:20
  430.2 8.9 convolution_bitcast_fusion.3
  439.1 16.8 %fusion.17 = (bf16[4,512,640]{2,1,0:T(8,128)(2,1)}, f32[4,512,640]{2,1,0:T(8,128)}, f32[4,640,512]{1,2,0:T(8,128)}) fusion(f32[4,640]{1,0:T(4,128)S(1)} %get-tuple-element.141, bf16[4,1280,640]{2,1,0:T(8,128)(2,1)S(1)} %bitcast.569, bf16[512,1280]{0,1:T(8,128)(2,1)S(1)} %get-tuple-element.100), kind=kOutput, calls=%fused_computation.37 | convolution fusion | flops 3441950720 | bytes 20981760 | tf_op jit(solution)/shard_map/rk,tkn->trn/dot_general | solution.py:20
  455.9 9.9 fusion.134
  465.8 7.3 multiply_reduce_fusion.1
  492.8 7.9 fusion.75
  506.4 17.4 %shard_map.223 = (bf16[4,512,640]{2,1,0:T(8,128)(2,1)S(1)}, bf16[4,512,320]{2,1,0:T(8,128)(2,1)S(1)}) custom-call(bf16[4,512,640]{2,1,0:T(8,128)(2,1)S(1)} %copy-done.3, bf16[4,512,320]{2,1,0:T(8,128)(2,1)S(1)} %bitcast.522, bf16[4,512,320]{2,1,0:T(8,128)(2,1)S(1)} %bitcast.523), custom_call_target="tpu_custom_call" | custom-call | tf_op jit(solution)/shard_map/pallas_call | solution.py:128
  523.8 6.7 convolution_bitcast_fusion.1
  547.0 6.3 fusion.94
  556.9 17.2 %shard_map.224 = (bf16[4,512,640]{2,1,0:T(8,128)(2,1)S(1)}, bf16[4,512,320]{2,1,0:T(8,128)(2,1)S(1)}) custom-call(bf16[4,512,640]{2,1,0:T(8,128)(2,1)S(1)} %copy-done.1, bf16[4,512,320]{2,1,0:T(8,128)(2,1)S(1)} %bitcast.520, bf16[4,512,320]{2,1,0:T(8,128)(2,1)S(1)} %bitcast.524), custom_call_target="tpu_custom_call" | custom-call | tf_op jit(solution)/shard_map/pallas_call | solution.py:128
  574.1 6.7 convolution_bitcast_fusion
  589.9 6.7 fusion.88
  634.9 270.3 %shard_map.225 = (f32[9,160,640]{2,1,0:T(8,128)}, bf16[8,1280,512]{2,1,0:T(8,128)(2,1)}, bf16[12,2,512,640]{3,2,1,0:T(8,128)(2,1)}) custom-call(bf16[8,1280,512]{2,1,0:T(8,128)(2,1)} %constant_dynamic-update-slice_fusion.2.pt_ref, bf16[12,2,2,512,640]{4,3,2,1,0:T(8,128)(2,1)} %constant_dynamic-update-slice_fusion.3.q_ref), custom_call_target="tpu_custom_call" | custom-call | tf_op jit(solution)/shard_map/pallas_call | solution.py:679
  925.0 6.4 fusion.96
  941.9 8.0 all-reduce.13.cloned.1.call-done
  960.2 6.7 fusion.44
  967.3 37.5 %psum.7 = f32[5440]{0:T(1024)S(1)} all-reduce(f32[5440]{0:T(1024)S(1)} %concatenate.68), channel_id=1, replica_groups=mesh['dp'=8,'tensor'=4] {'dp'}, use_global_device_ids=true, to_apply=%region_36.37 | all-reduce | flops 5440 | bytes 43520 | tf_op jit(solution)/shard_map/psum | solution.py:937
  (393 shorter events, 236.8 us)
Async XLA Ops:
  11.9 301.1 %all-to-all-start.2 = ((bf16[4,512,320]{1,2,0:T(8,128)(2,1)}), bf16[4,512,320]{1,2,0:T(8,128)(2,1)}, u32[]{:S(2)}, u32[]{:S(2)}) async-start(bf16[4,512,320]{1,2,0:T(8,128)(2,1)} %copy.282), calls=%async_computation.2 | async-start | bytes 2621440 | tf_op jit(solution)/shard_map/all_to_all | solution.py:747
  16.3 293.2 %all-reduce.11.cloned.1.call-start = ((), (), s32[]{:S(2)}) async-start(), calls=%async_computation.4 | async-start | bytes 180224
  24.0 237.7 %copy-start.48 = (bf16[1,16,320,128]{3,2,1,0:T(8,128)(2,1)S(1)}, bf16[1,16,320,128]{3,2,1,0:T(8,128)(2,1)}, u32[]{:S(2)}) copy-start(bf16[1,16,320,128]{3,2,1,0:T(8,128)(2,1)} %param.13) | copy-start | bytes 3932164
  263.0 28.4 %copy-start.12 = (bf16[1,16,320,128]{2,1,3,0:T(8,128)(2,1)}, bf16[1,16,320,128]{2,1,3,0:T(8,128)(2,1)S(1)}, u32[]{:S(2)}) copy-start(bf16[1,16,320,128]{2,1,3,0:T(8,128)(2,1)S(1)} %copy.248) | copy-start | bytes 3932164
  263.6 27.7 %copy-start.60 = (f32[320]{0:T(512)}, f32[320]{0:T(512)S(1)}, u32[]{:S(2)}) copy-start(f32[320]{0:T(512)S(1)} %sub.137) | copy-start | bytes 3844
  309.5 30.1 %copy-start.14 = (f32[512,1280]{0,1:T(8,128)}, f32[512,1280]{0,1:T(8,128)S(1)}, u32[]{:S(2)}) copy-start(f32[512,1280]{0,1:T(8,128)S(1)} %copy.255) | copy-start | bytes 7864324
  311.5 28.1 %copy-start.56 = (f32[1280]{0:T(1024)}, f32[1280]{0:T(1024)S(1)}, u32[]{:S(2)}) copy-start(f32[1280]{0:T(1024)S(1)} %mul.375) | copy-start | bytes 15364
  311.6 55.3 %copy-start.58 = (f32[1280]{0:T(1024)}, f32[1280]{0:T(1024)S(1)}, u32[]{:S(2)}) copy-start(f32[1280]{0:T(1024)S(1)} %mul.386) | copy-start | bytes 15364
  313.0 22.1 %all-to-all-start = ((bf16[4,512,320]{1,2,0:T(8,128)(2,1)}), bf16[4,512,320]{1,2,0:T(8,128)(2,1)}, u32[]{:S(2)}, u32[]{:S(2)}) async-start(bf16[4,512,320]{1,2,0:T(8,128)(2,1)} %copy.252), calls=%async_computation | async-start | bytes 2621440 | tf_op jit(solution)/shard_map/all_to_all | solution.py:747
  397.1 76.1 %copy-start.23 = (f32[512,1280]{0,1:T(8,128)}, f32[512,1280]{0,1:T(8,128)S(1)}, u32[]{:S(2)}) copy-start(f32[512,1280]{0,1:T(8,128)S(1)} %get-tuple-element.156) | copy-start | bytes 7864324
  397.5 22.3 %slice-start.2 = ((s8[6553600]{0:T(1024)(128)(4,1)}), s8[4194304]{0:T(1024)(128)(4,1)S(1)}, s32[]{:S(2)}) async-start(s8[6553600]{0:T(1024)(128)(4,1)} %bitcast.553), calls=%async_computation.8 | async-start | bytes 8388608
  397.5 41.6 %slice-start.10 = ((s8[6553600]{0:T(1024)(128)(4,1)}), s8[4194304]{0:T(1024)(128)(4,1)S(1)}, s32[]{:S(2)}) async-start(s8[6553600]{0:T(1024)(128)(4,1)} %bitcast.567), calls=%async_computation.16 | async-start | bytes 8388608
  399.0 20.7 %copy-start.22 = (f32[512,1280]{0,1:T(8,128)S(1)}, f32[512,1280]{0,1:T(8,128)}, u32[]{:S(2)}) copy-start(f32[512,1280]{0,1:T(8,128)} %copy.288) | copy-start | bytes 7864324
  399.0 20.7 %slice-start.3 = ((s8[6553600]{0:T(1024)(128)(4,1)}), s8[2359296]{0:T(1024)(128)(4,1)S(1)}, s32[]{:S(2)}) async-start(s8[6553600]{0:T(1024)(128)(4,1)} %bitcast.553), calls=%async_computation.9 | async-start | bytes 4718592
  399.0 40.0 %slice-start.11 = ((s8[6553600]{0:T(1024)(128)(4,1)}), s8[2359296]{0:T(1024)(128)(4,1)S(1)}, s32[]{:S(2)}) async-start(s8[6553600]{0:T(1024)(128)(4,1)} %bitcast.567), calls=%async_computation.17 | async-start | bytes 4718592
  430.2 25.7 %slice-start.8 = ((s8[6553600]{0:T(1024)(128)(4,1)}), s8[4194304]{0:T(1024)(128)(4,1)S(1)}, s32[]{:S(2)}) async-start(s8[6553600]{0:T(1024)(128)(4,1)} %bitcast.564), calls=%async_computation.14 | async-start | bytes 8388608
  439.1 16.8 %slice-start.9 = ((s8[6553600]{0:T(1024)(128)(4,1)}), s8[2359296]{0:T(1024)(128)(4,1)S(1)}, s32[]{:S(2)}) async-start(s8[6553600]{0:T(1024)(128)(4,1)} %bitcast.564), calls=%async_computation.15 | async-start | bytes 4718592
  912.3 21.5 %all-to-all-start.3 = ((bf16[4,512,320]{1,2,0:T(8,128)(2,1)}), bf16[4,512,320]{1,2,0:T(8,128)(2,1)S(1)}, u32[]{:S(2)}, u32[]{:S(2)}) async-start(bf16[4,512,320]{1,2,0:T(8,128)(2,1)} %bitcast.80), calls=%async_computation.3 | async-start | bytes 2621440 | tf_op jit(solution)/shard_map/all_to_all | solution.py:752
  915.9 34.0 %all-reduce.13.cloned.1.call-start = ((), (), s32[]{:S(2)}) async-start(), calls=%async_computation.5 | async-start | bytes 143360
  933.8 17.6 %copy-start.30 = (bf16[4,512,320]{1,2,0:T(8,128)(2,1)}, bf16[4,512,320]{1,2,0:T(8,128)(2,1)S(1)}, u32[]{:S(2)}) copy-start(bf16[4,512,320]{1,2,0:T(8,128)(2,1)S(1)} %all-to-all-done.3) | copy-start | bytes 3932164
  933.8 23.3 %all-to-all-start.1 = ((bf16[4,512,320]{1,2,0:T(8,128)(2,1)}), bf16[4,512,320]{1,2,0:T(8,128)(2,1)}, u32[]{:S(2)}, u32[]{:S(2)}) async-start(bf16[4,512,320]{1,2,0:T(8,128)(2,1)} %fusion.96), calls=%async_computation.1 | async-start | bytes 2621440 | tf_op jit(solution)/shard_map/all_to_all | solution.py:752
  940.7 12.8 %copy-start.63 = (f32[320]{0:T(512)S(1)}, f32[320]{0:T(512)}, u32[]{:S(2)}) copy-start(f32[320]{0:T(512)} %copy-done.62) | copy-start | bytes 3844
  940.7 12.8 %copy-start.65 = (f32[320]{0:T(512)S(1)}, f32[320]{0:T(512)}, u32[]{:S(2)}) copy-start(f32[320]{0:T(512)} %copy-done.64) | copy-start | bytes 3844
  967.0 41.3 %copy-start.29 = (f32[1,16,320,128]{2,1,3,0:T(8,128)S(1)}, f32[1,16,320,128]{2,1,3,0:T(8,128)}, u32[]{:S(2)}) copy-start(f32[1,16,320,128]{2,1,3,0:T(8,128)} %get-tuple-element.131) | copy-start | bytes 7864324
  (79 other events, 337.3 us)
Sparse Core Ops, SparseCore 0:
  20.1 34.5 all-reduce.10
  919.2 30.6 all-reduce.12

commit v3 on v2

--- a/solution.py
+++ b/solution.py
@@ -178,7 +178,40 @@
     pltpu.make_async_copy(ref, ref, sem).wait()
 
 
-def gather_kernel(shard_ref, whole_ref, local_sem, send_sem, recv_sem, core_sem):
+def forward_kernel(
+    shard_ref,
+    x_ref,
+    gains_ref,
+    shifts_ref,
+    biases_ref,
+    out_bias_ref,
+    hidden_bias_ref,
+    position_ref,
+    moved_part_ref,
+    whole_ref,
+    q_ref,
+    pt_ref,
+    stream_out_ref,
+    qk_ref,
+    v_ref,
+    slope_ref,
+    moved_ref,
+    stream,
+    xb,
+    ptb,
+    qkb,
+    vb,
+    attb,
+    hid,
+    slopeb,
+    wb,
+    tile_sem,
+    save_sem,
+    local_sem,
+    send_sem,
+    recv_sem,
+    core_sem,
+):
     at = Place()
     z, x, y, c = at.z, at.x, at.y, at.c
     share = shard_ref.shape[1]
@@ -332,6 +365,194 @@
 
     stages = (stage0, stage1, stage2, stage3, stage4, stage5, stage6)
 
+    rows_all = x_ref.shape[0]
+    width = v_ref.shape[3]
+    half_rows = rows_all // 2
+    scale = 1.0 / math.sqrt(HEAD)
+
+    def save(source, target):
+        copy = pltpu.make_async_copy(source, target, save_sem.at[0])
+        copy.start()
+        copy.wait()
+
+    def tile_load(unit, t):
+        return pltpu.make_async_copy(
+            whole_ref.at[unit, t // 2, t % 2], wb.at[t % 2], tile_sem.at[t % 2]
+        )
+
+    def each_tile(unit, use):
+        tile_load(unit, 0).start()
+
+        def one(t, carry):
+            pl.when(t < 3)(lambda: tile_load(unit, t + 1).start())
+            tile_load(unit, t).wait()
+            use(t, t % 2)
+            return carry
+
+        lax.fori_loop(0, 4, one, 0)
+
+    def tile(slot, first, last):
+        return wb[slot, :, :, :, first:last].reshape(C, last - first)
+
+    def spread_tile(source, slot, first, last, sink):
+        def one(step, carry):
+            rows = pl.ds(pl.multiple_of(step * half_rows, half_rows), half_rows)
+            sink(rows, dot_plain(source[rows, :], tile(slot, first, last)))
+            return carry
+
+        lax.fori_loop(0, 2, one, 0)
+
+    def collapse_tile(source, t, slot, first, last):
+        def one(step, carry):
+            rows = pl.ds(pl.multiple_of(step * half_rows, half_rows), half_rows)
+            stream[rows, :] += dot_rows(source[t, rows, first:last], tile(slot, first, last))
+            return carry
+
+        lax.fori_loop(0, 2, one, 0)
+
+    def turn_to(source, index):
+        def one(step, carry):
+            lanes = pl.ds(pl.multiple_of(step * 128, 128), 128)
+            ptb[lanes, :] = source[:, lanes].T
+            return carry
+
+        lax.fori_loop(0, C // 128, one, 0)
+        save(ptb, pt_ref.at[index])
+
+    chunk = 4 * FRAMES
+
+    def normalise(bias, norm, positions):
+        def one(step, carry):
+            rows = pl.ds(pl.multiple_of(step * chunk, chunk), chunk)
+            values = stream[rows, :] + biases_ref[bias : bias + 1, :]
+            stream[rows, :] = values
+            centre = jnp.mean(values, axis=1, keepdims=True)
+            offset = values - centre
+            inverse = lax.rsqrt(jnp.mean(offset * offset, axis=1, keepdims=True) + 1e-05)
+            normed = offset * inverse * gains_ref[norm : norm + 1, :] + shifts_ref[norm : norm + 1, :]
+            if positions:
+                normed = normed.reshape(chunk // FRAMES, FRAMES, C) + position_ref[...][None]
+                normed = normed.reshape(chunk, C)
+            xb[rows, :] = normed.astype(jnp.bfloat16)
+            return carry
+
+        lax.fori_loop(0, rows_all // chunk, one, 0)
+
+    def attention(place):
+        same = same_pixel(BLOCK)
+
+        def one(step, carry):
+            t, block = step // (rows_all // BLOCK), step % (rows_all // BLOCK)
+            rows = pl.ds(pl.multiple_of(block * BLOCK, BLOCK), BLOCK)
+            for head in range(width // HEAD):
+                low = head * HEAD
+                query = qkb[t, rows, low : low + HEAD]
+                key = qkb[t, rows, width + low : width + low + HEAD]
+                value = vb[t, rows, low : low + HEAD]
+                probs = head_probs(query, key, same, scale).astype(jnp.bfloat16)
+                attb[t, rows, place + low : place + low + HEAD] = dot_plain(probs, value).astype(
+                    jnp.bfloat16
+                )
+            return carry
+
+        lax.fori_loop(0, 4 * (rows_all // BLOCK), one, 0)
+
+    def attention_block(block):
+        normalise(block, 1 + block, True)
+        save(stream, stream_out_ref.at[block])
+
+        def qk_tile(t, slot):
+            def sink(rows, total):
+                qkb[t, rows, :] = total.astype(jnp.bfloat16)
+
+            spread_tile(xb, slot, 0, WIDE, sink)
+
+        def v_tile(t, slot):
+            def sink(rows, total):
+                vb[t, rows, :] = total[:, :width].astype(jnp.bfloat16)
+
+            spread_tile(xb, slot, 0, 384, sink)
+
+        each_tile(2 * block, qk_tile)
+        each_tile(2 * block + 1, v_tile)
+        attb[...] = jnp.zeros_like(attb)
+        attention((1 - block) * width)
+        save(attb, q_ref.at[10 if block == 0 else 4])
+        save(qkb, qk_ref.at[block])
+        save(vb, v_ref.at[block])
+        turn_to(xb, 4 - block)
+
+    def before_units():
+        turn_to(x_ref, 7)
+        save(moved_part_ref, q_ref.at[9])
+
+    def after_1():
+        for t in range(4):
+            tile_load(1, t).start()
+            tile_load(1, t).wait()
+
+            def sink(rows, total, t=t):
+                stream[rows, t * width : (t + 1) * width] = total[:, 64:384]
+
+            spread_tile(x_ref, t % 2, 256, WIDE, sink)
+        attention_block(0)
+
+    def after_3():
+        each_tile(3, lambda t, slot: collapse_tile(attb, t, slot, 256, WIDE))
+        attention_block(1)
+
+    def after_4():
+        each_tile(4, lambda t, slot: collapse_tile(attb, t, slot, 0, 384))
+        normalise(2, 3, False)
+        save(stream, stream_out_ref.at[2])
+        turn_to(xb, 1)
+
+    def after_up(half):
+        def up_tile(t, slot):
+            def sink(rows, total):
+                pre = total + hidden_bias_ref[t, half]
+                below = 0.5 * (1.0 + lax.erf(pre * math.sqrt(0.5)))
+                hid[half, t, rows, :] = (pre * below).astype(jnp.bfloat16)
+                density = jnp.exp(-0.5 * pre * pre) * (1.0 / math.sqrt(2.0 * math.pi))
+                slopeb[t, rows, :] = (below + pre * density).astype(jnp.bfloat16)
+
+            spread_tile(xb, slot, 0, WIDE, sink)
+
+        each_tile(5 + half, up_tile)
+        save(hid.at[half], q_ref.at[1 - half])
+        save(slopeb, slope_ref.at[half])
+
+    def after_down(half):
+        each_tile(7 + half, lambda t, slot: collapse_tile(hid.at[half], t, slot, 0, WIDE))
+        if half == 0:
+            return
+
+        def finish(step, carry):
+            rows = pl.ds(pl.multiple_of(step * chunk, chunk), chunk)
+            xb[rows, :] = (stream[rows, :] + biases_ref[3:4, :]).astype(jnp.bfloat16)
+            return carry
+
+        lax.fori_loop(0, rows_all // chunk, finish, 0)
+
+        def moved_tile(t, slot):
+            def sink(rows, total):
+                moved_ref[t, rows, :] = (total[:, 64:384] + out_bias_ref[t]).astype(jnp.bfloat16)
+
+            spread_tile(xb, slot, 256, WIDE, sink)
+
+        each_tile(4, moved_tile)
+        turn_to(xb, 5)
+
+    unit_work = {
+        1: after_1,
+        3: after_3,
+        4: after_4,
+        5: lambda: after_up(0),
+        6: lambda: after_up(1),
+        7: lambda: after_down(0),
+        8: lambda: after_down(1),
+    }
+
     def advance(turn, carry):
         for number in reversed(range(len(stages))):
             unit = turn - number
@@ -340,28 +561,57 @@
             def _(number=number, unit=unit):
                 stages[number](unit)
 
+        pl.when(turn == 1)(before_units)
+        ready = turn - (len(stages) - 1)
+        for unit, work in unit_work.items():
+            pl.when(ready == unit)(work)
         return carry
 
     lax.fori_loop(0, UNITS + len(stages) - 1, advance, 0)
 
 
-def gather_all(shards):
+def forward_all(shards, rows_in, gains, shifts, biases, hidden_bias, position, moved_part):
     units, share, wide = shards.shape
+    rows, width = rows_in.shape[0], wide // 2
+    low = jnp.bfloat16
+    out_bias = biases[4].reshape(4, 1, width)
+    hidden_bias = hidden_bias.reshape(4, 2, 1, wide)
+    anywhere, near = pl.BlockSpec(memory_space=pl.ANY), pl.BlockSpec(memory_space=pltpu.VMEM)
     return pl.pallas_call(
-        gather_kernel,
-        in_specs=[pl.BlockSpec(memory_space=pl.ANY)],
-        out_specs=pl.BlockSpec(memory_space=pl.ANY),
-        out_shape=jax.ShapeDtypeStruct((units, 2, 2, 4, 2, share, wide), jnp.bfloat16),
+        forward_kernel,
+        in_specs=[anywhere] + [near] * 7 + [anywhere],
+        out_specs=[anywhere] * 7 + [near],
+        out_shape=[
+            jax.ShapeDtypeStruct((units, 2, 2, 4, 2, share, wide), low),
+            jax.ShapeDtypeStruct((12, 4, rows, wide), low),
+            jax.ShapeDtypeStruct((8, C, rows), low),
+            jax.ShapeDtypeStruct((3, rows, C), jnp.float32),
+            jax.ShapeDtypeStruct((2, 4, rows, wide), low),
+            jax.ShapeDtypeStruct((2, 4, rows, width), low),
+            jax.ShapeDtypeStruct((2, 4, rows, wide), low),
+            jax.ShapeDtypeStruct((4, rows, width), low),
+        ],
         scratch_shapes=[
+            pltpu.VMEM((rows, C), jnp.float32),
+            pltpu.VMEM((rows, C), low),
+            pltpu.VMEM((C, rows), low),
+            pltpu.VMEM((4, rows, wide), low),
+            pltpu.VMEM((4, rows, width), low),
+            pltpu.VMEM((4, rows, wide), low),
+            pltpu.VMEM((2, 4, rows, wide), low),
+            pltpu.VMEM((4, rows, wide), low),
+            pltpu.VMEM((2, 4, 2, share, wide), low),
+            pltpu.SemaphoreType.DMA((2,)),
+            pltpu.SemaphoreType.DMA((1,)),
             pltpu.SemaphoreType.DMA((units,)),
             pltpu.SemaphoreType.DMA((units, 2, 5)),
             pltpu.SemaphoreType.DMA((units, 2, 2, 4, 2)),
             pltpu.SemaphoreType.DMA((units, 3)),
         ],
         compiler_params=pltpu.CompilerParams(
-            collective_id=0, has_side_effects=True, vmem_limit_bytes=16 << 20
+            collective_id=0, has_side_effects=True, vmem_limit_bytes=58 << 20
         ),
-    )(shards)
+    )(shards, rows_in, gains, shifts, biases, out_bias, hidden_bias, position, moved_part)
 
 
 def reduce_kernel(
@@ -712,8 +962,6 @@
             collective_id=1, has_side_effects=True, vmem_limit_bytes=60 << 20
         ),
     )(turned, parts)[0]
-
-
 def gather_plain(shards):
     units, share, wide = shards.shape
     whole = lax.all_gather(shards, MIXED, axis=1, tiled=True)
@@ -788,18 +1036,6 @@
     down_turned = weight_down.T
     shards += [down_turned[:, :wide], down_turned[:, wide:]]
     shards = jnp.stack(shards, 0)
-    if by_kernel:
-        whole = gather_all(shards).reshape(UNITS, tensor_size, C, wide)
-    else:
-        whole = gather_plain(shards)
-    full_qk = (whole[0], whole[2])
-    full_v = (whole[1, :, :, :width], whole[3, :, :, :width])
-    full_in = whole[1, :, :, width:]
-    full_out = (whole[3, :, :, width:], whole[4, :, :, :width])
-    full_proj = whole[4, :, :, width:]
-    full_up = (whole[5], whole[6])
-    full_down = (whole[7], whole[8])
-
     packed = jnp.concatenate([norm_gain, norm_shift, channel_bias], 0)
     packed = lax.all_gather(
         jnp.concatenate([packed.reshape(-1), hidden_bias]), "tensor", axis=0, tiled=False
@@ -826,33 +1062,69 @@
     bias_moved = jnp.sum(grad_moved_local, axis=(0, 1, 3))
     grad_moved = to_pixels(grad_moved_local.astype(jnp.bfloat16), tensor_size)
 
-    def join(parts):
-        return jnp.transpose(parts, (1, 0, 2)).reshape(rows, parts.shape[0] * parts.shape[2])
-
-    stream = join(spread(inputs_in, full_in)) + biases[0]
-    position = jnp.tile(make_positions(), (rows // FRAMES, 1))
-    kept = []
-    for block in range(2):
-        hat, inverse = layer_stats(stream)
-        lifted = (hat * gains[1 + block] + shifts[1 + block] + position).astype(jnp.bfloat16)
-        qk = spread(lifted, full_qk[block]).astype(jnp.bfloat16)
-        values = spread(lifted, full_v[block]).astype(jnp.bfloat16)
-        attended = attend(qk, values)
-        stream = stream + collapse(attended, full_out[block]) + biases[1 + block]
-        kept.append((hat, inverse, lifted, qk, values, attended))
-    hat_feed, inverse_feed = layer_stats(stream)
-    inputs_up = (hat_feed * gains[3] + shifts[3]).astype(jnp.bfloat16)
-    pre_act = [
-        spread(inputs_up, full_up[half])
-        + hidden_full[:, None, half * wide : half * wide + wide]
-        for half in range(2)
-    ]
-    hidden = [jax.nn.gelu(pre, approximate=False).astype(jnp.bfloat16) for pre in pre_act]
-    stream = stream + collapse(hidden[0], full_down[0]) + collapse(hidden[1], full_down[1])
-    stream = stream + biases[3]
-    inputs_proj = stream.astype(jnp.bfloat16)
-    moved = spread(inputs_proj, full_proj) + biases[4].reshape(tensor_size, 1, width)
-    moved_local = to_channels(moved.astype(jnp.bfloat16), slots, pixels).astype(jnp.float32)
+    if by_kernel:
+        empty = jnp.zeros((tensor_size, rows, width), jnp.bfloat16)
+        whole, q_all, pt_all, streams, qk_all, v_all, slopes, moved = forward_all(
+            shards,
+            inputs_in,
+            gains,
+            shifts,
+            biases,
+            hidden_full,
+            make_positions(),
+            side([empty, grad_moved], 2),
+        )
+        whole = whole.reshape(UNITS, tensor_size, C, wide)
+    else:
+        whole = gather_plain(shards)
+    full_qk = (whole[0], whole[2])
+    full_v = (whole[1, :, :, :width], whole[3, :, :, :width])
+    full_in = whole[1, :, :, width:]
+    full_out = (whole[3, :, :, width:], whole[4, :, :, :width])
+    full_proj = whole[4, :, :, width:]
+    full_up = (whole[5], whole[6])
+    full_down = (whole[7], whole[8])
+
+    if by_kernel:
+        kept = []
+        for block in range(2):
+            hat, inverse = layer_stats(streams[block])
+            kept.append((hat, inverse, pt_all[4 - block], qk_all[block], v_all[block], None))
+        hat_feed, inverse_feed = layer_stats(streams[2])
+    else:
+        def join(parts):
+            return jnp.transpose(parts, (1, 0, 2)).reshape(rows, parts.shape[0] * parts.shape[2])
+
+        stream = join(spread(inputs_in, full_in)) + biases[0]
+        position = jnp.tile(make_positions(), (rows // FRAMES, 1))
+        kept = []
+        for block in range(2):
+            hat, inverse = layer_stats(stream)
+            lifted = (hat * gains[1 + block] + shifts[1 + block] + position).astype(jnp.bfloat16)
+            qk = spread(lifted, full_qk[block]).astype(jnp.bfloat16)
+            values = spread(lifted, full_v[block]).astype(jnp.bfloat16)
+            attended = attend(qk, values)
+            stream = stream + collapse(attended, full_out[block]) + biases[1 + block]
+            kept.append((hat, inverse, lifted.T, qk, values, attended))
+        hat_feed, inverse_feed = layer_stats(stream)
+        inputs_up = (hat_feed * gains[3] + shifts[3]).astype(jnp.bfloat16)
+        pre_act = [
+            spread(inputs_up, full_up[half])
+            + hidden_full[:, None, half * wide : half * wide + wide]
+            for half in range(2)
+        ]
+        slopes = [
+            jax.vjp(partial(jax.nn.gelu, approximate=False), pre)[1](jnp.ones_like(pre))[0]
+            for pre in pre_act
+        ]
+        hidden = [jax.nn.gelu(pre, approximate=False).astype(jnp.bfloat16) for pre in pre_act]
+        stream = stream + collapse(hidden[0], full_down[0]) + collapse(hidden[1], full_down[1])
+        stream = stream + biases[3]
+        inputs_proj = stream.astype(jnp.bfloat16)
+        moved = spread(inputs_proj, full_proj) + biases[4].reshape(tensor_size, 1, width)
+        moved = moved.astype(jnp.bfloat16)
+
+    moved_local = to_channels(moved, slots, pixels).astype(jnp.float32)
     output = jnp.where(flags, start + moved_local, start).astype(jnp.bfloat16)
 
     bias_grads = [None] * 4
@@ -860,20 +1132,23 @@
     shift_grads = [None] * 3
     empty = jnp.zeros((tensor_size, rows, width), jnp.bfloat16)
     turned, parts = [None] * 8, [None] * 12
-    turned[5] = inputs_proj.T
-    parts[9] = side([empty, grad_moved], 2)
+    if by_kernel:
+        turned[1], turned[5], turned[7] = pt_all[1], pt_all[5], pt_all[7]
+        for index in (0, 1, 4, 9, 10):
+            parts[index] = q_all[index]
+    else:
+        turned[1], turned[5], turned[7] = inputs_up.T, inputs_proj.T, inputs_in.T
+        parts[9] = side([empty, grad_moved], 2)
+        parts[0], parts[1] = hidden[1], hidden[0]
     grad_stream = collapse(grad_moved, full_proj)
     bias_grads[3] = jnp.sum(grad_stream, 0)
     grad_low = grad_stream.astype(jnp.bfloat16)
     turned[0] = grad_low.T
-    parts[0], parts[1] = hidden[1], hidden[0]
-    turned[1] = inputs_up.T
     hidden_grads = [None, None]
     grad_normed = 0.0
     for half in (1, 0):
         grad_hidden = spread(grad_low, full_down[half])
-        unused, gelu_pull = jax.vjp(partial(jax.nn.gelu, approximate=False), pre_act[half])
-        grad_pre = gelu_pull(grad_hidden)[0]
+        grad_pre = grad_hidden * slopes[half]
         hidden_grads[half] = jnp.sum(grad_pre, 1)
         parts[3 - half] = grad_pre.astype(jnp.bfloat16)
         grad_normed = grad_normed + collapse(parts[3 - half], full_up[half])
@@ -883,15 +1158,16 @@
     )
     grad_stream = grad_stream + grad_layer
     for block in (1, 0):
-        hat, inverse, lifted, qk, values, attended = kept[block]
+        hat, inverse, lifted_turned, qk, values, attended = kept[block]
         bias_grads[1 + block] = jnp.sum(grad_stream, 0)
         grad_low = grad_stream.astype(jnp.bfloat16)
         turned[2 if block == 1 else 6] = grad_low.T
-        pair = [attended, empty] if block == 1 else [empty, attended]
-        parts[4 if block == 1 else 10] = side(pair, 2)
+        if not by_kernel:
+            pair = [attended, empty] if block == 1 else [empty, attended]
+            parts[4 if block == 1 else 10] = side(pair, 2)
         grad_attended = spread(grad_low, full_out[block]).astype(jnp.bfloat16)
         grad_qk, grad_values = attend_back(qk, values, grad_attended)
-        turned[3 if block == 1 else 4] = lifted.T
+        turned[3 if block == 1 else 4] = lifted_turned
         parts[5 if block == 1 else 7] = side([grad_values, empty], 2)
         parts[6 if block == 1 else 8] = grad_qk
         grad_lifted = collapse(grad_qk, full_qk[block]) + collapse(grad_values, full_v[block])
@@ -902,7 +1178,6 @@
     bias_grads[0] = jnp.sum(grad_stream, 0)
     grad_low = grad_stream.astype(jnp.bfloat16)
     grad_low_parts = jnp.transpose(grad_low.reshape(rows, tensor_size, width), (1, 0, 2))
-    turned[7] = inputs_in.T
     parts[11] = side([empty, grad_low_parts], 2)
     turned, parts = jnp.stack(turned, 0), jnp.stack(parts, 0)
     if by_kernel:

time: 1020 us -> 1090 us (1.069)
  Pallas kernels: 558 us -> 704 us
  matrix products: 178 us -> 81.7 us
  local copies, waits for them, and re-layouts: 159 us -> 170 us
    pallas_call x3 -> x1, Pallas kernels: 254 us -> 395 us  [forward_all(): pl.pallas_call(forward_kernel, in_specs=[anywhere] + [near] * 7 + [anywhe...]
    dot_general x12 -> x4, matrix products: 101 us -> 30 us  [spread(): jnp.einsum('rk,tkn->trn', rows, weight, preferred_element_type=jnp.float32)]
    dot_general x12 -> x8, matrix products: 77.5 us -> 51.7 us  [collapse(): jnp.einsum('trn,tkn->rk', parts, weight, preferred_element_type=jnp.float32)]
    pallas_call x0 -> x2, local copies, waits for them, and re-layouts: none -> 11.6 us  [forward_all(): pl.pallas_call(forward_kernel, in_specs=[anywhere] + [near] * 7 + [anywhe...]
    unnamed x223 -> x140, local copies, waits for them, and re-layouts: 71.5 us -> 60.1 us
    slice x4 -> x13, local copies, waits for them, and re-layouts: 32.7 us -> 42.4 us  [the longest x1 26.7 us: body(): full_qk = (whole[0], whole[2])]
  transfers between devices with their start and end apart: 6 -> 6, of which waited for: 3 -> 3; matrix products, arithmetic and copies ran while one was open for 10% -> 7% of each run, Pallas kernels for 23% -> 25%
where the time goes in v3:
time: 1090 us; the launch traced here: 1080 us
  Pallas kernels  704 us (65%)
  local copies, waits for them, and re-layouts  170 us (16%)
  matrix products  81.7 us (7%)
  other arithmetic  38.9 us (4%)
  blocking collectives  34.8 us (3%)
  waiting for transfers between devices  22.8 us (2%)
  between operations  16.8 us (2%)
  starting transfers between devices  15.9 us (1%)
    pallas_call x1, Pallas kernels, forward_all(): pl.pallas_call(forward_kernel, in_specs=[anywhere] + [near] * 7 + [anywhe...  395 us
    pallas_call x1, Pallas kernels, reduce_all(): pl.pallas_call(reduce_kernel, in_specs=[pl.BlockSpec(memory_space=pl.ANY)...  275 us
    unnamed x140, local copies, waits for them, and re-layouts  60.1 us
    dot_general x8, matrix products, collapse(): jnp.einsum('trn,tkn->rk', parts, weight, preferred_element_type=jnp.float32)  51.7 us
    psum x1, blocking collectives, body(): lax.psum(jnp.concatenate([vectors, group_gain_grad, group_shift_grad, bia...  34.8 us
    pallas_call x2, Pallas kernels, attend_back(): pl.pallas_call(partial(attend_back_kernel, 1.0 / math.sqrt(HEAD)), grid=(...  34 us
    dot_general x4, matrix products, spread(): jnp.einsum('rk,tkn->trn', rows, weight, preferred_element_type=jnp.float32)  30 us
    slice x1, local copies, waits for them, and re-layouts, body(): full_qk = (whole[0], whole[2])  26.7 us
  transfers between devices with their start and end apart: 6, of which 3 were waited for; matrix products, arithmetic and copies ran while one was open for 7% of the time, Pallas kernels for 25%

profile of v3, /device:TPU:0, one launch (start us, length us, event | category | flops | bytes accessed | tf_op | source)
XLA Modules:
  0.0 1085.0 jit_solution(6476349631944295116)
XLA Ops:
  43.7 12.2 %all-reduce.9.cloned.1.call-done = f32[21760]{0:T(1024)} async-done(((f32[21760]{0:T(1024)}), f32[21760]{0:T(1024)}) %all-reduce.9.cloned.1.call-update) | async-done | bytes 87056
  66.3 395.1 %shard_map.220 = (bf16[9,2,2,4,2,160,640]{6,5,4,3,2,1,0:T(8,128)(2,1)}, bf16[12,4,512,640]{3,2,1,0:T(8,128)(2,1)}, bf16[8,1280,512]{2,1,0:T(8,128)(2,1)}, f32[3,...) custom-call(bf16[9,160,640]{2,1,0:T(8,128)(2,1)} %fusion.47.shard_re, ...), custom_call_target="tpu_custom_call" | custom-call | tf_op jit(solution)/shard_map/pallas_call | solution.py:580
  461.4 26.7 %fusion.65 = (bf16[1,2,2,4,2,160,640]{6,5,4,3,2,1,0:T(8,128)(2,1)}, bf16[1,2,2,4,2,160,640]{6,5,4,3,2,1,0:T(8,128)(2,1)}, bf16[1,2,2,4,2,160,640]{6,5,4,3,2,1,0:...) fusion(bf16[9,2,2,4,2,160,640]{6,5,4,3,2,1,0:T(8,128)(2,1)} %ge, ...), kind=kLoop, calls=%fused_computation.194 | loop fusion | bytes 78643200 | tf_op jit(solution)/shard_map/slice | solution.py:1080
  488.0 7.1 fusion.73
  498.5 9.1 copy.201
  513.5 8.3 fusion.43
  521.8 10.3 fusion.16
  532.2 7.9 convolution_bitcast_fusion.3
  540.1 5.2 multiply_reduce_fusion.1
  551.3 5.1 fusion.37
  558.4 9.3 fusion.66
  587.6 17.0 %shard_map.221 = (bf16[4,512,640]{2,1,0:T(8,128)(2,1)S(1)}, bf16[4,512,320]{2,1,0:T(8,128)(2,1)S(1)}) custom-call(bf16[4,512,640]{2,1,0:T(8,128)(2,1)S(1)} %copy-done, bf16[4,512,320]{2,1,0:T(8,128)(2,1)S(1)} %copy-done.2, bf16[4,512,320]{2,1,0:T(8,128)(2,1)S(1)} %bitcast.298), custom_call_target="tpu_custom_call" | custom-call | tf_op jit(solution)/shard_map/pallas_call | solution.py:128
  606.5 7.2 convolution_bitcast_fusion.1
  613.7 5.1 multiply_reduce_fusion.2
  622.3 6.3 fusion.38
  633.9 17.0 %shard_map.222 = (bf16[4,512,640]{2,1,0:T(8,128)(2,1)S(1)}, bf16[4,512,320]{2,1,0:T(8,128)(2,1)S(1)}) custom-call(bf16[4,512,640]{2,1,0:T(8,128)(2,1)S(1)} %get-tuple-element.127.qk_ref, bf16[4,512,320]{2,1,0:T(8,128)(2,1)S(1)} %copy-done.1, bf16[4,512,320]{2,1,0:T(8,128)(2,1)S(1)} %bitcast.297), custom_call_target="tpu_custom_call" | custom-call | tf_op jit(solution)/shard_map/pallas_call | solution.py:128
  652.7 7.1 convolution_bitcast_fusion
  659.9 5.3 multiply_reduce_fusion.3
  666.6 6.7 fusion.33
  686.9 5.3 constant_dynamic-update-slice_fusion.11
  715.9 274.9 %shard_map.223 = (f32[9,160,640]{2,1,0:T(8,128)}, bf16[8,1280,512]{2,1,0:T(8,128)(2,1)}, bf16[12,2,512,640]{3,2,1,0:T(8,128)(2,1)}) custom-call(bf16[8,1280,512]{2,1,0:T(8,128)(2,1)} %slice_dynamic-update-slice_fusion.1.pt_ref, bf16[12,2,2,512,640]{4,3,2,1,0:T(8,128)(2,1)} %constant_dynamic-update-slice_fusion.2.q_ref), custom_call_target="tpu_custom_call" | custom-call | tf_op jit(solution)/shard_map/pallas_call | solution.py:929
  1018.9 6.1 all-to-all-done.2
  1028.0 6.7 fusion.6
  1035.1 34.8 %psum.7 = f32[5440]{0:T(1024)S(1)} all-reduce(f32[5440]{0:T(1024)S(1)} %concatenate.63), channel_id=1, replica_groups=mesh['dp'=8,'tensor'=4] {'dp'}, use_global_device_ids=true, to_apply=%region_36.37 | all-reduce | flops 5440 | bytes 43520 | tf_op jit(solution)/shard_map/psum | solution.py:1212
  (294 shorter events, 172.3 us)
Async XLA Ops:
  11.7 7.5 copy-start.46
  11.7 8.4 copy-start.32
  13.2 8.3 copy-start.29
  13.2 22.9 %all-to-all-start = ((bf16[4,512,320]{1,2,0:T(8,128)(2,1)}), bf16[4,512,320]{1,2,0:T(8,128)(2,1)}, u32[]{:S(2)}, u32[]{:S(2)}) async-start(bf16[4,512,320]{1,2,0:T(8,128)(2,1)} %copy.190), calls=%async_computation | async-start | bytes 2621440 | tf_op jit(solution)/shard_map/all_to_all | solution.py:995
  17.7 38.1 %all-reduce.9.cloned.1.call-start = ((), (), s32[]{:S(2)}) async-start(), calls=%async_computation.4 | async-start | bytes 180224
  27.1 12.7 %copy-start.35 = (bf16[160,1280]{1,0:T(8,128)(2,1)S(1)}, bf16[160,1280]{1,0:T(8,128)(2,1)}, u32[]{:S(2)}) copy-start(bf16[160,1280]{1,0:T(8,128)(2,1)} %param.23) | copy-start | bytes 1228804
  36.2 27.0 %all-to-all-start.1 = ((bf16[4,512,320]{1,2,0:T(8,128)(2,1)}), bf16[4,512,320]{1,2,0:T(8,128)(2,1)S(1)}, u32[]{:S(2)}, u32[]{:S(2)}) async-start(bf16[4,512,320]{1,2,0:T(8,128)(2,1)} %copy.195), calls=%async_computation.1 | async-start | bytes 2621440 | tf_op jit(solution)/shard_map/all_to_all | solution.py:995
  513.5 26.6 %slice-start.6 = ((s8[6553600]{0:T(1024)(128)(4,1)}), s8[4194304]{0:T(1024)(128)(4,1)S(1)}, s32[]{:S(2)}) async-start(s8[6553600]{0:T(1024)(128)(4,1)} %bitcast.324), calls=%async_computation.12 | async-start | bytes 8388608
  521.8 18.3 %slice-start.7 = ((s8[6553600]{0:T(1024)(128)(4,1)}), s8[2359296]{0:T(1024)(128)(4,1)S(1)}, s32[]{:S(2)}) async-start(s8[6553600]{0:T(1024)(128)(4,1)} %bitcast.324), calls=%async_computation.13 | async-start | bytes 4718592
  532.2 7.9 copy-start.25
  567.8 8.0 slice-start.8
  604.7 9.0 copy-start.5
  604.7 9.0 slice-start
  606.5 7.2 slice-start.1
  651.0 8.9 copy-start.7
  651.0 8.9 slice-start.2
  652.7 7.2 slice-start.3
  676.5 326.7 %all-to-all-start.3 = ((bf16[4,512,320]{1,2,0:T(8,128)(2,1)}), bf16[4,512,320]{1,2,0:T(8,128)(2,1)S(1)}, u32[]{:S(2)}, u32[]{:S(2)}) async-start(bf16[4,512,320]{1,2,0:T(8,128)(2,1)} %bitcast.336), calls=%async_computation.3 | async-start | bytes 2621440 | tf_op jit(solution)/shard_map/all_to_all | solution.py:1000
  680.1 331.3 %all-reduce.11.cloned.1.call-start = ((), (), s32[]{:S(2)}) async-start(), calls=%async_computation.5 | async-start | bytes 143360
  1003.3 9.8 copy-start.17
  1003.3 21.6 %all-to-all-start.2 = ((bf16[4,512,320]{1,2,0:T(8,128)(2,1)}), bf16[4,512,320]{1,2,0:T(8,128)(2,1)}, u32[]{:S(2)}, u32[]{:S(2)}) async-start(bf16[4,512,320]{1,2,0:T(8,128)(2,1)} %copy.198), calls=%async_computation.2 | async-start | bytes 2621440 | tf_op jit(solution)/shard_map/all_to_all | solution.py:1000
  1018.1 9.9 copy-start.15
  1028.0 6.7 copy-start.18
  1034.7 38.7 %copy-start.16 = (f32[1,16,320,128]{2,1,3,0:T(8,128)S(1)}, f32[1,16,320,128]{2,1,3,0:T(8,128)}, u32[]{:S(2)}) copy-start(f32[1,16,320,128]{2,1,3,0:T(8,128)} %get-tuple-element.145) | copy-start | bytes 7864324
  (40 other events, 129.1 us)
Sparse Core Ops, SparseCore 0:
  21.4 34.3 all-reduce.8
  684.5 33.8 all-reduce.10

commit v4 on v3

--- a/solution.py
+++ b/solution.py
@@ -155,6 +155,7 @@
             "x": (self.z * 2 + self.far_x, tn),
             "y": (dp, self.far_y * 2 + self.c),
             "core": (dp, self.y * 2 + 1 - self.c),
+            "cross": (dp, self.far_y * 2 + 1 - self.c),
             "up": (dp + 2, tn),
             "down": (dp - 2, tn),
         }
@@ -167,11 +168,11 @@
         def hello(name):
             pl.semaphore_signal(barrier, inc=1, device_id=self.to[name], device_id_type=MESH_ID)
 
-        for name in ("x", "y", "core"):
+        for name in ("x", "y", "core", "cross"):
             hello(name)
         pl.when(self.has_up)(lambda: hello("up"))
         pl.when(self.has_down)(lambda: hello("down"))
-        pl.semaphore_wait(barrier, 3 + (6 - self.z) // 4 + (self.z + 3) // 4)
+        pl.semaphore_wait(barrier, 4 + (6 - self.z) // 4 + (self.z + 3) // 4)
 
 
 def await_bytes(ref, sem):
@@ -181,13 +182,8 @@
 def forward_kernel(
     shard_ref,
     x_ref,
-    gains_ref,
-    shifts_ref,
-    biases_ref,
-    out_bias_ref,
-    hidden_bias_ref,
+    params_ref,
     position_ref,
-    moved_part_ref,
     whole_ref,
     q_ref,
     pt_ref,
@@ -196,9 +192,13 @@
     v_ref,
     slope_ref,
     moved_ref,
+    joined_ref,
     stream,
     xb,
     ptb,
+    x_got,
+    params_got,
+    hidden_bias,
     qkb,
     vb,
     attb,
@@ -207,6 +207,8 @@
     wb,
     tile_sem,
     save_sem,
+    peer_send,
+    peer_recv,
     local_sem,
     send_sem,
     recv_sem,
@@ -365,31 +367,78 @@
 
     stages = (stage0, stage1, stage2, stage3, stage4, stage5, stage6)
 
-    rows_all = x_ref.shape[0]
-    width = v_ref.shape[3]
+    rows_all, width = x_ref.shape[1], x_ref.shape[2]
     half_rows = rows_all // 2
     scale = 1.0 / math.sqrt(HEAD)
+    own_t = y * 2 + c
+    pending = []
 
     def save(source, target):
-        copy = pltpu.make_async_copy(source, target, save_sem.at[0])
+        copy = pltpu.make_async_copy(source, target, save_sem.at[len(pending)])
+        pending.append(copy)
+        state = [False]
+
+        def begin():
+            copy.start()
+
+        def wait():
+            if not state[0]:
+                state[0] = True
+                copy.wait()
+
+        return begin, wait
+
+    peers = (("y", at.far_y * 2 + c), ("core", y * 2 + 1 - c), ("cross", at.far_y * 2 + 1 - c))
+
+    def peer_copies(index):
+        kind, t = peers[index]
+        target = {"device_id": at.to[kind], "device_id_type": MESH_ID}
+        return (
+            pltpu.make_async_remote_copy(
+                src_ref=params_ref,
+                dst_ref=params_got.at[own_t],
+                send_sem=peer_send.at[0, index],
+                recv_sem=peer_recv.at[0, index],
+                **target,
+            ),
+            pltpu.make_async_remote_copy(
+                src_ref=x_ref.at[t],
+                dst_ref=x_got.at[own_t],
+                send_sem=peer_send.at[1, index],
+                recv_sem=peer_recv.at[1, index],
+                **target,
+            ),
+        )
+
+    own_peer = (
+        pltpu.make_async_copy(params_ref, params_got.at[own_t], peer_send.at[0, 3]),
+        pltpu.make_async_copy(x_ref.at[own_t], x_got.at[own_t], peer_send.at[1, 3]),
+    )
+    for index in range(3):
+        for copy in peer_copies(index):
+            copy.start()
+    for copy in own_peer:
         copy.start()
-        copy.wait()
-
-    def tile_load(unit, t):
-        return pltpu.make_async_copy(
-            whole_ref.at[unit, t // 2, t % 2], wb.at[t % 2], tile_sem.at[t % 2]
-        )
-
-    def each_tile(unit, use):
-        tile_load(unit, 0).start()
-
-        def one(t, carry):
-            pl.when(t < 3)(lambda: tile_load(unit, t + 1).start())
-            tile_load(unit, t).wait()
-            use(t, t % 2)
-            return carry
-
-        lax.fori_loop(0, 4, one, 0)
+
+    def tile_pieces(uses):
+        def load(index):
+            unit, t, use = uses[index]
+            return pltpu.make_async_copy(
+                whole_ref.at[unit, t // 2, t % 2], wb.at[index % 2], tile_sem.at[index % 2]
+            )
+
+        def piece(index):
+            def run():
+                if index == 0:
+                    load(0).start()
+                if index + 1 < len(uses):
+                    load(index + 1).start()
+                load(index).wait()
+                uses[index][2](uses[index][1], index % 2)
+
+            return run
+
+        return [piece(index) for index in range(len(uses))]
 
     def tile(slot, first, last):
         return wb[slot, :, :, :, first:last].reshape(C, last - first)
@@ -410,177 +459,243 @@
 
         lax.fori_loop(0, 2, one, 0)
 
+    turned_before = [None]
+
     def turn_to(source, index):
-        def one(step, carry):
-            lanes = pl.ds(pl.multiple_of(step * 128, 128), 128)
-            ptb[lanes, :] = source[:, lanes].T
-            return carry
-
-        lax.fori_loop(0, C // 128, one, 0)
-        save(ptb, pt_ref.at[index])
+        begin, wait = save(ptb, pt_ref.at[index])
+        earlier, turned_before[0] = turned_before[0], wait
+
+        def run():
+            if earlier is not None:
+                earlier()
+
+            def one(step, carry):
+                lanes = pl.ds(pl.multiple_of(step * 128, 128), 128)
+                ptb[lanes, :] = source[:, lanes].T
+                return carry
+
+            lax.fori_loop(0, C // 128, one, 0)
+            begin()
+
+        return run
 
     chunk = 4 * FRAMES
 
     def normalise(bias, norm, positions):
         def one(step, carry):
             rows = pl.ds(pl.multiple_of(step * chunk, chunk), chunk)
-            values = stream[rows, :] + biases_ref[bias : bias + 1, :]
+            values = stream[rows, :] + joined_ref[8 + bias : 9 + bias, :]
             stream[rows, :] = values
             centre = jnp.mean(values, axis=1, keepdims=True)
             offset = values - centre
             inverse = lax.rsqrt(jnp.mean(offset * offset, axis=1, keepdims=True) + 1e-05)
-            normed = offset * inverse * gains_ref[norm : norm + 1, :] + shifts_ref[norm : norm + 1, :]
+            normed = offset * inverse * joined_ref[norm : norm + 1, :]
+            normed = normed + joined_ref[4 + norm : 5 + norm, :]
             if positions:
                 normed = normed.reshape(chunk // FRAMES, FRAMES, C) + position_ref[...][None]
                 normed = normed.reshape(chunk, C)
             xb[rows, :] = normed.astype(jnp.bfloat16)
             return carry
 
-        lax.fori_loop(0, rows_all // chunk, one, 0)
-
-    def attention(place):
-        same = same_pixel(BLOCK)
-
-        def one(step, carry):
-            t, block = step // (rows_all // BLOCK), step % (rows_all // BLOCK)
-            rows = pl.ds(pl.multiple_of(block * BLOCK, BLOCK), BLOCK)
-            for head in range(width // HEAD):
-                low = head * HEAD
-                query = qkb[t, rows, low : low + HEAD]
-                key = qkb[t, rows, width + low : width + low + HEAD]
-                value = vb[t, rows, low : low + HEAD]
-                probs = head_probs(query, key, same, scale).astype(jnp.bfloat16)
-                attb[t, rows, place + low : place + low + HEAD] = dot_plain(probs, value).astype(
-                    jnp.bfloat16
-                )
-            return carry
-
-        lax.fori_loop(0, 4 * (rows_all // BLOCK), one, 0)
-
-    def attention_block(block):
-        normalise(block, 1 + block, True)
-        save(stream, stream_out_ref.at[block])
-
-        def qk_tile(t, slot):
+        def run():
+            lax.fori_loop(0, rows_all // chunk, one, 0)
+
+        return run
+
+    def attention(block, t):
+        place = (1 - block) * width
+
+        def run():
+            same = same_pixel(BLOCK)
+            for start in range(0, rows_all, BLOCK):
+                here = slice(start, start + BLOCK)
+                for head in range(width // HEAD):
+                    low = head * HEAD
+                    query = qkb[block, t, here, low : low + HEAD]
+                    key = qkb[block, t, here, width + low : width + low + HEAD]
+                    value = vb[block, t, here, low : low + HEAD]
+                    probs = head_probs(query, key, same, scale).astype(jnp.bfloat16)
+                    attb[block, t, here, place + low : place + low + HEAD] = dot_plain(
+                        probs, value
+                    ).astype(jnp.bfloat16)
+            empty = pl.ds(0, width) if block == 0 else pl.ds(width, width)
+            attb[block, t, :, empty] = jnp.zeros((rows_all, width), jnp.bfloat16)
+
+        return run
+
+    def join_input():
+        for index in range(3):
+            for copy in peer_copies(index):
+                copy.wait_recv()
+        for copy in own_peer:
+            copy.wait()
+        for t in range(4):
+            lanes = slice(t * width, (t + 1) * width)
+            joined_ref[:, lanes] = params_got[t, 0:16, :]
+            xb[:, lanes] = x_got[t]
+            for half in range(2):
+                for part in range(2):
+                    row = 16 + 2 * half + part
+                    hidden_bias[t, half : half + 1, part * width : (part + 1) * width] = params_got[
+                        t, row : row + 1, :
+                    ]
+
+    def in_tile(t, slot):
+        def sink(rows, total):
+            stream[rows, t * width : (t + 1) * width] = total[:, 64:384]
+
+        spread_tile(xb, slot, 256, WIDE, sink)
+
+    def qk_tile(block):
+        def use(t, slot):
             def sink(rows, total):
-                qkb[t, rows, :] = total.astype(jnp.bfloat16)
+                qkb[block, t, rows, :] = total.astype(jnp.bfloat16)
 
             spread_tile(xb, slot, 0, WIDE, sink)
 
-        def v_tile(t, slot):
+        return use
+
+    def v_tile(block):
+        def use(t, slot):
             def sink(rows, total):
-                vb[t, rows, :] = total[:, :width].astype(jnp.bfloat16)
+                vb[block, t, rows, :] = total[:, :width].astype(jnp.bfloat16)
 
             spread_tile(xb, slot, 0, 384, sink)
 
-        each_tile(2 * block, qk_tile)
-        each_tile(2 * block + 1, v_tile)
-        attb[...] = jnp.zeros_like(attb)
-        attention((1 - block) * width)
-        save(attb, q_ref.at[10 if block == 0 else 4])
-        save(qkb, qk_ref.at[block])
-        save(vb, v_ref.at[block])
-        turn_to(xb, 4 - block)
-
-    def before_units():
-        turn_to(x_ref, 7)
-        save(moved_part_ref, q_ref.at[9])
-
-    def after_1():
-        for t in range(4):
-            tile_load(1, t).start()
-            tile_load(1, t).wait()
-
-            def sink(rows, total, t=t):
-                stream[rows, t * width : (t + 1) * width] = total[:, 64:384]
-
-            spread_tile(x_ref, t % 2, 256, WIDE, sink)
-        attention_block(0)
-
-    def after_3():
-        each_tile(3, lambda t, slot: collapse_tile(attb, t, slot, 256, WIDE))
-        attention_block(1)
-
-    def after_4():
-        each_tile(4, lambda t, slot: collapse_tile(attb, t, slot, 0, 384))
-        normalise(2, 3, False)
-        save(stream, stream_out_ref.at[2])
-        turn_to(xb, 1)
-
-    def after_up(half):
-        def up_tile(t, slot):
+        return use
+
+    def up_tile(half):
+        def use(t, slot):
             def sink(rows, total):
-                pre = total + hidden_bias_ref[t, half]
+                pre = total + hidden_bias[t, half : half + 1, :]
                 below = 0.5 * (1.0 + lax.erf(pre * math.sqrt(0.5)))
                 hid[half, t, rows, :] = (pre * below).astype(jnp.bfloat16)
                 density = jnp.exp(-0.5 * pre * pre) * (1.0 / math.sqrt(2.0 * math.pi))
-                slopeb[t, rows, :] = (below + pre * density).astype(jnp.bfloat16)
+                slopeb[half, t, rows, :] = (below + pre * density).astype(jnp.bfloat16)
 
             spread_tile(xb, slot, 0, WIDE, sink)
 
-        each_tile(5 + half, up_tile)
-        save(hid.at[half], q_ref.at[1 - half])
-        save(slopeb, slope_ref.at[half])
-
-    def after_down(half):
-        each_tile(7 + half, lambda t, slot: collapse_tile(hid.at[half], t, slot, 0, WIDE))
-        if half == 0:
-            return
-
-        def finish(step, carry):
+        return use
+
+    def down_tile(half):
+        return lambda t, slot: collapse_tile(hid.at[half], t, slot, 0, WIDE)
+
+    def last_stream():
+        def one(step, carry):
             rows = pl.ds(pl.multiple_of(step * chunk, chunk), chunk)
-            xb[rows, :] = (stream[rows, :] + biases_ref[3:4, :]).astype(jnp.bfloat16)
+            xb[rows, :] = (stream[rows, :] + joined_ref[11:12, :]).astype(jnp.bfloat16)
             return carry
 
-        lax.fori_loop(0, rows_all // chunk, finish, 0)
-
-        def moved_tile(t, slot):
-            def sink(rows, total):
-                moved_ref[t, rows, :] = (total[:, 64:384] + out_bias_ref[t]).astype(jnp.bfloat16)
-
-            spread_tile(xb, slot, 256, WIDE, sink)
-
-        each_tile(4, moved_tile)
-        turn_to(xb, 5)
-
+        lax.fori_loop(0, rows_all // chunk, one, 0)
+
+    def moved_tile(t, slot):
+        def sink(rows, total):
+            moved_ref[t, rows, :] = (total[:, 64:384] + params_got[t, 12:13, :]).astype(
+                jnp.bfloat16
+            )
+
+        spread_tile(xb, slot, 256, WIDE, sink)
+
+    four = range(4)
+    streams = [save(stream, stream_out_ref.at[index]) for index in range(3)]
+    kept = [
+        (
+            save(attb.at[block], q_ref.at[10 if block == 0 else 4]),
+            save(qkb.at[block], qk_ref.at[block]),
+            save(vb.at[block], v_ref.at[block]),
+        )
+        for block in range(2)
+    ]
+    hid_save = [save(hid.at[half], q_ref.at[1 - half]) for half in range(2)]
+    slope_save = [save(slopeb.at[half], slope_ref.at[half]) for half in range(2)]
+
+    def start_saves(*saves):
+        def run():
+            for begin, wait in saves:
+                begin()
+
+        return run
+
+    input_turn = turn_to(xb, 7)
     unit_work = {
-        1: after_1,
-        3: after_3,
-        4: after_4,
-        5: lambda: after_up(0),
-        6: lambda: after_up(1),
-        7: lambda: after_down(0),
-        8: lambda: after_down(1),
+        1: tile_pieces([(1, t, in_tile) for t in four])
+        + [normalise(0, 1, True), start_saves(streams[0])]
+        + tile_pieces([(0, t, qk_tile(0)) for t in four] + [(1, t, v_tile(0)) for t in four]),
+        2: [turn_to(xb, 4)]
+        + [attention(0, t) for t in four]
+        + [start_saves(*kept[0]), streams[0][1]],
+        3: tile_pieces(
+            [(3, t, lambda t, slot: collapse_tile(attb.at[0], t, slot, 256, WIDE)) for t in four]
+        )
+        + [normalise(1, 2, True), start_saves(streams[1])]
+        + tile_pieces([(2, t, qk_tile(1)) for t in four] + [(3, t, v_tile(1)) for t in four]),
+        4: [turn_to(xb, 3)]
+        + [attention(1, t) for t in four]
+        + [start_saves(*kept[1]), streams[1][1]]
+        + tile_pieces(
+            [(4, t, lambda t, slot: collapse_tile(attb.at[1], t, slot, 0, 384)) for t in four]
+        )
+        + [normalise(2, 3, False), start_saves(streams[2])],
+        5: [turn_to(xb, 1)]
+        + tile_pieces([(5, t, up_tile(0)) for t in four])
+        + [start_saves(hid_save[0], slope_save[0])],
+        6: tile_pieces([(6, t, up_tile(1)) for t in four])
+        + [start_saves(hid_save[1], slope_save[1]), streams[2][1]],
+        7: tile_pieces([(7, t, down_tile(0)) for t in four]),
+        8: tile_pieces([(8, t, down_tile(1)) for t in four])
+        + [last_stream]
+        + tile_pieces([(4, t, moved_tile) for t in four])
+        + [turn_to(xb, 5)],
     }
 
     def advance(turn, carry):
-        for number in reversed(range(len(stages))):
+        count = len(stages)
+        ready = turn - (count - 1)
+        for place, number in enumerate(reversed(range(count))):
             unit = turn - number
 
             @pl.when((unit >= 0) & (unit < UNITS))
             def _(number=number, unit=unit):
                 stages[number](unit)
 
-        pl.when(turn == 1)(before_units)
-        ready = turn - (len(stages) - 1)
-        for unit, work in unit_work.items():
-            pl.when(ready == unit)(work)
+            for owner, pieces in unit_work.items():
+                size = len(pieces)
+                mine = pieces[size * place // count : size * (place + 1) // count]
+                if mine:
+
+                    @pl.when(ready == owner)
+                    def _(mine=mine):
+                        for piece in mine:
+                            piece()
+
+        @pl.when(turn == 2)
+        def _():
+            join_input()
+            input_turn()
+
         return carry
 
     lax.fori_loop(0, UNITS + len(stages) - 1, advance, 0)
-
-
-def forward_all(shards, rows_in, gains, shifts, biases, hidden_bias, position, moved_part):
+    for wait in (
+        [turned_before[0]]
+        + [entry[1] for group in kept for entry in group]
+        + [entry[1] for entry in hid_save + slope_save]
+    ):
+        wait()
+    for index in range(3):
+        for copy in peer_copies(index):
+            copy.wait_send()
+
+
+def forward_all(shards, rows_in, params, position):
     units, share, wide = shards.shape
-    rows, width = rows_in.shape[0], wide // 2
+    rows, width = rows_in.shape[1], rows_in.shape[2]
     low = jnp.bfloat16
-    out_bias = biases[4].reshape(4, 1, width)
-    hidden_bias = hidden_bias.reshape(4, 2, 1, wide)
     anywhere, near = pl.BlockSpec(memory_space=pl.ANY), pl.BlockSpec(memory_space=pltpu.VMEM)
     return pl.pallas_call(
         forward_kernel,
-        in_specs=[anywhere] + [near] * 7 + [anywhere],
-        out_specs=[anywhere] * 7 + [near],
+        in_specs=[anywhere, anywhere, near, near],
+        out_specs=[anywhere] * 7 + [near] * 2,
         out_shape=[
             jax.ShapeDtypeStruct((units, 2, 2, 4, 2, share, wide), low),
             jax.ShapeDtypeStruct((12, 4, rows, wide), low),
@@ -590,28 +705,34 @@
             jax.ShapeDtypeStruct((2, 4, rows, width), low),
             jax.ShapeDtypeStruct((2, 4, rows, wide), low),
             jax.ShapeDtypeStruct((4, rows, width), low),
+            jax.ShapeDtypeStruct((16, C), jnp.float32),
         ],
         scratch_shapes=[
             pltpu.VMEM((rows, C), jnp.float32),
             pltpu.VMEM((rows, C), low),
             pltpu.VMEM((C, rows), low),
-            pltpu.VMEM((4, rows, wide), low),
             pltpu.VMEM((4, rows, width), low),
-            pltpu.VMEM((4, rows, wide), low),
+            pltpu.VMEM((4,) + params.shape, jnp.float32),
+            pltpu.VMEM((4, 8, wide), jnp.float32),
             pltpu.VMEM((2, 4, rows, wide), low),
-            pltpu.VMEM((4, rows, wide), low),
+            pltpu.VMEM((2, 4, rows, width), low),
+            pltpu.VMEM((2, 4, rows, wide), low),
+            pltpu.VMEM((2, 4, rows, wide), low),
+            pltpu.VMEM((2, 4, rows, wide), low),
             pltpu.VMEM((2, 4, 2, share, wide), low),
             pltpu.SemaphoreType.DMA((2,)),
-            pltpu.SemaphoreType.DMA((1,)),
+            pltpu.SemaphoreType.DMA((24,)),
+            pltpu.SemaphoreType.DMA((2, 4)),
+            pltpu.SemaphoreType.DMA((2, 3)),
             pltpu.SemaphoreType.DMA((units,)),
             pltpu.SemaphoreType.DMA((units, 2, 5)),
             pltpu.SemaphoreType.DMA((units, 2, 2, 4, 2)),
             pltpu.SemaphoreType.DMA((units, 3)),
         ],
         compiler_params=pltpu.CompilerParams(
-            collective_id=0, has_side_effects=True, vmem_limit_bytes=58 << 20
+            collective_id=0, has_side_effects=True, vmem_limit_bytes=60 << 20
         ),
-    )(shards, rows_in, gains, shifts, biases, out_bias, hidden_bias, position, moved_part)
+    )(shards, rows_in, params, position)
 
 
 def reduce_kernel(
@@ -988,11 +1109,14 @@
     return jnp.stack(reduced[::-1], 0)
 
 
-def to_pixels(values, tensor_size):
+def by_pixels(values, tensor_size):
     slots, frames, width, pixels = values.shape
     own = pixels // tensor_size
-    turned = jnp.transpose(values, (3, 0, 1, 2)).reshape(tensor_size, own * slots * frames, width)
-    return lax.all_to_all(turned, "tensor", 0, 0, tiled=True)
+    return jnp.transpose(values, (3, 0, 1, 2)).reshape(tensor_size, own * slots * frames, width)
+
+
+def exchange(parts):
+    return lax.all_to_all(parts, "tensor", 0, 0, tiled=True)
 
 
 def to_channels(values, slots, pixels):
@@ -1036,14 +1160,9 @@
     down_turned = weight_down.T
     shards += [down_turned[:, :wide], down_turned[:, wide:]]
     shards = jnp.stack(shards, 0)
-    packed = jnp.concatenate([norm_gain, norm_shift, channel_bias], 0)
-    packed = lax.all_gather(
-        jnp.concatenate([packed.reshape(-1), hidden_bias]), "tensor", axis=0, tiled=False
-    )
-    channel_params = packed[:, : 13 * width].reshape(tensor_size, 13, width)
-    channel_params = jnp.transpose(channel_params, (1, 0, 2)).reshape(13, C)
-    gains, shifts, biases = channel_params[:4], channel_params[4:8], channel_params[8:]
-    hidden_full = packed[:, 13 * width :]
+    params = jnp.zeros((24, width), jnp.float32)
+    params = params.at[:13].set(side([norm_gain, norm_shift, channel_bias], 0))
+    params = params.at[16:20].set(hidden_bias.reshape(4, width))
 
     start = latent.astype(jnp.float32)
     cot = cotangent.astype(jnp.float32)
@@ -1054,28 +1173,26 @@
     group_inverse = lax.rsqrt(jnp.mean(offset * offset, axis=(1, 3, 4), keepdims=True) + 1e-06)
     group_hat = (offset * group_inverse).reshape(start.shape)
     normed = group_hat * norm_gain[0][:, None] + norm_shift[0][:, None]
-    arrived = to_pixels(normed.astype(jnp.bfloat16), tensor_size)
-    rows = arrived.shape[1]
-    inputs_in = jnp.transpose(arrived, (1, 0, 2)).reshape(rows, C)
+    sent = by_pixels(normed.astype(jnp.bfloat16), tensor_size)
+    rows = sent.shape[1]
 
     grad_moved_local = jnp.where(flags, cot, 0.0)
     bias_moved = jnp.sum(grad_moved_local, axis=(0, 1, 3))
-    grad_moved = to_pixels(grad_moved_local.astype(jnp.bfloat16), tensor_size)
+    grad_moved = exchange(by_pixels(grad_moved_local.astype(jnp.bfloat16), tensor_size))
 
     if by_kernel:
-        empty = jnp.zeros((tensor_size, rows, width), jnp.bfloat16)
-        whole, q_all, pt_all, streams, qk_all, v_all, slopes, moved = forward_all(
-            shards,
-            inputs_in,
-            gains,
-            shifts,
-            biases,
-            hidden_full,
-            make_positions(),
-            side([empty, grad_moved], 2),
-        )
+        whole, q_all, pt_all, streams, qk_all, v_all, slopes, moved, joined = forward_all(
+            shards, sent, params, make_positions()
+        )
+        gains = joined[:4]
         whole = whole.reshape(UNITS, tensor_size, C, wide)
     else:
+        arrived = exchange(sent)
+        inputs_in = jnp.transpose(arrived, (1, 0, 2)).reshape(rows, C)
+        packed = lax.all_gather(params, "tensor", axis=0, tiled=False)
+        joined = jnp.transpose(packed[:, :13], (1, 0, 2)).reshape(13, C)
+        gains, shifts, biases = joined[:4], joined[4:8], joined[8:]
+        hidden_full = packed[:, 16:20].reshape(tensor_size, 2 * wide)
         whole = gather_plain(shards)
     full_qk = (whole[0], whole[2])
     full_v = (whole[1, :, :, :width], whole[3, :, :, :width])
@@ -1134,12 +1251,12 @@
     turned, parts = [None] * 8, [None] * 12
     if by_kernel:
         turned[1], turned[5], turned[7] = pt_all[1], pt_all[5], pt_all[7]
-        for index in (0, 1, 4, 9, 10):
+        for index in (0, 1, 4, 10):
             parts[index] = q_all[index]
     else:
         turned[1], turned[5], turned[7] = inputs_up.T, inputs_proj.T, inputs_in.T
-        parts[9] = side([empty, grad_moved], 2)
         parts[0], parts[1] = hidden[1], hidden[0]
+    parts[9] = side([empty, grad_moved], 2)
     grad_stream = collapse(grad_moved, full_proj)
     bias_grads[3] = jnp.sum(grad_stream, 0)
     grad_low = grad_stream.astype(jnp.bfloat16)

time: 1090 us -> 959 us (0.88)
  Pallas kernels: 704 us -> 604 us
  waiting for transfers between devices: 22.8 us -> 3.79 us
  local copies, waits for them, and re-layouts: 170 us -> 157 us
    pallas_call x1, Pallas kernels: 395 us -> 295 us  [forward_all(): pl.pallas_call(forward_kernel, in_specs=[anywhere, anywhere, near, near],...]
    unnamed x4 -> x2, waiting for transfers between devices: 12.2 us -> 0.04 us
    unnamed x140 -> x149, local copies, waits for them, and re-layouts: 60.1 us -> 59.9 us
  transfers between devices with their start and end apart: 6 -> 4, of which waited for: 3 -> 1; matrix products, arithmetic and copies ran while one was open for 7% -> 25% of each run, Pallas kernels for 25% -> 63%
where the time goes in v4:
time: 959 us; the launch traced here: 952 us
  Pallas kernels  604 us (63%)
  local copies, waits for them, and re-layouts  157 us (16%)
  matrix products  84.7 us (9%)
  other arithmetic  39.3 us (4%)
  blocking collectives  35.5 us (4%)
  between operations  16.1 us (2%)
  starting transfers between devices  12.3 us (1%)
    pallas_call x1, Pallas kernels, forward_all(): pl.pallas_call(forward_kernel, in_specs=[anywhere, anywhere, near, near],...  295 us
    pallas_call x1, Pallas kernels, reduce_all(): pl.pallas_call(reduce_kernel, in_specs=[pl.BlockSpec(memory_space=pl.ANY)...  275 us
    unnamed x149, local copies, waits for them, and re-layouts  59.9 us
    dot_general x8, matrix products, collapse(): jnp.einsum('trn,tkn->rk', parts, weight, preferred_element_type=jnp.float32)  54 us
    psum x1, blocking collectives, body(): lax.psum(jnp.concatenate([vectors, group_gain_grad, group_shift_grad, bia...  35.5 us
    pallas_call x2, Pallas kernels, attend_back(): pl.pallas_call(partial(attend_back_kernel, 1.0 / math.sqrt(HEAD)), grid=(...  34.1 us
    dot_general x4, matrix products, spread(): jnp.einsum('rk,tkn->trn', rows, weight, preferred_element_type=jnp.float32)  30.7 us
    slice x1, local copies, waits for them, and re-layouts, body(): full_qk = (whole[0], whole[2])  26.6 us
  transfers between devices with their start and end apart: 4, of which 1 were waited for; matrix products, arithmetic and copies ran while one was open for 25% of the time, Pallas kernels for 63%

profile of v4, /device:TPU:0, one launch (start us, length us, event | category | flops | bytes accessed | tf_op | source)
XLA Modules:
  0.0 952.4 jit_solution(601929579011581764)
XLA Ops:
  11.8 4.4 all-to-all-start.1
  28.1 294.8 %shard_map.220 = (bf16[9,2,2,4,2,160,640]{6,5,4,3,2,1,0:T(8,128)(2,1)}, bf16[12,4,512,640]{3,2,1,0:T(8,128)(2,1)}, bf16[8,1280,512]{2,1,0:T(8,128)(2,1)}, f32[3,...) custom-call(bf16[9,160,640]{2,1,0:T(8,128)(2,1)} %copy-done.31, ...), custom_call_target="tpu_custom_call" | custom-call | tf_op jit(solution)/shard_map/pallas_call | solution.py:695
  323.0 9.1 copy.181
  338.1 26.6 %fusion.65 = (bf16[1,2,2,4,2,160,640]{6,5,4,3,2,1,0:T(8,128)(2,1)}, bf16[1,2,2,4,2,160,640]{6,5,4,3,2,1,0:T(8,128)(2,1)}, bf16[1,2,2,4,2,160,640]{6,5,4,3,2,1,0:...) fusion(bf16[9,2,2,4,2,160,640]{6,5,4,3,2,1,0:T(8,128)(2,1)} %ge, ...), kind=kLoop, calls=%fused_computation.196 | loop fusion | bytes 78643200 | tf_op jit(solution)/shard_map/slice | solution.py:1197
  375.6 5.4 fusion.66
  381.0 4.6 slice_bitcast_fusion.26
  390.0 7.5 fusion.71
  404.2 8.4 fusion.43
  412.7 10.9 %fusion.16 = (f32[4,640]{1,0:T(4,128)S(1)}, f32[4,640]{1,0:T(4,128)S(1)}, bf16[4,512,640]{2,1,0:T(8,128)(2,1)}, bf16[4,512,640]{2,1,0:T(8,128)(2,1)}) fusion(bf16[2,4,512,640]{3,2,1,0:T(8,128)(2,1)} %get-tuple-element.53, f32[4,640,512]{1,2,0:T(8,128)} %fusion.43, bf16[4,1280,640]{2,1,0:T(8,128)(2,1)} %bitcast.323, f32[512,1280]{0,1:T(8,128)S(1)} %copy-done.12), kind=kOutput, calls=%fused_computation.31 | convolution fusion | flops 3366579200 | bytes 24924160 | tf_op jit(solution)/shard_map/rk,tkn->trn/dot_general | solution.py:20
  423.6 8.9 convolution_bitcast_fusion.3
  432.5 6.5 multiply_reduce_fusion.1
  445.0 5.1 fusion.37
  452.1 4.4 slice_dynamic-update-slice_fusion
  463.6 17.0 %shard_map.221 = (bf16[4,512,640]{2,1,0:T(8,128)(2,1)S(1)}, bf16[4,512,320]{2,1,0:T(8,128)(2,1)S(1)}) custom-call(bf16[4,512,640]{2,1,0:T(8,128)(2,1)S(1)} %copy-done, bf16[4,512,320]{2,1,0:T(8,128)(2,1)S(1)} %copy-done.2, bf16[4,512,320]{2,1,0:T(8,128)(2,1)S(1)} %bitcast.292), custom_call_target="tpu_custom_call" | custom-call | tf_op jit(solution)/shard_map/pallas_call | solution.py:128
  480.7 7.5 convolution_bitcast_fusion.1
  488.3 5.1 multiply_reduce_fusion.2
  496.8 6.3 fusion.38
  509.0 17.0 %shard_map.222 = (bf16[4,512,640]{2,1,0:T(8,128)(2,1)S(1)}, bf16[4,512,320]{2,1,0:T(8,128)(2,1)S(1)}) custom-call(bf16[4,512,640]{2,1,0:T(8,128)(2,1)S(1)} %get-tuple-element.153.qk_ref, bf16[4,512,320]{2,1,0:T(8,128)(2,1)S(1)} %copy-done.1, bf16[4,512,320]{2,1,0:T(8,128)(2,1)S(1)} %bitcast.291), custom_call_target="tpu_custom_call" | custom-call | tf_op jit(solution)/shard_map/pallas_call | solution.py:128
  526.4 6.4 convolution_bitcast_fusion
  532.8 5.3 multiply_reduce_fusion.3
  540.6 6.7 fusion.33
  586.3 275.3 %shard_map.223 = (f32[9,160,640]{2,1,0:T(8,128)}, bf16[8,1280,512]{2,1,0:T(8,128)(2,1)}, bf16[12,2,512,640]{3,2,1,0:T(8,128)(2,1)}) custom-call(bf16[8,1280,512]{2,1,0:T(8,128)(2,1)} %slice_dynamic-update-slice_fusion.1.pt_ref, bf16[12,2,2,512,640]{4,3,2,1,0:T(8,128)(2,1)} %constant_dynamic-update-slice_fusion.2.q_ref), custom_call_target="tpu_custom_call" | custom-call | tf_op jit(solution)/shard_map/pallas_call | solution.py:1050
  894.8 6.7 fusion.6
  901.9 35.5 %psum.7 = f32[5440]{0:T(1024)S(1)} all-reduce(f32[5440]{0:T(1024)S(1)} %concatenate.62), channel_id=1, replica_groups=mesh['dp'=8,'tensor'=4] {'dp'}, use_global_device_ids=true, to_apply=%region_36.37 | all-reduce | flops 5440 | bytes 43520 | tf_op jit(solution)/shard_map/psum | solution.py:1329
  (278 shorter events, 150.7 us)
Async XLA Ops:
  11.8 373.8 %all-to-all-start.1 = ((bf16[4,512,320]{1,2,0:T(8,128)(2,1)}), bf16[4,512,320]{1,2,0:T(8,128)(2,1)}, u32[]{:S(2)}, u32[]{:S(2)}) async-start(bf16[4,512,320]{1,2,0:T(8,128)(2,1)} %copy.179), calls=%async_computation.1 | async-start | bytes 2621440 | tf_op jit(solution)/shard_map/all_to_all | solution.py:1119
  24.2 298.7 %copy-start.43 = (f32[320]{0:T(512)}, f32[320]{0:T(512)S(1)}, u32[]{:S(2)}) copy-start(f32[320]{0:T(512)S(1)} %sub.108) | copy-start | bytes 3844
  25.1 297.8 %copy-start.45 = (f32[320]{0:T(512)}, f32[320]{0:T(512)S(1)}, u32[]{:S(2)}) copy-start(f32[320]{0:T(512)S(1)} %mul.232) | copy-start | bytes 3844
  25.2 297.8 %copy-start.47 = (f32[320]{0:T(512)}, f32[320]{0:T(512)S(1)}, u32[]{:S(2)}) copy-start(f32[320]{0:T(512)S(1)} %get-tuple-element.192) | copy-start | bytes 3844
  338.1 26.6 %copy-start.27 = (bf16[2,4,512,320]{3,2,1,0:T(8,128)(2,1)S(1)}, bf16[2,4,512,320]{3,2,1,0:T(8,128)(2,1)}, u32[]{:S(2)}) copy-start(bf16[2,4,512,320]{3,2,1,0:T(8,128)(2,1)} %get-tuple-element.56) | copy-start | bytes 7864324
  385.6 481.4 %all-to-all-start = ((bf16[4,512,320]{1,2,0:T(8,128)(2,1)}), bf16[4,512,320]{1,2,0:T(8,128)(2,1)}, u32[]{:S(2)}, u32[]{:S(2)}) async-start(bf16[4,512,320]{1,2,0:T(8,128)(2,1)} %copy.176), calls=%async_computation | async-start | bytes 2621440 | tf_op jit(solution)/shard_map/all_to_all | solution.py:1124
  389.9 492.5 %all-reduce.8.cloned.1.call-start = ((), (), s32[]{:S(2)}) async-start(), calls=%async_computation.3 | async-start | bytes 143360
  404.2 28.3 %slice-start = ((s8[7864320]{0:T(1024)(128)(4,1)}), s8[4194304]{0:T(1024)(128)(4,1)S(1)}, s32[]{:S(2)}) async-start(s8[7864320]{0:T(1024)(128)(4,1)} %bitcast.295), calls=%async_computation.4 | async-start | bytes 8388608
  404.2 28.3 %slice-start.6 = ((s8[6553600]{0:T(1024)(128)(4,1)}), s8[4194304]{0:T(1024)(128)(4,1)S(1)}, s32[]{:S(2)}) async-start(s8[6553600]{0:T(1024)(128)(4,1)} %bitcast.319), calls=%async_computation.10 | async-start | bytes 8388608
  412.7 19.8 %slice-start.1 = ((s8[7864320]{0:T(1024)(128)(4,1)}), s8[3670016]{0:T(1024)(128)(4,1)S(1)}, s32[]{:S(2)}) async-start(s8[7864320]{0:T(1024)(128)(4,1)} %bitcast.295), calls=%async_computation.5 | async-start | bytes 7340032
  412.7 19.8 %slice-start.7 = ((s8[6553600]{0:T(1024)(128)(4,1)}), s8[2359296]{0:T(1024)(128)(4,1)S(1)}, s32[]{:S(2)}) async-start(s8[6553600]{0:T(1024)(128)(4,1)} %bitcast.319), calls=%async_computation.11 | async-start | bytes 4718592
  423.6 9.0 copy-start.28
  463.6 24.6 %slice-start.2 = ((s8[7864320]{0:T(1024)(128)(4,1)}), s8[3670016]{0:T(1024)(128)(4,1)S(1)}, s32[]{:S(2)}) async-start(s8[7864320]{0:T(1024)(128)(4,1)} %bitcast.297), calls=%async_computation.6 | async-start | bytes 7340032
  480.6 7.6 copy-start.5
  480.6 7.6 copy-start.9
  480.6 7.6 slice-start.3
  509.0 23.8 %slice-start.4 = ((s8[7864320]{0:T(1024)(128)(4,1)}), s8[3670016]{0:T(1024)(128)(4,1)S(1)}, s32[]{:S(2)}) async-start(s8[7864320]{0:T(1024)(128)(4,1)} %bitcast.299), calls=%async_computation.8 | async-start | bytes 7340032
  867.0 20.8 %all-to-all-start.2 = ((bf16[4,512,320]{1,2,0:T(8,128)(2,1)}), bf16[4,512,320]{1,2,0:T(8,128)(2,1)S(1)}, u32[]{:S(2)}, u32[]{:S(2)}) async-start(bf16[4,512,320]{1,2,0:T(8,128)(2,1)} %bitcast.62), calls=%async_computation.2 | async-start | bytes 2621440 | tf_op jit(solution)/shard_map/all_to_all | solution.py:1124
  882.3 8.6 copy-start.11
  882.3 8.6 copy-start.44
  882.3 8.6 copy-start.46
  882.4 8.6 copy-start.48
  894.7 6.7 copy-start.19
  901.5 39.3 %copy-start.17 = (f32[1,16,320,128]{2,1,3,0:T(8,128)S(1)}, f32[1,16,320,128]{2,1,3,0:T(8,128)}, u32[]{:S(2)}) copy-start(f32[1,16,320,128]{2,1,3,0:T(8,128)} %get-tuple-element.171) | copy-start | bytes 7864324
  (42 other events, 123.8 us)
Sparse Core Ops, SparseCore 0:
  554.1 34.1 all-reduce.7

commit v5 on v4

v5 whole, which is shorter than its diff:
```python
from functools import partial
import math

import jax
import jax.numpy as jnp
from jax import lax
from jax.experimental import pallas as pl
from jax.experimental.pallas import tpu as pltpu
from jax.sharding import PartitionSpec as P

C = 1280
GROUPS = 32
FRAMES = 16
HEAD = 160
BLOCK = 128
MIXED = ("tensor", "dp")


def spread(rows, weight):
    return jnp.einsum("rk,tkn->trn", rows, weight, preferred_element_type=jnp.float32)


def collapse(parts, weight):
    return jnp.einsum("trn,tkn->rk", parts, weight, preferred_element_type=jnp.float32)


def make_positions():
    channel_ids = jnp.arange(C)
    pair_rate = jnp.exp((channel_ids // 2).astype(jnp.float32) * (-2.0 * math.log(10000.0) / C))
    angles = jnp.arange(FRAMES).astype(jnp.float32)[:, None] * pair_rate[None, :]
    return jnp.where(channel_ids[None, :] % 2 == 0, jnp.sin(angles), jnp.cos(angles))


def layer_stats(stream):
    centre = jnp.mean(stream, axis=1, keepdims=True)
    offset = stream - centre
    inverse = lax.rsqrt(jnp.mean(offset * offset, axis=1, keepdims=True) + 1e-05)
    return offset * inverse, inverse


def layer_back(grad_out, normal_part, inverse, gain):
    scaled = grad_out * gain
    first = jnp.mean(scaled, axis=1, keepdims=True)
    second = jnp.mean(scaled * normal_part, axis=1, keepdims=True)
    grad_in = inverse * (scaled - first - normal_part * second)
    return grad_in, jnp.sum(grad_out * normal_part, 0), jnp.sum(grad_out, 0)


def dot_rows(left, right):
    return lax.dot_general(left, right, (((1,), (1,)), ((), ())), preferred_element_type=jnp.float32)


def dot_plain(left, right):
    return lax.dot_general(left, right, (((1,), (0,)), ((), ())), preferred_element_type=jnp.float32)


def dot_first(left, right):
    return lax.dot_general(left, right, (((0,), (0,)), ((), ())), preferred_element_type=jnp.float32)


def same_pixel(block):
    row = lax.broadcasted_iota(jnp.int32, (block, block), 0) // FRAMES
    col = lax.broadcasted_iota(jnp.int32, (block, block), 1) // FRAMES
    return row == col


def head_probs(query, key, same, scale):
    scores = jnp.where(same, dot_rows(query, key) * scale, -1e30)
    top = jnp.max(scores, axis=1, keepdims=True)
    weights = jnp.where(same, jnp.exp(scores - top), 0.0)
    return weights / jnp.sum(weights, axis=1, keepdims=True)


def attend_kernel(scale, qk_ref, v_ref, out_ref):
    rows, width = out_ref.shape[1], out_ref.shape[2]
    block = min(BLOCK, rows)
    same = same_pixel(block)
    for start in range(0, rows, block):
        for head in range(width // HEAD):
            here, low = slice(start, start + block), head * HEAD
            query = qk_ref[0, here, low : low + HEAD]
            key = qk_ref[0, here, width + low : width + low + HEAD]
            value = v_ref[0, here, low : low + HEAD]
            probs = head_probs(query, key, same, scale).astype(jnp.bfloat16)
            out_ref[0, here, low : low + HEAD] = dot_plain(probs, value).astype(jnp.bfloat16)


def part_spec(array):
    return pl.BlockSpec((1,) + array.shape[1:], lambda t: (t, 0, 0))


def attend(qk, values):
    return pl.pallas_call(
        partial(attend_kernel, 1.0 / math.sqrt(HEAD)),
        grid=(qk.shape[0],),
        in_specs=[part_spec(qk), part_spec(values)],
        out_specs=part_spec(values),
        out_shape=jax.ShapeDtypeStruct(values.shape, jnp.bfloat16),
        compiler_params=pltpu.CompilerParams(vmem_limit_bytes=32 << 20),
    )(qk, values)


def attend_back_kernel(scale, qk_ref, v_ref, grad_ref, dqk_ref, dv_ref):
    rows, width = grad_ref.shape[1], grad_ref.shape[2]
    block = min(BLOCK, rows)
    same = same_pixel(block)
    for start in range(0, rows, block):
        for head in range(width // HEAD):
            here, low = slice(start, start + block), head * HEAD
            query = qk_ref[0, here, low : low + HEAD]
            key = qk_ref[0, here, width + low : width + low + HEAD]
            value = v_ref[0, here, low : low + HEAD]
            grad = grad_ref[0, here, low : low + HEAD]
            probs = head_probs(query, key, same, scale)
            grad_probs = dot_rows(grad, value)
            centred = jnp.sum(probs * grad_probs, axis=1, keepdims=True)
            grad_raw = (probs * (grad_probs - centred) * scale).astype(jnp.bfloat16)
            dqk_ref[0, here, low : low + HEAD] = dot_plain(grad_raw, key).astype(jnp.bfloat16)
            dqk_ref[0, here, width + low : width + low + HEAD] = dot_first(grad_raw, query).astype(
                jnp.bfloat16
            )
            dv_ref[0, here, low : low + HEAD] = dot_first(probs.astype(jnp.bfloat16), grad).astype(
                jnp.bfloat16
            )


def attend_back(qk, values, grad):
    return pl.pallas_call(
        partial(attend_back_kernel, 1.0 / math.sqrt(HEAD)),
        grid=(qk.shape[0],),
        in_specs=[part_spec(qk), part_spec(values), part_spec(values)],
        out_specs=[part_spec(qk), part_spec(values)],
        out_shape=[
            jax.ShapeDtypeStruct(qk.shape, jnp.bfloat16),
            jax.ShapeDtypeStruct(values.shape, jnp.bfloat16),
        ],
        compiler_params=pltpu.CompilerParams(vmem_limit_bytes=32 << 20),
    )(qk, values, grad)


UNITS = 9
WIDE = 640
SLOTS_IN_FLIGHT = 6
SLOTS_RECEIVED = 4
ROWS_A = 96
MESH_ID = pl.DeviceIdType.MESH


class Place:
    def __init__(self):
        dp, tn = lax.axis_index("dp"), lax.axis_index("tensor")
        self.z, self.x = dp // 2, dp % 2
        self.y, self.c = tn // 2, tn % 2
        self.far_x, self.far_y = 1 - self.x, 1 - self.y
        self.to = {
            "x": (self.z * 2 + self.far_x, tn),
            "y": (dp, self.far_y * 2 + self.c),
            "core": (dp, self.y * 2 + 1 - self.c),
            "cross": (dp, self.far_y * 2 + 1 - self.c),
            "up": (dp + 2, tn),
            "down": (dp - 2, tn),
        }
        self.has_up = self.z < 3
        self.has_down = self.z > 0

    def greet(self):
        barrier = pltpu.get_barrier_semaphore()

        def hello(name):
            pl.semaphore_signal(barrier, inc=1, device_id=self.to[name], device_id_type=MESH_ID)

        for name in ("x", "y", "core", "cross"):
            hello(name)
        pl.when(self.has_up)(lambda: hello("up"))
        pl.when(self.has_down)(lambda: hello("down"))
        pl.semaphore_wait(barrier, 4 + (6 - self.z) // 4 + (self.z + 3) // 4)


class Plan:
    FIELDS = (("kind", 16), ("unit", 9), ("t", 4), ("aux", 80), ("slot", 2), ("fresh", 2), ("next", 37))

    def __init__(self, per_turn):
        self.per_turn = per_turn
        self.steps = {}

    def fill(self, turn, steps):
        tiles = [index for index, step in enumerate(steps) if step[1] is not None]
        for index, (kind, unit, t, aux) in enumerate(steps):
            slot = fresh = following = 0
            if unit is not None:
                order = tiles.index(index)
                slot, fresh = order % 2, int(order == 0)
                if order + 1 < len(tiles):
                    later = steps[tiles[order + 1]]
                    following = 1 + later[1] * 4 + later[2]
            values = (kind, unit or 0, t, aux, slot, fresh, following)
            code, scale = 0, 1
            for (name, size), value in zip(self.FIELDS, values):
                assert 0 <= value < size
                code += scale * value
                scale *= size
            place = turn * self.per_turn + index * self.per_turn // len(steps)
            assert place not in self.steps
            self.steps[place] = code

    def read(self, place):
        code = jnp.int32(0)
        for where, value in self.steps.items():
            code = code + jnp.where(place == where, jnp.int32(value), jnp.int32(0))
        out = {}
        for name, size in self.FIELDS:
            out[name] = code % size
            code = code // size
        return out


def await_bytes(ref, sem):
    pltpu.make_async_copy(ref, ref, sem).wait()


def forward_kernel(
    shard_ref,
    x_ref,
    params_ref,
    position_ref,
    whole_ref,
    q_ref,
    pt_ref,
    stream_out_ref,
    qk_ref,
    v_ref,
    slope_ref,
    moved_ref,
    joined_ref,
    stream,
    xb,
    ptb,
    x_got,
    params_got,
    hidden_bias,
    qkb,
    vb,
    cols,
    slopeb,
    first_rows,
    total,
    wb,
    tile_sem,
    save_sem,
    kept_sem,
    peer_send,
    peer_recv,
    local_sem,
    send_sem,
    recv_sem,
    core_sem,
):
    at = Place()
    z, x, y, c = at.z, at.x, at.y, at.c
    share = shard_ref.shape[1]
    cut = (pl.ds(0, ROWS_A), pl.ds(ROWS_A, share - ROWS_A))
    kinds = {"up": 0, "down": 1, "x": 2, "y": 3, "core": 4}
    at.greet()

    def send(unit, colour, yy, zz, xx, kind, own=False):
        place = whole_ref.at[unit, yy, c, zz, xx, cut[colour]]
        pltpu.make_async_remote_copy(
            src_ref=shard_ref.at[unit, cut[colour]] if own else place,
            dst_ref=place,
            send_sem=send_sem.at[unit, colour, kinds[kind]],
            recv_sem=recv_sem.at[unit, colour, yy, zz, xx],
            device_id=at.to[kind],
            device_id_type=MESH_ID,
        ).start()

    def arrived(unit, colour, yy, zz, xx):
        await_bytes(
            whole_ref.at[unit, yy, c, zz, xx, cut[colour]], recv_sem.at[unit, colour, yy, zz, xx]
        )

    def own_copy(unit):
        return pltpu.make_async_copy(
            shard_ref.at[unit], whole_ref.at[unit, y, c, z, x], local_sem.at[unit]
        )

    def to_core(unit, part):
        if part == 2:
            place = whole_ref.at[unit, :, c, :, :, cut[1]]
        else:
            place = whole_ref.at[unit, y if part == 0 else at.far_y, c, :, :, cut[0]]
        return pltpu.make_async_remote_copy(
            src_ref=place,
            dst_ref=place,
            send_sem=send_sem.at[unit, part // 2, 4],
            recv_sem=core_sem.at[unit, part],
            device_id=at.to["core"],
            device_id_type=MESH_ID,
        )

    def from_z(unit, colour, step, yy):
        @pl.when(z >= step)
        def _():
            zz = z - step
            arrived(unit, colour, yy, zz, x)
            pl.when(at.has_up)(lambda: send(unit, colour, yy, zz, x, "up"))
            send(unit, colour, yy, zz, x, "x")
            if colour == 0:
                send(unit, colour, yy, zz, x, "y")

        @pl.when(z + step <= 3)
        def _():
            zz = z + step
            arrived(unit, colour, yy, zz, x)
            pl.when(at.has_down)(lambda: send(unit, colour, yy, zz, x, "down"))
            send(unit, colour, yy, zz, x, "x")
            if colour == 0:
                send(unit, colour, yy, zz, x, "y")

    def from_x(unit, step):
        def one(zz):
            arrived(unit, 0, y, zz, at.far_x)
            send(unit, 0, y, zz, at.far_x, "y")

        if step == 0:
            one(z)
        else:
            pl.when(z >= step)(lambda: one(z - step))
            pl.when(z + step <= 3)(lambda: one(z + step))

    def stage0(unit):
        own_copy(unit).start()
        pl.when(at.has_up)(lambda: send(unit, 0, y, z, x, "up", True))
        pl.when(at.has_down)(lambda: send(unit, 0, y, z, x, "down", True))
        send(unit, 1, y, z, x, "y", True)
        send(unit, 0, y, z, x, "x", True)
        pl.when(at.has_up)(lambda: send(unit, 1, y, z, x, "up", True))
        pl.when(at.has_down)(lambda: send(unit, 1, y, z, x, "down", True))
        send(unit, 0, y, z, x, "y", True)
        send(unit, 1, y, z, x, "x", True)

    def stage1(unit):
        from_z(unit, 0, 1, y)
        arrived(unit, 1, at.far_y, z, x)
        pl.when(at.has_up)(lambda: send(unit, 1, at.far_y, z, x, "up"))
        pl.when(at.has_down)(lambda: send(unit, 1, at.far_y, z, x, "down"))
        send(unit, 1, at.far_y, z, x, "x")
        from_z(unit, 1, 1, y)
        from_x(unit, 0)

    def stage2(unit):
        from_z(unit, 0, 2, y)
        from_z(unit, 1, 1, at.far_y)
        from_z(unit, 1, 2, y)
        from_x(unit, 1)

    def stage3(unit):
        from_z(unit, 0, 3, y)
        from_z(unit, 1, 2, at.far_y)
        from_z(unit, 1, 3, y)
        from_x(unit, 2)

    def stage4(unit):
        from_z(unit, 1, 3, at.far_y)
        from_x(unit, 3)
        own_copy(unit).wait()
        to_core(unit, 0).start()

    def stage5(unit):
        for zz in range(4):
            for xx in range(2):
                arrived(unit, 0, at.far_y, zz, xx)
        to_core(unit, 1).start()
        for zz in range(4):
            for yy in range(2):
                arrived(unit, 1, yy, zz, at.far_x)
        to_core(unit, 2).start()

    def stage6(unit):
        other = 1 - c
        await_bytes(whole_ref.at[unit, y, other, :, :, cut[0]], core_sem.at[unit, 0])
        await_bytes(whole_ref.at[unit, at.far_y, other, :, :, cut[0]], core_sem.at[unit, 1])
        await_bytes(whole_ref.at[unit, :, other, :, :, cut[1]], core_sem.at[unit, 2])
        for colour in range(2):
            rows = cut[colour]
            await_bytes(whole_ref.at[unit, :, c, :, :, rows], send_sem.at[unit, colour, 4])
            whole_x = whole_ref.at[unit, 0, c, :, 0, rows] if colour == 0 else None
            if colour == 0:
                await_bytes(whole_x, send_sem.at[unit, 0, 2])
                await_bytes(whole_ref.at[unit, 0, c, :, :, rows], send_sem.at[unit, 0, 3])
            else:
                await_bytes(whole_ref.at[unit, 0, c, :, :, rows], send_sem.at[unit, 1, 2])
                await_bytes(whole_ref.at[unit, 0, c, 0, 0, rows], send_sem.at[unit, 1, 3])
            for level in range(3):

                def ups(level=level):
                    if colour == 0:
                        ref = whole_ref.at[unit, 0, c, pl.ds(0, level + 1), 0, rows]
                    else:
                        ref = whole_ref.at[unit, :, c, pl.ds(0, level + 1), 0, rows]
                    return ref

                pl.when(z == level)(
                    lambda level=level: await_bytes(ups(level), send_sem.at[unit, colour, 0])
                )
                pl.when(z == 3 - level)(
                    lambda level=level: await_bytes(ups(level), send_sem.at[unit, colour, 1])
                )

    stages = (stage0, stage1, stage2, stage3, stage4, stage5, stage6)

    rows_all, width = x_ref.shape[1], x_ref.shape[2]
    half_rows = rows_all // 2
    scale = 1.0 / math.sqrt(HEAD)
    own_t = y * 2 + c

    def save_now(source, target):
        copy = pltpu.make_async_copy(source, target, save_sem.at[0])
        copy.start()
        copy.wait()

    peers = (("y", at.far_y * 2 + c), ("core", y * 2 + 1 - c), ("cross", at.far_y * 2 + 1 - c))

    def peer_copies(index):
        kind, t = peers[index]
        target = {"device_id": at.to[kind], "device_id_type": MESH_ID}
        return (
            pltpu.make_async_remote_copy(
                src_ref=params_ref,
                dst_ref=params_got.at[own_t],
                send_sem=peer_send.at[0, index],
                recv_sem=peer_recv.at[0, index],
                **target,
            ),
            pltpu.make_async_remote_copy(
                src_ref=x_ref.at[t],
                dst_ref=x_got.at[own_t],
                send_sem=peer_send.at[1, index],
                recv_sem=peer_recv.at[1, index],
                **target,
            ),
        )

    own_peer = (
        pltpu.make_async_copy(params_ref, params_got.at[own_t], peer_send.at[0, 3]),
        pltpu.make_async_copy(x_ref.at[own_t], x_got.at[own_t], peer_send.at[1, 3]),
    )
    for index in range(3):
        for copy in peer_copies(index):
            copy.start()
    for copy in own_peer:
        copy.start()

    def each(count, size, use):
        def one(step, carry):
            use(pl.ds(pl.multiple_of(step * size, size), size))
            return carry

        lax.fori_loop(0, count, one, 0)

    def tile_load(unit, t, slot):
        return pltpu.make_async_copy(whole_ref.at[unit, t // 2, t % 2], wb.at[slot], tile_sem.at[slot])

    def kept_copies(which, t):
        target = (10, 4, 1, 0)[which]
        copies = [
            pltpu.make_async_copy(cols.at[which, t], q_ref.at[target, t], kept_sem.at[which, t, 0])
        ]
        if which < 2:
            pairs = [(qkb.at[which, t], qk_ref.at[which, t]), (vb.at[which, t], v_ref.at[which, t])]
        else:
            pairs = [(slopeb.at[which - 2, t], slope_ref.at[which - 2, t])]
        for index, (source, target_ref) in enumerate(pairs):
            copies.append(
                pltpu.make_async_copy(source, target_ref, kept_sem.at[which, t, 1 + index])
            )
        return copies

    def do_spread(op):
        matrix = op["slot"]
        t, aux = op["t"], op["aux"]

        def multiply(rows):
            total[rows, :] = dot_plain(xb[rows, :], wb[matrix].reshape(C, WIDE))

        each(2, half_rows, multiply)
        quarter = rows_all // 4

        @pl.when(aux == 0)
        def _():
            def use(rows):
                first_rows[t, rows, :] = total[rows, width:]

            each(4, quarter, use)

        @pl.when((aux == 1) | (aux == 3))
        def _():
            def use(rows):
                qkb[(aux - 1) // 2, t, rows, :] = total[rows, :].astype(jnp.bfloat16)

            each(4, quarter, use)

        @pl.when((aux == 2) | (aux == 4))
        def _():
            def use(rows):
                vb[(aux - 2) // 2, t, rows, :] = total[rows, 0:width].astype(jnp.bfloat16)

            each(4, quarter, use)

        @pl.when((aux == 5) | (aux == 6))
        def _():
            half = aux - 5

            def use(rows):
                pre = total[rows, :] + hidden_bias[t, pl.ds(half, 1), :]
                below = 0.5 * (1.0 + lax.erf(pre * math.sqrt(0.5)))
                cols[2 + half, t, rows, :] = (pre * below).astype(jnp.bfloat16)
                density = jnp.exp(-0.5 * pre * pre) * (1.0 / math.sqrt(2.0 * math.pi))
                slopeb[half, t, rows, :] = (below + pre * density).astype(jnp.bfloat16)

            each(rows_all // 32, 32, use)
            for which in (2, 3):

                @pl.when(half == which - 2)
                def _(which=which):
                    for copy in kept_copies(which, t):
                        copy.start()

        @pl.when(aux == 7)
        def _():
            def use(rows):
                moved_ref[t, rows, :] = (total[rows, width:] + params_got[t, 12:13, :]).astype(
                    jnp.bfloat16
                )

            each(4, quarter, use)

    def do_collapse(op):
        def multiply(rows):
            stream[rows, :] += dot_rows(cols[op["aux"], op["t"], rows, :], wb[op["slot"]].reshape(C, WIDE))

        each(2, half_rows, multiply)

    def do_attention(op):
        block, t = op["aux"], op["t"]
        same = same_pixel(BLOCK)

        def write(place):
            for start in range(0, rows_all, BLOCK):
                here = slice(start, start + BLOCK)
                for head in range(width // HEAD):
                    low = head * HEAD
                    query = qkb[block, t, here, low : low + HEAD]
                    key = qkb[block, t, here, width + low : width + low + HEAD]
                    value = vb[block, t, here, low : low + HEAD]
                    probs = head_probs(query, key, same, scale).astype(jnp.bfloat16)
                    total[here, low : low + HEAD] = dot_plain(probs, value)

        write(0)
        for which in range(2):

            @pl.when(block == which)
            def _(which=which):
                own = slice(width, 2 * width) if which == 0 else slice(0, width)
                other = slice(0, width) if which == 0 else slice(width, 2 * width)

                def use(rows):
                    cols[which, t, rows, own] = total[rows, 0:width].astype(jnp.bfloat16)
                    cols[which, t, rows, other] = jnp.zeros((rows_all // 4, width), jnp.bfloat16)

                each(4, rows_all // 4, use)
                for copy in kept_copies(which, t):
                    copy.start()

    chunk = 4 * FRAMES

    def do_norm(op):
        layer = op["aux"]

        def use(rows):
            @pl.when(layer == 0)
            def _():
                for t in range(4):
                    stream[rows, t * width : (t + 1) * width] = first_rows[t, rows, :]

            values = stream[rows, :] + joined_ref[pl.ds(8 + layer, 1), :]
            stream[rows, :] = values
            centre = jnp.mean(values, axis=1, keepdims=True)
            offset = values - centre
            inverse = lax.rsqrt(jnp.mean(offset * offset, axis=1, keepdims=True) + 1e-05)
            normed = offset * inverse * joined_ref[pl.ds(1 + layer, 1), :]
            normed = normed + joined_ref[pl.ds(5 + layer, 1), :]
            added = jnp.where(layer < 2, position_ref[...], 0.0)
            normed = normed.reshape(chunk // FRAMES, FRAMES, C) + added[None]
            xb[rows, :] = normed.reshape(chunk, C).astype(jnp.bfloat16)

        each(rows_all // chunk, chunk, use)
        save_now(stream, stream_out_ref.at[layer])

    def do_turn(op):
        def one(step, carry):
            lanes = pl.ds(pl.multiple_of(step * 128, 128), 128)
            ptb[lanes, :] = xb[:, lanes].T
            return carry

        lax.fori_loop(0, C // 128, one, 0)
        save_now(ptb, pt_ref.at[op["aux"]])

    def do_last(op):
        def use(rows):
            xb[rows, :] = (stream[rows, :] + joined_ref[11:12, :]).astype(jnp.bfloat16)

        each(rows_all // chunk, chunk, use)

    def do_join(op):
        for index in range(3):
            for copy in peer_copies(index):
                copy.wait_recv()
        for copy in own_peer:
            copy.wait()
        for t in range(4):
            lanes = slice(t * width, (t + 1) * width)
            joined_ref[:, lanes] = params_got[t, 0:16, :]

            def use(rows, t=t, lanes=lanes):
                xb[rows, lanes] = x_got[t, rows, :]

            each(4, rows_all // 4, use)
            for half in range(2):
                for part in range(2):
                    row = 16 + 2 * half + part
                    hidden_bias[t, half : half + 1, part * width : (part + 1) * width] = params_got[
                        t, row : row + 1, :
                    ]

    works = (None, do_spread, do_collapse, do_attention, do_norm, do_turn, do_last, do_join)
    four = range(4)

    def spreads(unit, aux):
        return [(1, unit, t, aux) for t in four]

    def collapses(unit, aux):
        return [(2, unit, t, aux) for t in four]

    def attentions(aux):
        return [(3, None, t, aux) for t in four]

    count = len(stages)
    places = 2 * count
    plan = Plan(places)
    for ready, steps in {
        -4: [(7, None, 0, 0), (5, None, 0, 7)],
        1: spreads(1, 0) + [(4, None, 0, 0)] + spreads(0, 1) + spreads(1, 2),
        2: [(5, None, 0, 4)] + attentions(0),
        3: collapses(3, 0) + [(4, None, 0, 1)] + spreads(2, 3) + spreads(3, 4),
        4: [(5, None, 0, 3)] + attentions(1) + collapses(4, 1) + [(4, None, 0, 2)],
        5: [(5, None, 0, 1)] + spreads(5, 5),
        6: spreads(6, 6),
        7: collapses(7, 2),
        8: collapses(8, 3) + [(6, None, 0, 0)] + spreads(4, 7) + [(5, None, 0, 5)],
    }.items():
        plan.fill(ready + count - 1, steps)

    def do_step(place):
        op = plan.read(place)
        has_tile = (op["kind"] == 1) | (op["kind"] == 2)

        @pl.when(has_tile)
        def _():
            pl.when(op["fresh"] == 1)(lambda: tile_load(op["unit"], op["t"], op["slot"]).start())

            @pl.when(op["next"] > 0)
            def _():
                following = op["next"] - 1
                tile_load(following // 4, following % 4, 1 - op["slot"]).start()

            tile_load(op["unit"], op["t"], op["slot"]).wait()

        for kind in range(1, len(works)):

            @pl.when(op["kind"] == kind)
            def _(kind=kind):
                works[kind](op)

    def advance(now, carry):
        turn, place = now // count, now % count
        for number in range(count):
            unit = turn - number

            @pl.when((place == count - 1 - number) & (unit >= 0) & (unit < UNITS))
            def _(number=number, unit=unit):
                stages[number](unit)

        def two(step, carry):
            do_step(2 * now + step)
            return carry

        lax.fori_loop(0, 2, two, 0)
        return carry

    lax.fori_loop(0, (UNITS + count - 1) * count, advance, 0)
    for which in range(4):
        for t in range(4):
            for copy in kept_copies(which, t):
                copy.wait()
    for index in range(3):
        for copy in peer_copies(index):
            copy.wait_send()


def forward_all(shards, rows_in, params, position):
    units, share, wide = shards.shape
    rows, width = rows_in.shape[1], rows_in.shape[2]
    low = jnp.bfloat16
    anywhere, near = pl.BlockSpec(memory_space=pl.ANY), pl.BlockSpec(memory_space=pltpu.VMEM)
    return pl.pallas_call(
        forward_kernel,
        in_specs=[anywhere, anywhere, near, near],
        out_specs=[anywhere] * 7 + [near] * 2,
        out_shape=[
            jax.ShapeDtypeStruct((units, 2, 2, 4, 2, share, wide), low),
            jax.ShapeDtypeStruct((12, 4, rows, wide), low),
            jax.ShapeDtypeStruct((8, C, rows), low),
            jax.ShapeDtypeStruct((3, rows, C), jnp.float32),
            jax.ShapeDtypeStruct((2, 4, rows, wide), low),
            jax.ShapeDtypeStruct((2, 4, rows, width), low),
            jax.ShapeDtypeStruct((2, 4, rows, wide), low),
            jax.ShapeDtypeStruct((4, rows, width), low),
            jax.ShapeDtypeStruct((16, C), jnp.float32),
        ],
        scratch_shapes=[
            pltpu.VMEM((rows, C), jnp.float32),
            pltpu.VMEM((rows, C), low),
            pltpu.VMEM((C, rows), low),
            pltpu.VMEM((4, rows, width), low),
            pltpu.VMEM((4,) + params.shape, jnp.float32),
            pltpu.VMEM((4, 8, wide), jnp.float32),
            pltpu.VMEM((2, 4, rows, wide), low),
            pltpu.VMEM((2, 4, rows, width), low),
            pltpu.VMEM((4, 4, rows, wide), low),
            pltpu.VMEM((2, 4, rows, wide), low),
            pltpu.VMEM((4, rows, width), jnp.float32),
            pltpu.VMEM((rows, wide), jnp.float32),
            pltpu.VMEM((2, 4, 2, share, wide), low),
            pltpu.SemaphoreType.DMA((2,)),
            pltpu.SemaphoreType.DMA((1,)),
            pltpu.SemaphoreType.DMA((4, 4, 3)),
            pltpu.SemaphoreType.DMA((2, 4)),
            pltpu.SemaphoreType.DMA((2, 3)),
            pltpu.SemaphoreType.DMA((units,)),
            pltpu.SemaphoreType.DMA((units, 2, 5)),
            pltpu.SemaphoreType.DMA((units, 2, 2, 4, 2)),
            pltpu.SemaphoreType.DMA((units, 3)),
        ],
        compiler_params=pltpu.CompilerParams(
            collective_id=0, has_side_effects=True, vmem_limit_bytes=60 << 20
        ),
    )(shards, rows_in, params, position)


def backward_kernel(
    whole_ref,
    q_given,
    pt_given,
    streams_ref,
    qk_ref,
    v_ref,
    slope_ref,
    moved_ref,
    joined_ref,
    out_ref,
    q_ref,
    pt_ref,
    ptx_ref,
    qx_ref,
    got_ref,
    vec_ref,
    hidden_ref,
    p_buf,
    q_buf,
    dw,
    rya,
    rxa,
    rua,
    rda,
    rxb,
    rub,
    rdb,
    ryb,
    gs,
    gn,
    xb,
    ptb,
    wb,
    cb,
    av,
    datt,
    total,
    sb,
    ob,
    dn,
    load_sem,
    give_sem,
    take_sem,
    send_sem,
    recv_sem,
    tile_sem,
    aux_sem,
    route_sem,
    misc_sem,
    out_sem,
    peer_send,
    peer_recv,
):
    at = Place()
    z, x, y, c = at.z, at.x, at.y, at.c
    far_x, far_y = at.far_x, at.far_y
    share = out_ref.shape[1]
    row_a, row_b = pl.ds(0, ROWS_A), pl.ds(ROWS_A, share - ROWS_A)
    rows_all, width = got_ref.shape[1], got_ref.shape[2]
    half_rows = rows_all // 2
    count_p = pt_ref.shape[0]
    scale = 1.0 / math.sqrt(HEAD)
    own_t = y * 2 + c
    at.greet()

    def give_p(index, source=None):
        return pltpu.make_async_remote_copy(
            src_ref=pt_ref.at[index] if source is None else source,
            dst_ref=ptx_ref.at[index],
            send_sem=give_sem.at[index],
            recv_sem=take_sem.at[index],
            device_id=at.to["core"],
            device_id_type=MESH_ID,
        )

    def give_q(index, yy, source):
        return pltpu.make_async_remote_copy(
            src_ref=source,
            dst_ref=qx_ref.at[index, yy],
            send_sem=give_sem.at[count_p + 2 * index + yy],
            recv_sem=take_sem.at[count_p + 2 * index + yy],
            device_id=at.to["core"],
            device_id_type=MESH_ID,
        )

    def known_q(index, yy):
        source = moved_ref if index == 9 else q_ref.at[index]
        return give_q(index, yy, source.at[2 * yy + 1 - c])

    known = (0, 1, 4, 9, 10)
    known_p = (1, 5, 3, 4, 7)
    for index in known[:2]:
        for yy in range(2):
            known_q(index, yy).start()
    give_p(1).start()
    for index in known[2:]:
        for yy in range(2):
            known_q(index, yy).start()
    for index in known_p[1:]:
        give_p(index).start()
    moved_own = [
        pltpu.make_async_copy(
            moved_ref.at[2 * yy + c], q_ref.at[9, 2 * yy + c], misc_sem.at[yy]
        )
        for yy in range(2)
    ]
    for copy in moved_own:
        copy.start()

    def each(count, size, use):
        def one(step, carry):
            use(pl.ds(pl.multiple_of(step * size, size), size))
            return carry

        lax.fori_loop(0, count, one, 0)

    def aux_load(source, target, number):
        return pltpu.make_async_copy(source, target, aux_sem.at[number])

    def tile_load(unit, t, slot):
        return pltpu.make_async_copy(whole_ref.at[unit, t // 2, t % 2], wb.at[slot], tile_sem.at[slot])

    def route(source, index, t):
        yy = t // 2
        local = pltpu.make_async_copy(source, q_ref.at[index, t], route_sem.at[index, yy])

        def begin():
            pl.when(c == t % 2)(lambda: local.start())
            pl.when(c != t % 2)(lambda: give_q(index, yy, source).start())

        def wait():
            pl.when(c == t % 2)(lambda: local.wait())
            pl.when(c != t % 2)(lambda: give_q(index, yy, source).wait_send())

        return begin, wait

    chunk = 4 * FRAMES
    quarter = rows_all // 4

    def column_sum(row, values):
        vec_ref[pl.ds(row, 1), :] += jnp.sum(values, axis=0, keepdims=True)

    def do_spread(op):
        t, aux = op["t"], op["aux"]
        side = t % 2

        def slope_load():
            return aux_load(slope_ref.at[aux, t], cb.at[4], 0)

        def head_loads():
            return (
                aux_load(qk_ref.at[aux - 2, t], cb.at[4], 0),
                aux_load(v_ref.at[aux - 2, t], av, 1),
            )

        pl.when(aux < 2)(lambda: slope_load().start())

        @pl.when(aux >= 2)
        def _():
            for load in head_loads():
                load.start()

        def multiply(rows):
            total[rows, :] = dot_plain(xb[rows, :], wb[op["slot"]].reshape(C, WIDE))

        each(2, half_rows, multiply)

        @pl.when(aux < 2)
        def _():
            slope_load().wait()

            def use(rows):
                grad = total[rows, :] * cb[4, rows, :].astype(jnp.float32)
                hidden_ref[t, pl.ds(aux, 1), :] += jnp.sum(grad, axis=0, keepdims=True)
                cb[side, rows, :] = grad.astype(jnp.bfloat16)

            each(4, quarter, use)
            route(cb.at[side], 3 - aux, t)[0]()

        @pl.when(aux >= 2)
        def _():
            for load in head_loads():
                load.wait()

            for block in range(2):

                @pl.when(aux == 2 + block)
                def _(block=block):
                    low = width if block == 0 else 0

                    def use(rows):
                        datt[rows, :] = total[rows, low : low + width].astype(jnp.bfloat16)

                    each(4, quarter, use)

    def do_collapse(op):
        which, routed, t = op["aux"] % 5, op["aux"] // 5, op["t"]

        @pl.when(which == 4)
        def _():
            load = aux_load(moved_ref.at[t], cb.at[4], 0)
            load.start()
            load.wait()

        def multiply(rows):
            gn[rows, :] += dot_rows(cb[which, rows, :], wb[op["slot"]].reshape(C, WIDE))

        each(2, half_rows, multiply)
        pl.when(routed > 0)(lambda: route(cb.at[which], routed - 1, t)[1]())

    def do_attention(op):
        block, t = op["aux"], op["t"]
        side = t % 2
        same = same_pixel(BLOCK)
        for start in range(0, rows_all, BLOCK):
            here = slice(start, start + BLOCK)
            for head in range(width // HEAD):
                low = head * HEAD
                query = cb[4, here, low : low + HEAD]
                key = cb[4, here, width + low : width + low + HEAD]
                value = av[here, low : low + HEAD]
                grad = datt[here, low : low + HEAD]
                probs = head_probs(query, key, same, scale)
                grad_probs = dot_rows(grad, value)
                centred = jnp.sum(probs * grad_probs, axis=1, keepdims=True)
                grad_raw = (probs * (grad_probs - centred) * scale).astype(jnp.bfloat16)
                cb[side, here, low : low + HEAD] = dot_plain(grad_raw, key).astype(jnp.bfloat16)
                cb[side, here, width + low : width + low + HEAD] = dot_first(
                    grad_raw, query
                ).astype(jnp.bfloat16)
                cb[2 + side, here, low : low + HEAD] = dot_first(
                    probs.astype(jnp.bfloat16), grad
                ).astype(jnp.bfloat16)
        route(cb.at[side], 7 - 2 * block, t)[0]()
        route(cb.at[2 + side], 8 - 2 * block, t)[0]()

    def do_layer(op):
        layer = op["aux"]

        def load(step):
            rows = pl.ds(pl.multiple_of(step * chunk, chunk), chunk)
            return pltpu.make_async_copy(
                streams_ref.at[layer, rows], sb.at[step % 2], misc_sem.at[3 + step % 2]
            )

        def one(step, carry):
            pl.when(step + 1 < rows_all // chunk)(lambda: load(step + 1).start())
            load(step).wait()
            rows = pl.ds(pl.multiple_of(step * chunk, chunk), chunk)
            values = sb[step % 2]
            centre = jnp.mean(values, axis=1, keepdims=True)
            offset = values - centre
            inverse = lax.rsqrt(jnp.mean(offset * offset, axis=1, keepdims=True) + 1e-05)
            hat = offset * inverse
            grad = gn[rows, :]
            column_sum(layer, grad * hat)
            column_sum(3 + layer, grad)
            scaled = grad * joined_ref[pl.ds(1 + layer, 1), :]
            first = jnp.mean(scaled, axis=1, keepdims=True)
            second = jnp.mean(scaled * hat, axis=1, keepdims=True)
            result = gs[rows, :] + inverse * (scaled - first - hat * second)
            gs[rows, :] = result
            column_sum(6 + layer, result)
            xb[rows, :] = result.astype(jnp.bfloat16)
            gn[rows, :] = jnp.zeros((chunk, C), jnp.float32)
            return carry

        load(0).start()
        lax.fori_loop(0, rows_all // chunk, one, 0)

    def do_turn(op):
        index = op["aux"]

        def one(step, carry):
            lanes = pl.ds(pl.multiple_of(step * 128, 128), 128)
            ptb[lanes, :] = xb[:, lanes].T
            return carry

        lax.fori_loop(0, C // 128, one, 0)
        local = pltpu.make_async_copy(ptb, pt_ref.at[index], misc_sem.at[2])
        local.start()
        give_p(index, ptb).start()
        local.wait()
        give_p(index, ptb).wait_send()

    def do_first(op):
        def use(rows):
            values = gn[rows, :]
            gs[rows, :] = values
            column_sum(9, values)
            xb[rows, :] = values.astype(jnp.bfloat16)
            gn[rows, :] = jnp.zeros((chunk, C), jnp.float32)

        each(rows_all // chunk, chunk, use)

    def do_place(op):
        t = op["t"]
        side = t % 2
        for block in range(4):

            @pl.when(t == block)
            def _(block=block):
                def use(rows):
                    cb[side, rows, 0:width] = jnp.zeros((quarter, width), jnp.bfloat16)
                    cb[side, rows, width:] = xb[rows, block * width : (block + 1) * width]

                each(4, quarter, use)

        route(cb.at[side], 11, t)[0]()

    peers = (("y", far_y * 2 + c), ("core", y * 2 + 1 - c), ("cross", far_y * 2 + 1 - c))

    def peer_copy(index):
        kind, t = peers[index]
        return pltpu.make_async_remote_copy(
            src_ref=dn.at[t],
            dst_ref=got_ref.at[own_t],
            send_sem=peer_send.at[index],
            recv_sem=peer_recv.at[index],
            device_id=at.to[kind],
            device_id_type=MESH_ID,
        )

    own_peer = pltpu.make_async_copy(dn.at[own_t], got_ref.at[own_t], peer_send.at[3])

    def do_send(op):
        for t in range(4):

            def use(rows, t=t):
                dn[t, rows, :] = gn[rows, t * width : (t + 1) * width].astype(jnp.bfloat16)

            each(4, quarter, use)
        for index in range(3):
            peer_copy(index).start()
        own_peer.start()

    def do_moved(op):
        for copy in moved_own:
            copy.wait()

    works = (
        None,
        do_spread,
        do_collapse,
        do_attention,
        do_layer,
        do_turn,
        do_first,
        do_place,
        do_send,
        do_moved,
    )
    four = range(4)

    def feed(half):
        steps = []
        for t in four:
            steps += [(1, 7 + half, t, half), (2, 5 + half, t, t % 2 + 5 * (4 - half))]
        return steps

    def heads(block, t):
        return [
            (1, 3 + block, t, 2 + block),
            (3, None, t, block),
            (2, 2 * block, t, t % 2 + 5 * (8 - 2 * block)),
            (2, 2 * block + 1, t, 2 + t % 2 + 5 * (9 - 2 * block)),
        ]

    def inputs(t):
        return [(7, None, t, 0), (2, 1, t, t % 2 + 5 * 12)]

    stage_count = 6
    plan = Plan(2 * stage_count)
    for turn, steps in {
        -1: [(2, 4, t, 4) for t in four] + [(6, None, 0, 0), (5, None, 0, 0)],
        0: feed(1),
        1: feed(0),
        2: [(4, None, 0, 2), (5, None, 0, 2)] + heads(1, 0) + [(9, None, 0, 0)],
        3: heads(1, 1) + heads(1, 2),
        4: heads(1, 3),
        5: [(4, None, 0, 1), (5, None, 0, 6)] + heads(0, 0),
        6: heads(0, 1) + heads(0, 2) + heads(0, 3),
        7: [(4, None, 0, 0)] + inputs(0) + inputs(1) + inputs(2) + inputs(3),
        8: [(8, None, 0, 0)],
    }.items():
        plan.fill(turn + 1, steps)

    def do_step(place):
        op = plan.read(place)
        has_tile = (op["kind"] == 1) | (op["kind"] == 2)

        @pl.when(has_tile)
        def _():
            pl.when(op["fresh"] == 1)(lambda: tile_load(op["unit"], op["t"], op["slot"]).start())

            @pl.when(op["next"] > 0)
            def _():
                following = op["next"] - 1
                tile_load(following // 4, following % 4, 1 - op["slot"]).start()

            tile_load(op["unit"], op["t"], op["slot"]).wait()

        for kind in range(1, len(works)):

            @pl.when(op["kind"] == kind)
            def _(kind=kind):
                works[kind](op)

    vec_ref[...] = jnp.zeros_like(vec_ref)
    hidden_ref[...] = jnp.zeros_like(hidden_ref)

    def clear(rows):
        gn[rows, :] = jnp.zeros((chunk, C), jnp.float32)
        cb[2, rows, :] = jnp.zeros((chunk, WIDE), jnp.bfloat16)
        cb[3, rows, :] = jnp.zeros((chunk, WIDE), jnp.bfloat16)

    each(rows_all // chunk, chunk, clear)

    names = ["ya0", "ya1", "xa", "ua0", "ua1", "ua2", "da0", "da1", "da2"]
    names += ["xb0", "xb1", "ub0", "ub1", "ub2", "db0", "db1", "db2", "yb"]
    number = {name: index for index, name in enumerate(names)}

    class Slot:
        def __init__(self, turn):
            self.d, self.r = turn % SLOTS_IN_FLIGHT, turn % SLOTS_RECEIVED

    def copy(slot, name, src, dst, kind, shift=0):
        index = number[name] + shift
        return pltpu.make_async_remote_copy(
            src_ref=src,
            dst_ref=dst,
            send_sem=send_sem.at[slot.d, index],
            recv_sem=recv_sem.at[slot.r, index],
            device_id=at.to[kind],
            device_id_type=MESH_ID,
        )

    def ya(slot, part):
        side = far_x if part == 0 else x
        return copy(
            slot, f"ya{part}", dw.at[slot.d, far_y, :, side, row_a], rya.at[slot.r, part], "y"
        )

    def xa(slot):
        return copy(slot, "xa", dw.at[slot.d, y, :, far_x, row_a], rxa.at[slot.r], "x")

    def xb_copy(slot, part):
        return copy(
            slot, f"xb{part}", dw.at[slot.d, part, :, far_x, row_b], rxb.at[slot.r, part], "x"
        )

    def yb(slot):
        return copy(slot, "yb", dw.at[slot.d, far_y, z, x, row_b], ryb.at[slot.r], "y")

    def up(slot, colour, d):
        if colour == 0:
            return copy(
                slot, "ua0", dw.at[slot.d, y, d, x, row_a], rua.at[slot.r, d - 1], "up", d - 1
            )
        return copy(slot, "ub0", dw.at[slot.d, :, d, x, row_b], rub.at[slot.r, d - 1], "up", d - 1)

    def down(slot, colour, d):
        if colour == 0:
            return copy(slot, "da0", dw.at[slot.d, y, d, x, row_a], rda.at[slot.r, d], "down", d)
        return copy(slot, "db0", dw.at[slot.d, :, d, x, row_b], rdb.at[slot.r, d], "down", d)

    def add(place, got):
        total = place[...].astype(jnp.float32) + got[...].astype(jnp.float32)
        place[...] = total.astype(jnp.bfloat16)

    def products(slot, p_index, q_index, more):
        loads = [
            pltpu.make_async_copy(pt_ref.at[p_index], p_buf.at[0], load_sem.at[0]),
            pltpu.make_async_copy(ptx_ref.at[p_index], p_buf.at[1], load_sem.at[1]),
        ]
        for yy in range(2):
            loads += [
                pltpu.make_async_copy(
                    q_ref.at[q_index, 2 * yy + c], q_buf.at[0, yy], load_sem.at[2 + yy]
                ),
                pltpu.make_async_copy(
                    qx_ref.at[q_index, yy], q_buf.at[1, yy], load_sem.at[4 + yy]
                ),
            ]
        for load in loads:
            load.start()
        for load in loads:
            load.wait()

        def one(step, carry):
            side, zz = step // 4, step % 4
            yy = jnp.where(side == 0, far_y, y)
            rows = pl.ds(pl.multiple_of(zz * 2 * share, 2 * share), 2 * share)
            result = dot_plain(p_buf[0, rows, :], q_buf[0, yy]) + dot_plain(
                p_buf[1, rows, :], q_buf[1, yy]
            )
            result = result.reshape(2, share, WIDE)
            earlier = dw[slot.d, yy, zz].astype(jnp.float32)
            result = result + jnp.where(more == 1, earlier, 0.0)
            dw[slot.d, yy, zz] = result.astype(jnp.bfloat16)
            return carry

        lax.fori_loop(0, 8, one, 0)

    def take_p(index):
        await_bytes(ptx_ref.at[index], take_sem.at[index])

    def take_q(index):
        for yy in range(2):
            await_bytes(qx_ref.at[index, yy], take_sem.at[count_p + 2 * index + yy])

    def stage0(turn):
        slot = Slot(turn)
        p_index = (turn + turn // 5) // 2

        @pl.when((turn + turn // 5) % 2 == 0)
        def _():
            take_p(p_index)

        take_q(turn)
        mixed = (turn >= 4).astype(jnp.int32) * (1 - turn % 2)
        extra = (turn - 4) // 2

        @pl.when(mixed == 1)
        def _():
            take_p(5 + extra)
            take_q(UNITS + extra)

        def one_pass(more, carry):
            products(
                slot,
                jnp.where(more == 1, 5 + extra, p_index),
                jnp.where(more == 1, UNITS + extra, turn),
                more,
            )
            return carry

        lax.fori_loop(0, 1 + mixed, one_pass, 0)

        ya(slot, 0).start()
        xb_copy(slot, 0).start()
        ya(slot, 1).start()
        xb_copy(slot, 1).start()

    def z_step(slot, colour, step):
        @pl.when(z <= step - 1)
        def _():
            d = z + 4 - step

            @pl.when(z >= 1)
            def _():
                up(slot, colour, d).wait_recv()
                if colour == 0:
                    add(dw.at[slot.d, y, d, x, row_a], rua.at[slot.r, d - 1])
                else:
                    add(dw.at[slot.d, 0, d, x, row_b], rub.at[slot.r, d - 1, 0])
                    add(dw.at[slot.d, 1, d, x, row_b], rub.at[slot.r, d - 1, 1])

            up(slot, colour, d).start()

        @pl.when(3 - z <= step - 1)
        def _():
            d = z - 4 + step

            @pl.when(z <= 2)
            def _():
                down(slot, colour, d).wait_recv()
                if colour == 0:
                    add(dw.at[slot.d, y, d, x, row_a], rda.at[slot.r, d])
                else:
                    add(dw.at[slot.d, 0, d, x, row_b], rdb.at[slot.r, d, 0])
                    add(dw.at[slot.d, 1, d, x, row_b], rdb.at[slot.r, d, 1])

            down(slot, colour, d).start()

    def stage1(turn):
        slot = Slot(turn)
        for part in range(2):
            xb_copy(slot, part).wait_recv()
            for zz in range(4):
                add(dw.at[slot.d, part, zz, x, row_b], rxb.at[slot.r, part, zz])
        z_step(slot, 1, 1)
        ya(slot, 0).wait_recv()
        for zz in range(4):
            add(dw.at[slot.d, y, zz, far_x, row_a], rya.at[slot.r, 0, zz])
        xa(slot).start()
        ya(slot, 1).wait_recv()
        for zz in range(4):
            add(dw.at[slot.d, y, zz, x, row_a], rya.at[slot.r, 1, zz])

    def stage2(turn):
        slot = Slot(turn)
        z_step(slot, 1, 2)
        xa(slot).wait_recv()
        for zz in range(4):
            add(dw.at[slot.d, y, zz, x, row_a], rxa.at[slot.r, zz])
        z_step(slot, 0, 1)

    def stage3(turn):
        slot = Slot(turn)
        z_step(slot, 1, 3)
        z_step(slot, 0, 2)

    def stage4(turn):
        slot = Slot(turn)
        z_step(slot, 0, 3)

        @pl.when(z >= 1)
        def _():
            up(slot, 1, z).wait_recv()
            for yy in range(2):
                add(dw.at[slot.d, yy, z, x, row_b], rub.at[slot.r, z - 1, yy])

        @pl.when(z <= 2)
        def _():
            down(slot, 1, z).wait_recv()
            for yy in range(2):
                add(dw.at[slot.d, yy, z, x, row_b], rdb.at[slot.r, z, yy])

        yb(slot).start()

    def out_copy(turn):
        return pltpu.make_async_copy(ob.at[turn % 2], out_ref.at[turn], out_sem.at[turn % 2])

    def stage5(turn):
        slot = Slot(turn)
        side = turn % 2
        pl.when(turn >= 2)(lambda: out_copy(turn - 2).wait())
        ob[side, row_a, :] = dw[slot.d, y, z, x, row_a, :].astype(jnp.float32)

        @pl.when(z >= 1)
        def _():
            up(slot, 0, z).wait_recv()
            ob[side, row_a, :] += rua[slot.r, z - 1].astype(jnp.float32)

        @pl.when(z <= 2)
        def _():
            down(slot, 0, z).wait_recv()
            ob[side, row_a, :] += rda[slot.r, z].astype(jnp.float32)

        yb(slot).wait_recv()
        ob[side, row_b, :] = dw[slot.d, y, z, x, row_b, :].astype(jnp.float32) + ryb[
            slot.r
        ].astype(jnp.float32)
        out_copy(turn).start()

        ya(slot, 0).wait_send()
        ya(slot, 1).wait_send()
        xa(slot).wait_send()
        xb_copy(slot, 0).wait_send()
        xb_copy(slot, 1).wait_send()
        yb(slot).wait_send()
        for colour in range(2):
            for step in range(1, 4):

                @pl.when(z <= step - 1)
                def _(colour=colour, step=step):
                    up(slot, colour, z + 4 - step).wait_send()

                @pl.when(3 - z <= step - 1)
                def _(colour=colour, step=step):
                    down(slot, colour, z - 4 + step).wait_send()

    stages = (stage0, stage1, stage2, stage3, stage4, stage5)

    def advance(now, carry):
        for step in range(stage_count):
            turn = now // stage_count - 1 - step

            @pl.when((now % stage_count == step) & (turn >= 0) & (turn < UNITS))
            def _(step=step, turn=turn):
                stages[step](turn)

        def two(step, carry):
            do_step(2 * now + step)
            return carry

        lax.fori_loop(0, 2, two, 0)
        return carry

    lax.fori_loop(0, (UNITS + stage_count) * stage_count, advance, 0)
    out_copy(UNITS - 2).wait()
    out_copy(UNITS - 1).wait()
    for index in range(3):
        peer_copy(index).wait()
    own_peer.wait()
    for index in known:
        for yy in range(2):
            known_q(index, yy).wait_send()
    for index in known_p:
        give_p(index).wait_send()


def backward_all(whole, q_all, pt_all, streams, qk, values, slopes, moved_part, joined):
    share = whole.shape[5]
    count_p, unused, rows = pt_all.shape
    width = values.shape[3]
    low = jnp.bfloat16
    slots, taken, rest = SLOTS_IN_FLIGHT, SLOTS_RECEIVED, share - ROWS_A
    anywhere, near = pl.BlockSpec(memory_space=pl.ANY), pl.BlockSpec(memory_space=pltpu.VMEM)
    return pl.pallas_call(
        backward_kernel,
        in_specs=[anywhere] * 8 + [near],
        out_specs=[anywhere] * 6 + [near] * 2,
        out_shape=[
            jax.ShapeDtypeStruct((UNITS, share, WIDE), jnp.float32),
            jax.ShapeDtypeStruct(q_all.shape, low),
            jax.ShapeDtypeStruct(pt_all.shape, low),
            jax.ShapeDtypeStruct(pt_all.shape, low),
            jax.ShapeDtypeStruct((q_all.shape[0], 2, rows, WIDE), low),
            jax.ShapeDtypeStruct((4, rows, width), low),
            jax.ShapeDtypeStruct((16, C), jnp.float32),
            jax.ShapeDtypeStruct((4, 8, WIDE), jnp.float32),
        ],
        input_output_aliases={1: 1, 2: 2},
        scratch_shapes=[
            pltpu.VMEM((2, C, rows), low),
            pltpu.VMEM((2, 2, rows, WIDE), low),
            pltpu.VMEM((slots, 2, 4, 2, share, WIDE), low),
            pltpu.VMEM((taken, 2, 4, ROWS_A, WIDE), low),
            pltpu.VMEM((taken, 4, ROWS_A, WIDE), low),
            pltpu.VMEM((taken, 3, ROWS_A, WIDE), low),
            pltpu.VMEM((taken, 3, ROWS_A, WIDE), low),
            pltpu.VMEM((taken, 2, 4, rest, WIDE), low),
            pltpu.VMEM((taken, 3, 2, rest, WIDE), low),
            pltpu.VMEM((taken, 3, 2, rest, WIDE), low),
            pltpu.VMEM((taken, rest, WIDE), low),
            pltpu.VMEM((rows, C), jnp.float32),
            pltpu.VMEM((rows, C), jnp.float32),
            pltpu.VMEM((rows, C), low),
            pltpu.VMEM((C, rows), low),
            pltpu.VMEM((2, 4, 2, share, WIDE), low),
            pltpu.VMEM((5, rows, WIDE), low),
            pltpu.VMEM((rows, width), low),
            pltpu.VMEM((rows, width), low),
            pltpu.VMEM((rows, WIDE), jnp.float32),
            pltpu.VMEM((2, 4 * FRAMES, C), jnp.float32),
            pltpu.VMEM((2, share, WIDE), jnp.float32),
            pltpu.VMEM((4, rows, width), low),
            pltpu.SemaphoreType.DMA((6,)),
            pltpu.SemaphoreType.DMA((32,)),
            pltpu.SemaphoreType.DMA((32,)),
            pltpu.SemaphoreType.DMA((slots, 18)),
            pltpu.SemaphoreType.DMA((taken, 18)),
            pltpu.SemaphoreType.DMA((2,)),
            pltpu.SemaphoreType.DMA((4,)),
            pltpu.SemaphoreType.DMA((12, 2)),
            pltpu.SemaphoreType.DMA((5,)),
            pltpu.SemaphoreType.DMA((2,)),
            pltpu.SemaphoreType.DMA((4,)),
            pltpu.SemaphoreType.DMA((3,)),
        ],
        compiler_params=pltpu.CompilerParams(
            collective_id=1, has_side_effects=True, vmem_limit_bytes=63 << 20
        ),
    )(whole, q_all, pt_all, streams, qk, values, slopes, moved_part, joined)


def gather_plain(shards):
    units, share, wide = shards.shape
    whole = lax.all_gather(shards, MIXED, axis=1, tiled=True)
    return whole.reshape(units, lax.axis_size("tensor"), C, wide)


def reduce_plain(turned, parts):
    reduced = []
    for turn in range(UNITS):
        pairs = [(turned[(turn + turn // 5) // 2], parts[turn])]
        if turn in (4, 6, 8):
            extra = (turn - 4) // 2
            pairs.append((turned[5 + extra], parts[UNITS + extra]))
        whole = sum(
            jnp.einsum("kr,trn->tkn", left, right, preferred_element_type=jnp.float32)
            for left, right in pairs
        )
        whole = whole.astype(jnp.bfloat16).reshape(-1, whole.shape[2])
        reduced.append(
            lax.psum_scatter(whole, MIXED, scatter_dimension=0, tiled=True).astype(jnp.float32)
        )
    return jnp.stack(reduced, 0)


def by_pixels(values, tensor_size):
    slots, frames, width, pixels = values.shape
    own = pixels // tensor_size
    return jnp.transpose(values, (3, 0, 1, 2)).reshape(tensor_size, own * slots * frames, width)


def exchange(parts):
    return lax.all_to_all(parts, "tensor", 0, 0, tiled=True)


def back_to_channels(arrived, slots, pixels):
    width = arrived.shape[2]
    return jnp.transpose(arrived.reshape(pixels, slots, FRAMES, width), (1, 2, 3, 0))


def body(
    by_kernel,
    latent,
    clip_flags,
    cotangent,
    norm_gain,
    norm_shift,
    channel_bias,
    hidden_bias,
    weight_in,
    weight_qkv,
    weight_out,
    weight_up,
    weight_down,
    weight_proj,
):
    tensor_size = lax.axis_size("tensor")
    slots, frames, width, pixels = latent.shape
    share = weight_in.shape[0]
    hidden_width = hidden_bias.shape[0]
    flags = (clip_flags > 0)[:, None, None, None]

    wide = 2 * width

    shards = []
    side = jnp.concatenate
    for block in range(2):
        shards.append(weight_qkv[block, :, :2].reshape(share, wide))
        other = weight_in if block == 0 else weight_out[0].T
        shards.append(side([weight_qkv[block, :, 2], other], 1))
    shards.append(side([weight_out[1].T, weight_proj], 1))
    shards += [weight_up[:, :wide], weight_up[:, wide:]]
    down_turned = weight_down.T
    shards += [down_turned[:, :wide], down_turned[:, wide:]]
    shards = jnp.stack(shards, 0)
    params = jnp.zeros((24, width), jnp.float32)
    params = params.at[:13].set(side([norm_gain, norm_shift, channel_bias], 0))
    params = params.at[16:20].set(hidden_bias.reshape(4, width))

    start = latent.astype(jnp.float32)
    cot = cotangent.astype(jnp.float32)
    group_width = C // GROUPS
    grouped = start.reshape(slots, frames, width // group_width, group_width, pixels)
    group_centre = jnp.mean(grouped, axis=(1, 3, 4), keepdims=True)
    offset = grouped - group_centre
    group_inverse = lax.rsqrt(jnp.mean(offset * offset, axis=(1, 3, 4), keepdims=True) + 1e-06)
    group_hat = (offset * group_inverse).reshape(start.shape)
    normed = group_hat * norm_gain[0][:, None] + norm_shift[0][:, None]
    sent = by_pixels(normed.astype(jnp.bfloat16), tensor_size)
    rows = sent.shape[1]

    grad_moved_local = jnp.where(flags, cot, 0.0)
    bias_moved = jnp.sum(grad_moved_local, axis=(0, 1, 3))
    grad_moved = exchange(by_pixels(grad_moved_local.astype(jnp.bfloat16), tensor_size))

    empty = jnp.zeros((tensor_size, rows, width), jnp.bfloat16)
    moved_part = side([empty, grad_moved], 2)
    if by_kernel:
        whole, q_all, pt_all, streams, qk_all, v_all, slopes, moved, joined = forward_all(
            shards, sent, params, make_positions()
        )
        gains = joined[:4]
        reduced, q_all, pt_all, unused, unused, arrived_grad, sums, hidden_sums = backward_all(
            whole, q_all, pt_all, streams, qk_all, v_all, slopes, moved_part, joined
        )
        vectors = sums[:10]
        hidden_grad = hidden_sums[:, :2].reshape(tensor_size, 2 * wide)
    else:
        arrived = exchange(sent)
        inputs_in = jnp.transpose(arrived, (1, 0, 2)).reshape(rows, C)
        packed = lax.all_gather(params, "tensor", axis=0, tiled=False)
        joined = jnp.transpose(packed[:, :13], (1, 0, 2)).reshape(13, C)
        gains, shifts, biases = joined[:4], joined[4:8], joined[8:]
        hidden_full = packed[:, 16:20].reshape(tensor_size, 2 * wide)
        whole = gather_plain(shards)
        full_qk = (whole[0], whole[2])
        full_v = (whole[1, :, :, :width], whole[3, :, :, :width])
        full_in = whole[1, :, :, width:]
        full_out = (whole[3, :, :, width:], whole[4, :, :, :width])
        full_proj = whole[4, :, :, width:]
        full_up = (whole[5], whole[6])
        full_down = (whole[7], whole[8])

        def join(parts):
            return jnp.transpose(parts, (1, 0, 2)).reshape(rows, parts.shape[0] * parts.shape[2])

        stream = join(spread(inputs_in, full_in)) + biases[0]
        position = jnp.tile(make_positions(), (rows // FRAMES, 1))
        kept = []
        for block in range(2):
            hat, inverse = layer_stats(stream)
            lifted = (hat * gains[1 + block] + shifts[1 + block] + position).astype(jnp.bfloat16)
            qk = spread(lifted, full_qk[block]).astype(jnp.bfloat16)
            values = spread(lifted, full_v[block]).astype(jnp.bfloat16)
            attended = attend(qk, values)
            stream = stream + collapse(attended, full_out[block]) + biases[1 + block]
            kept.append((hat, inverse, lifted.T, qk, values, attended))
        hat_feed, inverse_feed = layer_stats(stream)
        inputs_up = (hat_feed * gains[3] + shifts[3]).astype(jnp.bfloat16)
        pre_act = [
            spread(inputs_up, full_up[half])
            + hidden_full[:, None, half * wide : half * wide + wide]
            for half in range(2)
        ]
        slopes = [
            jax.vjp(partial(jax.nn.gelu, approximate=False), pre)[1](jnp.ones_like(pre))[0]
            for pre in pre_act
        ]
        hidden = [jax.nn.gelu(pre, approximate=False).astype(jnp.bfloat16) for pre in pre_act]
        stream = stream + collapse(hidden[0], full_down[0]) + collapse(hidden[1], full_down[1])
        stream = stream + biases[3]
        inputs_proj = stream.astype(jnp.bfloat16)
        moved = spread(inputs_proj, full_proj) + biases[4].reshape(tensor_size, 1, width)
        moved = moved.astype(jnp.bfloat16)

        bias_grads = [None] * 4
        gain_grads = [None] * 3
        shift_grads = [None] * 3
        turned, parts = [None] * 8, [None] * 12
        turned[1], turned[5], turned[7] = inputs_up.T, inputs_proj.T, inputs_in.T
        parts[0], parts[1] = hidden[1], hidden[0]
        parts[9] = moved_part
        grad_stream = collapse(grad_moved, full_proj)
        bias_grads[3] = jnp.sum(grad_stream, 0)
        grad_low = grad_stream.astype(jnp.bfloat16)
        turned[0] = grad_low.T
        hidden_grads = [None, None]
        grad_normed = 0.0
        for half in (1, 0):
            grad_hidden = spread(grad_low, full_down[half])
            grad_pre = grad_hidden * slopes[half]
            hidden_grads[half] = jnp.sum(grad_pre, 1)
            parts[3 - half] = grad_pre.astype(jnp.bfloat16)
            grad_normed = grad_normed + collapse(parts[3 - half], full_up[half])
        hidden_grad = side(hidden_grads, 1)
        grad_layer, gain_grads[2], shift_grads[2] = layer_back(
            grad_normed, hat_feed, inverse_feed, gains[3]
        )
        grad_stream = grad_stream + grad_layer
        for block in (1, 0):
            hat, inverse, lifted_turned, qk, values, attended = kept[block]
            bias_grads[1 + block] = jnp.sum(grad_stream, 0)
            grad_low = grad_stream.astype(jnp.bfloat16)
            turned[2 if block == 1 else 6] = grad_low.T
            pair = [attended, empty] if block == 1 else [empty, attended]
            parts[4 if block == 1 else 10] = side(pair, 2)
            grad_attended = spread(grad_low, full_out[block]).astype(jnp.bfloat16)
            grad_qk, grad_values = attend_back(qk, values, grad_attended)
            turned[3 if block == 1 else 4] = lifted_turned
            parts[6 if block == 1 else 8] = side([grad_values, empty], 2)
            parts[5 if block == 1 else 7] = grad_qk
            grad_lifted = collapse(grad_qk, full_qk[block]) + collapse(grad_values, full_v[block])
            grad_layer, gain_grads[block], shift_grads[block] = layer_back(
                grad_lifted, hat, inverse, gains[1 + block]
            )
            grad_stream = grad_stream + grad_layer
        bias_grads[0] = jnp.sum(grad_stream, 0)
        grad_low = grad_stream.astype(jnp.bfloat16)
        grad_low_parts = jnp.transpose(grad_low.reshape(rows, tensor_size, width), (1, 0, 2))
        parts[11] = side([empty, grad_low_parts], 2)
        turned, parts = jnp.stack(turned, 0), jnp.stack(parts, 0)
        reduced = reduce_plain(turned, parts)
        grad_normed = collapse(grad_low_parts, full_in).astype(jnp.bfloat16)
        grad_normed = jnp.transpose(grad_normed.reshape(rows, tensor_size, width), (1, 0, 2))
        arrived_grad = exchange(grad_normed)
        vectors = jnp.stack(gain_grads + shift_grads + bias_grads, 0)

    moved_local = back_to_channels(exchange(moved), slots, pixels).astype(jnp.float32)
    output = jnp.where(flags, start + moved_local, start).astype(jnp.bfloat16)

    qkv_grads = [
        side([reduced[7 - 2 * block], reduced[8 - 2 * block, :, :width]], 1).reshape(share, 3, width)
        for block in range(2)
    ]
    out_grads = [reduced[6, :, width:].T, reduced[4, :, :width].T]
    in_grad, proj_grad = reduced[8, :, width:], reduced[4, :, width:]
    up_grad = side([reduced[3], reduced[2]], 1)
    down_grad = side([reduced[1], reduced[0]], 1)
    grad_normed = back_to_channels(arrived_grad, slots, pixels).astype(jnp.float32)
    scaled = grad_normed * norm_gain[0][:, None]
    scaled_groups = scaled.reshape(grouped.shape)
    hat_groups = group_hat.reshape(grouped.shape)
    first = jnp.mean(scaled_groups, axis=(1, 3, 4), keepdims=True)
    second = jnp.mean(scaled_groups * hat_groups, axis=(1, 3, 4), keepdims=True)
    grad_group = group_inverse * (scaled_groups - first - hat_groups * second)
    latent_grad = cot + grad_group.reshape(start.shape)
    group_gain_grad = jnp.sum(grad_normed * group_hat, axis=(0, 1, 3))
    group_shift_grad = jnp.sum(grad_normed, axis=(0, 1, 3))

    vectors = jnp.transpose(vectors.reshape(10, tensor_size, width), (1, 0, 2))
    vectors = jnp.concatenate([vectors.reshape(tensor_size, 10 * width), hidden_grad], 1)
    vectors = lax.psum_scatter(vectors, "tensor", scatter_dimension=0, tiled=False)
    sums = lax.psum(
        jnp.concatenate([vectors, group_gain_grad, group_shift_grad, bias_moved]), "dp"
    )
    channel_sums = sums[: 10 * width].reshape(10, width)
    hidden_bias_grad = sums[10 * width : 10 * width + hidden_width]
    local_sums = sums[10 * width + hidden_width :].reshape(3, width)
    gain_grad = jnp.concatenate([local_sums[0:1], channel_sums[0:3]], 0)
    shift_grad = jnp.concatenate([local_sums[1:2], channel_sums[3:6]], 0)
    channel_bias_grad = jnp.concatenate([channel_sums[6:10], local_sums[2:3]], 0)
    return (
        output,
        latent_grad,
        gain_grad,
        shift_grad,
        channel_bias_grad,
        hidden_bias_grad,
        in_grad,
        jnp.stack(qkv_grads, 0),
        jnp.stack(out_grads, 0),
        up_grad,
        down_grad.T,
        proj_grad,
    )


def solution(mesh):
    placed = (
        P("dp", None, "tensor", None),
        P("dp"),
        P("dp", None, "tensor", None),
        P(None, "tensor"),
        P(None, "tensor"),
        P(None, "tensor"),
        P("tensor"),
        P("dp", "tensor"),
        P(None, "dp", None, "tensor"),
        P(None, "tensor", "dp"),
        P("dp", "tensor"),
        P("tensor", "dp"),
        P("dp", "tensor"),
    )
    return jax.shard_map(
        partial(body, tuple(mesh.shape[name] for name in ("dp", "tensor")) == (8, 4)),
        mesh=mesh,
        in_specs=placed,
        out_specs=(
            P("dp", None, "tensor", None),
            P("dp", None, "tensor", None),
            P(None, "tensor"),
            P(None, "tensor"),
            P(None, "tensor"),
            P("tensor"),
            P("dp", "tensor"),
            P(None, "dp", None, "tensor"),
            P(None, "tensor", "dp"),
            P("dp", "tensor"),
            P("tensor", "dp"),
            P("dp", "tensor"),
        ),
        check_vma=False,
    )
```

time: 959 us -> 826 us (0.86)
  local copies, waits for them, and re-layouts: 157 us -> 62.8 us
  matrix products: 84.7 us -> 0 us
  Pallas kernels: 604 us -> 670 us
    dot_general x12 -> x0, matrix products: 84.7 us -> none  [the longest x8 54 us: collapse(): jnp.einsum('trn,tkn->rk', parts, weight, preferred_element_type=jnp.float32)]
    pallas_call x3 -> x1, Pallas kernels: 309 us -> 376 us  [backward_all(): pl.pallas_call(backward_kernel, in_specs=[anywhere] * 8 + [near], out_spe...]
    unnamed x149 -> x69, local copies, waits for them, and re-layouts: 59.9 us -> 21.4 us
    slice x4 -> x0, local copies, waits for them, and re-layouts: 35.9 us -> none  [the longest x1 26.6 us: body(): full_qk = (whole[0], whole[2])]
  transfers between devices with their start and end apart: 4 -> 3, of which waited for: 1 -> 0; matrix products, arithmetic and copies ran while one was open for 25% -> 10% of each run, Pallas kernels for 63% -> 81%
where the time goes in v5:
time: 826 us; the launch traced here: 824 us
  Pallas kernels  670 us (81%)
  local copies, waits for them, and re-layouts  62.8 us (8%)
  blocking collectives  35 us (4%)
  other arithmetic  32.7 us (4%)
  between operations  15 us (2%)
  starting transfers between devices  8.57 us (1%)
    pallas_call x1, Pallas kernels, backward_all(): pl.pallas_call(backward_kernel, in_specs=[anywhere] * 8 + [near], out_spe...  376 us
    pallas_call x1, Pallas kernels, forward_all(): pl.pallas_call(forward_kernel, in_specs=[anywhere, anywhere, near, near],...  294 us
    psum x1, blocking collectives, body(): lax.psum(jnp.concatenate([vectors, group_gain_grad, group_shift_grad, bia...  35 us
    unnamed x69, local copies, waits for them, and re-layouts  21.4 us
  transfers between devices with their start and end apart: 3, of which 0 were waited for; matrix products, arithmetic and copies ran while one was open for 10% of the time, Pallas kernels for 81%

profile of v5, /device:TPU:0, one launch (start us, length us, event | category | flops | bytes accessed | tf_op | source)
XLA Modules:
  0.0 824.2 jit_solution(8727218470010721126)
XLA Ops:
  7.2 2.1 copy.68
  11.8 4.2 all-to-all-start.1
  16.1 1.8 fusion.31
  20.0 2.1 copy.63
  28.9 1.7 fusion.18
  32.1 1.7 fusion.20
  38.8 1.6 fusion.16.shard_ref
  40.5 1.8 fusion.9
  43.3 294.2 %shard_map.220 = (bf16[9,2,2,4,2,160,640]{6,5,4,3,2,1,0:T(8,128)(2,1)}, bf16[12,4,512,640]{3,2,1,0:T(8,128)(2,1)}, bf16[8,1280,512]{2,1,0:T(8,128)(2,1)}, f32[3,...) custom-call(bf16[9,160,640]{2,1,0:T(8,128)(2,1)} %fusion.16.shard_re, ...), custom_call_target="tpu_custom_call" | custom-call | tf_op jit(solution)/shard_map/pallas_call | solution.py:715
  337.5 2.5 copy.66
  340.7 4.3 all-to-all-start
  345.9 2.3 concatenate.50.moved_ref
  348.2 375.9 %shard_map.221 = (f32[9,160,640]{2,1,0:T(8,128)}, bf16[12,4,512,640]{3,2,1,0:T(8,128)(2,1)}, bf16[8,1280,512]{2,1,0:T(8,128)(2,1)}, bf16[8,1280,512]{2,1,0:T(8,1...) custom-call(bf16[9,2,2,4,2,160,640]{6,5,4,3,2,1,0:T(8,128)(2,1)} %ge, ...), custom_call_target="tpu_custom_call", output_to_operand_aliasing={{1}: (1, {}), {2}: (2, {})} | custom-call | tf_op jit(solution)/shard_map/pallas_call | solution.py:1461
  724.1 2.7 slice_bitcast_fusion.1
  726.7 2.7 slice_bitcast_fusion.6
  733.2 1.7 reshape.266
  740.6 1.7 copy-done.2
  742.3 1.7 fusion.13
  754.5 3.3 pad_maximum_fusion
  760.6 3.1 copy.67
  763.7 6.8 fusion
  772.9 2.2 copy.73
  775.1 2.8 copy.72
  779.6 35.0 %psum.7 = f32[5440]{0:T(1024)S(1)} all-reduce(f32[5440]{0:T(1024)S(1)} %concatenate.52), channel_id=1, replica_groups=mesh['dp'=8,'tensor'=4] {'dp'}, use_global_device_ids=true, to_apply=%region_12.13 | all-reduce | flops 5440 | bytes 43520 | tf_op jit(solution)/shard_map/psum | solution.py:1750
  (135 shorter events, 49.3 us)
Async XLA Ops:
  11.8 328.8 %all-to-all-start.1 = ((bf16[4,512,320]{1,2,0:T(8,128)(2,1)}), bf16[4,512,320]{1,2,0:T(8,128)(2,1)S(1)}, u32[]{:S(2)}, u32[]{:S(2)}) async-start(bf16[4,512,320]{1,2,0:T(8,128)(2,1)} %copy.69), calls=%async_computation.1 | async-start | bytes 2621440 | tf_op jit(solution)/shard_map/all_to_all | solution.py:1550
  22.2 18.3 %copy-start = (bf16[1,16,320,128]{2,1,3,0:T(8,128)(2,1)}, bf16[1,16,320,128]{2,1,3,0:T(8,128)(2,1)S(1)}, u32[]{:S(2)}) copy-start(bf16[1,16,320,128]{2,1,3,0:T(8,128)(2,1)S(1)} %copy.63) | copy-start | bytes 3932164
  22.9 17.6 %copy-start.14 = (f32[320]{0:T(512)}, f32[320]{0:T(512)S(1)}, u32[]{:S(2)}) copy-start(f32[320]{0:T(512)S(1)} %sub.51) | copy-start | bytes 3844
  22.9 14.2 %copy-start.21 = (f32[4,320]{1,0:T(4,128)S(1)}, f32[4,320]{1,0:T(4,128)}, u32[]{:S(2)}) copy-start(f32[4,320]{1,0:T(4,128)} %param.21) | copy-start | bytes 15364
  22.9 14.2 %copy-start.22 = (f32[4,320]{1,0:T(4,128)S(1)}, f32[4,320]{1,0:T(4,128)}, u32[]{:S(2)}) copy-start(f32[4,320]{1,0:T(4,128)} %param.20) | copy-start | bytes 15364
  22.9 14.2 %copy-start.20 = (f32[5,320]{1,0:T(8,128)S(1)}, f32[5,320]{1,0:T(8,128)}, u32[]{:S(2)}) copy-start(f32[5,320]{1,0:T(8,128)} %param.22) | copy-start | bytes 19204
  22.9 14.2 %copy-start.25 = (f32[1280]{0:T(1024)S(1)}, f32[1280]{0:T(1024)}, u32[]{:S(2)}) copy-start(f32[1280]{0:T(1024)} %param.23) | copy-start | bytes 15364
  23.8 16.7 %copy-start.16 = (f32[320]{0:T(512)}, f32[320]{0:T(512)S(1)}, u32[]{:S(2)}) copy-start(f32[320]{0:T(512)S(1)} %mul.103) | copy-start | bytes 3844
  30.6 11.6 %copy-start.26 = (f32[16]{0:T(128)S(1)}, f32[16]{0:T(128)}, u32[]{:S(2)}) copy-start(f32[16]{0:T(128)} %iota_convert_fusion) | copy-start | bytes 196
  37.1 300.4 %copy-start.18 = (f32[320]{0:T(512)}, f32[320]{0:T(512)S(1)}, u32[]{:S(2)}) copy-start(f32[320]{0:T(512)S(1)} %get-tuple-element.142) | copy-start | bytes 3844
  38.8 4.4 copy-start.13
  43.3 296.8 %copy-start.27 = (u32[32]{0:T(128)S(1)}, u32[32]{0:T(128)}, u32[]{:S(2)}) copy-start(u32[32]{0:T(128)} %constant.109) | copy-start | bytes 388
  340.7 419.9 %all-to-all-start = ((bf16[4,512,320]{1,2,0:T(8,128)(2,1)}), bf16[4,512,320]{1,2,0:T(8,128)(2,1)}, u32[]{:S(2)}, u32[]{:S(2)}) async-start(bf16[4,512,320]{1,2,0:T(8,128)(2,1)} %copy.66), calls=%async_computation | async-start | bytes 2621440 | tf_op jit(solution)/shard_map/all_to_all | solution.py:1550
  344.9 433.0 %all-reduce.5.cloned.1.call-start = ((), (), s32[]{:S(2)}) async-start(), calls=%async_computation.2 | async-start | bytes 143360
  729.4 11.0 %copy-start.7 = (bf16[4,512,320]{2,1,0:T(8,128)(2,1)S(1)}, bf16[4,512,320]{2,1,0:T(8,128)(2,1)}, u32[]{:S(2)}) copy-start(bf16[4,512,320]{2,1,0:T(8,128)(2,1)} %get-tuple-element.58) | copy-start | bytes 3932164
  733.2 9.1 %copy-start.1 = (bf16[1,16,320,128]{2,1,3,0:T(8,128)(2,1)S(1)}, bf16[1,16,320,128]{2,1,3,0:T(8,128)(2,1)}, u32[]{:S(2)}) copy-start(bf16[1,16,320,128]{2,1,3,0:T(8,128)(2,1)} %copy-done) | copy-start | bytes 3932164
  754.5 4.2 copy-start.9
  754.5 4.2 copy-start.10
  754.5 5.2 copy-start.8
  763.7 6.8 copy-start.11
  763.7 6.8 copy-start.12
  763.7 7.6 copy-start.6
  772.9 6.6 copy-start.23
  772.9 6.6 copy-start.24
  (7 other events, 16.4 us)
Sparse Core Ops, SparseCore 0:
  740.5 29.0 all-reduce.4

commit v6 on v5

--- a/solution.py
+++ b/solution.py
@@ -177,14 +177,27 @@
 
 
 class Plan:
-    FIELDS = (("kind", 16), ("unit", 9), ("t", 4), ("aux", 80), ("slot", 2), ("fresh", 2), ("next", 37))
-
-    def __init__(self, per_turn):
-        self.per_turn = per_turn
+    FIELDS = (
+        ("kind", 16),
+        ("unit", 16),
+        ("t", 4),
+        ("aux", 128),
+        ("slot", 2),
+        ("fresh", 2),
+        ("next", 64),
+        ("early", 32),
+    )
+
+    def __init__(self, per_turn, loads_early=False):
+        self.per_turn, self.loads_early = per_turn, loads_early
         self.steps = {}
 
     def fill(self, turn, steps):
         tiles = [index for index, step in enumerate(steps) if step[1] is not None]
+        early = {}
+        for order, index in enumerate(tiles):
+            if self.loads_early and steps[index][0] == 1:
+                early[tiles[order - 1] if order else index] = 1 + steps[index][3] * 4 + steps[index][2]
         for index, (kind, unit, t, aux) in enumerate(steps):
             slot = fresh = following = 0
             if unit is not None:
@@ -193,7 +206,7 @@
                 if order + 1 < len(tiles):
                     later = steps[tiles[order + 1]]
                     following = 1 + later[1] * 4 + later[2]
-            values = (kind, unit or 0, t, aux, slot, fresh, following)
+            values = (kind, unit or 0, t, aux, slot, fresh, following, early.get(index, 0))
             code, scale = 0, 1
             for (name, size), value in zip(self.FIELDS, values):
                 assert 0 <= value < size
@@ -203,10 +216,13 @@
             assert place not in self.steps
             self.steps[place] = code
 
-    def read(self, place):
+    def code(self, place):
         code = jnp.int32(0)
         for where, value in self.steps.items():
-            code = code + jnp.where(place == where, jnp.int32(value), jnp.int32(0))
+            code = jnp.where(place == where, jnp.int32(value), code)
+        return code
+
+    def fields(self, code):
         out = {}
         for name, size in self.FIELDS:
             out[name] = code % size
@@ -661,7 +677,11 @@
         plan.fill(ready + count - 1, steps)
 
     def do_step(place):
-        op = plan.read(place)
+        code = plan.code(place)
+        pl.when(code > 0)(lambda: do_filled(code))
+
+    def do_filled(code):
+        op = plan.fields(code)
         has_tile = (op["kind"] == 1) | (op["kind"] == 2)
 
         @pl.when(has_tile)
@@ -681,23 +701,24 @@
             def _(kind=kind):
                 works[kind](op)
 
-    def advance(now, carry):
-        turn, place = now // count, now % count
-        for number in range(count):
-            unit = turn - number
-
-            @pl.when((place == count - 1 - number) & (unit >= 0) & (unit < UNITS))
-            def _(number=number, unit=unit):
-                stages[number](unit)
-
-        def two(step, carry):
-            do_step(2 * now + step)
-            return carry
-
-        lax.fori_loop(0, 2, two, 0)
-        return carry
-
-    lax.fori_loop(0, (UNITS + count - 1) * count, advance, 0)
+    def advance(turn, carry):
+        def inner(place, carry):
+            for number in range(count):
+                unit = turn - number
+
+                @pl.when((place == count - 1 - number) & (unit >= 0) & (unit < UNITS))
+                def _(number=number, unit=unit):
+                    stages[number](unit)
+
+            def two(step, carry):
+                do_step(2 * (turn * count + place) + step)
+                return carry
+
+            return lax.fori_loop(0, 2, two, carry)
+
+        return lax.fori_loop(0, count, inner, carry)
+
+    lax.fori_loop(0, UNITS + count - 1, advance, 0)
     for which in range(4):
         for t in range(4):
             for copy in kept_copies(which, t):
@@ -714,7 +735,7 @@
     anywhere, near = pl.BlockSpec(memory_space=pl.ANY), pl.BlockSpec(memory_space=pltpu.VMEM)
     return pl.pallas_call(
         forward_kernel,
-        in_specs=[anywhere, anywhere, near, near],
+        in_specs=[near, anywhere, near, near],
         out_specs=[anywhere] * 7 + [near] * 2,
         out_shape=[
             jax.ShapeDtypeStruct((units, 2, 2, 4, 2, share, wide), low),
@@ -858,15 +879,6 @@
             known_q(index, yy).start()
     for index in known_p[1:]:
         give_p(index).start()
-    moved_own = [
-        pltpu.make_async_copy(
-            moved_ref.at[2 * yy + c], q_ref.at[9, 2 * yy + c], misc_sem.at[yy]
-        )
-        for yy in range(2)
-    ]
-    for copy in moved_own:
-        copy.start()
-
     def each(count, size, use):
         def one(step, carry):
             use(pl.ds(pl.multiple_of(step * size, size), size))
@@ -900,26 +912,28 @@
     def column_sum(row, values):
         vec_ref[pl.ds(row, 1), :] += jnp.sum(values, axis=0, keepdims=True)
 
+    def slope_load(aux, t):
+        return aux_load(slope_ref.at[aux, t], cb.at[4], 0)
+
+    def head_loads(aux, t):
+        return (
+            aux_load(qk_ref.at[aux - 2, t], cb.at[4], 0),
+            aux_load(v_ref.at[aux - 2, t], av, 1),
+        )
+
+    def load_early(code):
+        aux, t = code // 4, code % 4
+        pl.when(aux < 2)(lambda: slope_load(aux, t).start())
+
+        @pl.when(aux >= 2)
+        def _():
+            for load in head_loads(aux, t):
+                load.start()
+
     def do_spread(op):
         t, aux = op["t"], op["aux"]
         side = t % 2
 
-        def slope_load():
-            return aux_load(slope_ref.at[aux, t], cb.at[4], 0)
-
-        def head_loads():
-            return (
-                aux_load(qk_ref.at[aux - 2, t], cb.at[4], 0),
-                aux_load(v_ref.at[aux - 2, t], av, 1),
-            )
-
-        pl.when(aux < 2)(lambda: slope_load().start())
-
-        @pl.when(aux >= 2)
-        def _():
-            for load in head_loads():
-                load.start()
-
         def multiply(rows):
             total[rows, :] = dot_plain(xb[rows, :], wb[op["slot"]].reshape(C, WIDE))
 
@@ -927,7 +941,7 @@
 
         @pl.when(aux < 2)
         def _():
-            slope_load().wait()
+            slope_load(aux, t).wait()
 
             def use(rows):
                 grad = total[rows, :] * cb[4, rows, :].astype(jnp.float32)
@@ -939,7 +953,7 @@
 
         @pl.when(aux >= 2)
         def _():
-            for load in head_loads():
+            for load in head_loads(aux, t):
                 load.wait()
 
             for block in range(2):
@@ -952,6 +966,9 @@
                         datt[rows, :] = total[rows, low : low + width].astype(jnp.bfloat16)
 
                     each(4, quarter, use)
+
+    def moved_own(t):
+        return pltpu.make_async_copy(cb.at[4], q_ref.at[9, t], misc_sem.at[0])
 
     def do_collapse(op):
         which, routed, t = op["aux"] % 5, op["aux"] // 5, op["t"]
@@ -961,12 +978,14 @@
             load = aux_load(moved_ref.at[t], cb.at[4], 0)
             load.start()
             load.wait()
+            pl.when(c == t % 2)(lambda: moved_own(t).start())
 
         def multiply(rows):
             gn[rows, :] += dot_rows(cb[which, rows, :], wb[op["slot"]].reshape(C, WIDE))
 
         each(2, half_rows, multiply)
         pl.when(routed > 0)(lambda: route(cb.at[which], routed - 1, t)[1]())
+        pl.when((which == 4) & (c == t % 2))(lambda: moved_own(t).wait())
 
     def do_attention(op):
         block, t = op["aux"], op["t"]
@@ -1037,11 +1056,15 @@
             return carry
 
         lax.fori_loop(0, C // 128, one, 0)
-        local = pltpu.make_async_copy(ptb, pt_ref.at[index], misc_sem.at[2])
-        local.start()
+        turn_copy(index).start()
         give_p(index, ptb).start()
-        local.wait()
-        give_p(index, ptb).wait_send()
+
+    def turn_copy(index):
+        return pltpu.make_async_copy(ptb, pt_ref.at[index], misc_sem.at[2])
+
+    def do_turned(op):
+        turn_copy(op["aux"]).wait()
+        give_p(op["aux"], ptb).wait_send()
 
     def do_first(op):
         def use(rows):
@@ -1094,10 +1117,6 @@
             peer_copy(index).start()
         own_peer.start()
 
-    def do_moved(op):
-        for copy in moved_own:
-            copy.wait()
-
     works = (
         None,
         do_spread,
@@ -1108,7 +1127,7 @@
         do_first,
         do_place,
         do_send,
-        do_moved,
+        do_turned,
     )
     four = range(4)
 
@@ -1130,15 +1149,15 @@
         return [(7, None, t, 0), (2, 1, t, t % 2 + 5 * 12)]
 
     stage_count = 6
-    plan = Plan(2 * stage_count)
+    plan = Plan(2 * stage_count, True)
     for turn, steps in {
-        -1: [(2, 4, t, 4) for t in four] + [(6, None, 0, 0), (5, None, 0, 0)],
+        -1: [(2, 4, t, 4) for t in four] + [(6, None, 0, 0), (5, None, 0, 0), (9, None, 0, 0)],
         0: feed(1),
         1: feed(0),
-        2: [(4, None, 0, 2), (5, None, 0, 2)] + heads(1, 0) + [(9, None, 0, 0)],
+        2: [(4, None, 0, 2), (5, None, 0, 2)] + heads(1, 0) + [(9, None, 0, 2)],
         3: heads(1, 1) + heads(1, 2),
         4: heads(1, 3),
-        5: [(4, None, 0, 1), (5, None, 0, 6)] + heads(0, 0),
+        5: [(4, None, 0, 1), (5, None, 0, 6)] + heads(0, 0) + [(9, None, 0, 6)],
         6: heads(0, 1) + heads(0, 2) + heads(0, 3),
         7: [(4, None, 0, 0)] + inputs(0) + inputs(1) + inputs(2) + inputs(3),
         8: [(8, None, 0, 0)],
@@ -1146,7 +1165,11 @@
         plan.fill(turn + 1, steps)
 
     def do_step(place):
-        op = plan.read(place)
+        code = plan.code(place)
+        pl.when(code > 0)(lambda: do_filled(code))
+
+    def do_filled(code):
+        op = plan.fields(code)
         has_tile = (op["kind"] == 1) | (op["kind"] == 2)
 
         @pl.when(has_tile)
@@ -1158,6 +1181,7 @@
                 following = op["next"] - 1
                 tile_load(following // 4, following % 4, 1 - op["slot"]).start()
 
+            pl.when(op["early"] > 0)(lambda: load_early(op["early"] - 1))
             tile_load(op["unit"], op["t"], op["slot"]).wait()
 
         for kind in range(1, len(works)):
@@ -1228,7 +1252,7 @@
         total = place[...].astype(jnp.float32) + got[...].astype(jnp.float32)
         place[...] = total.astype(jnp.bfloat16)
 
-    def products(slot, p_index, q_index, more):
+    def product_loads(p_index, q_index):
         loads = [
             pltpu.make_async_copy(pt_ref.at[p_index], p_buf.at[0], load_sem.at[0]),
             pltpu.make_async_copy(ptx_ref.at[p_index], p_buf.at[1], load_sem.at[1]),
@@ -1242,9 +1266,10 @@
                     qx_ref.at[q_index, yy], q_buf.at[1, yy], load_sem.at[4 + yy]
                 ),
             ]
-        for load in loads:
-            load.start()
-        for load in loads:
+        return loads
+
+    def products(slot, p_index, q_index, more):
+        for load in product_loads(p_index, q_index):
             load.wait()
 
         def one(step, carry):
@@ -1269,15 +1294,20 @@
         for yy in range(2):
             await_bytes(qx_ref.at[index, yy], take_sem.at[count_p + 2 * index + yy])
 
+    def prepare(turn):
+        p_index = (turn + turn // 5) // 2
+
+        @pl.when((turn + turn // 5) % 2 == 0)
+        def _():
+            take_p(p_index)
+
+        take_q(turn)
+        for load in product_loads(p_index, turn):
+            load.start()
+
     def stage0(turn):
         slot = Slot(turn)
         p_index = (turn + turn // 5) // 2
-
-        @pl.when((turn + turn // 5) % 2 == 0)
-        def _():
-            take_p(p_index)
-
-        take_q(turn)
         mixed = (turn >= 4).astype(jnp.int32) * (1 - turn % 2)
         extra = (turn - 4) // 2
 
@@ -1287,6 +1317,11 @@
             take_q(UNITS + extra)
 
         def one_pass(more, carry):
+            @pl.when(more == 1)
+            def _():
+                for load in product_loads(5 + extra, UNITS + extra):
+                    load.start()
+
             products(
                 slot,
                 jnp.where(more == 1, 5 + extra, p_index),
@@ -1424,21 +1459,25 @@
     stages = (stage0, stage1, stage2, stage3, stage4, stage5)
 
     def advance(now, carry):
-        for step in range(stage_count):
-            turn = now // stage_count - 1 - step
-
-            @pl.when((now % stage_count == step) & (turn >= 0) & (turn < UNITS))
-            def _(step=step, turn=turn):
-                stages[step](turn)
-
-        def two(step, carry):
-            do_step(2 * now + step)
-            return carry
-
-        lax.fori_loop(0, 2, two, 0)
+        def inner(place, carry):
+            for spot, step in enumerate(range(stage_count)):
+                turn = now - 1 - step
+
+                @pl.when((place == spot) & (turn >= 0) & (turn < UNITS))
+                def _(step=step, turn=turn):
+                    stages[step](turn)
+
+            def two(step, carry):
+                do_step(2 * (now * stage_count + place) + step)
+                return carry
+
+            return lax.fori_loop(0, 2, two, carry)
+
+        lax.fori_loop(0, stage_count, inner, 0)
+        pl.when(now < UNITS)(lambda: prepare(now))
         return carry
 
-    lax.fori_loop(0, (UNITS + stage_count) * stage_count, advance, 0)
+    lax.fori_loop(0, UNITS + stage_count, advance, 0)
     out_copy(UNITS - 2).wait()
     out_copy(UNITS - 1).wait()
     for index in range(3):
@@ -1555,8 +1594,361 @@
     return jnp.transpose(arrived.reshape(pixels, slots, FRAMES, width), (1, 2, 3, 0))
 
 
+def group_total(values):
+    width = values.shape[0]
+    size = C // GROUPS
+    grouped = values.reshape(width // size, size, 1)
+    summed = jnp.sum(grouped, axis=1, keepdims=True)
+    return jnp.broadcast_to(summed, grouped.shape).reshape(width, 1)
+
+
+def enter_kernel(
+    latent_ref,
+    cot_ref,
+    flag_ref,
+    gain_ref,
+    shift_ref,
+    in_ref,
+    qkv_ref,
+    out_ref,
+    up_ref,
+    down_ref,
+    proj_ref,
+    sent_ref,
+    moved_ref,
+    shards_ref,
+    centre_ref,
+    inverse_ref,
+    bias_ref,
+    rows_buf,
+):
+    frames, width, pixels = latent_ref.shape[1:]
+    cells = frames * pixels * (C // GROUPS)
+    shards_ref[0, :, 0:width] = qkv_ref[0, 0]
+    shards_ref[0, :, width:] = qkv_ref[0, 1]
+    shards_ref[1, :, 0:width] = qkv_ref[0, 2]
+    shards_ref[1, :, width:] = in_ref[...]
+    shards_ref[2, :, 0:width] = qkv_ref[1, 0]
+    shards_ref[2, :, width:] = qkv_ref[1, 1]
+    shards_ref[3, :, 0:width] = qkv_ref[1, 2]
+    shards_ref[3, :, width:] = out_ref[0]
+    shards_ref[4, :, 0:width] = out_ref[1]
+    shards_ref[4, :, width:] = proj_ref[...]
+    for half in range(2):
+        lanes = slice(half * WIDE, (half + 1) * WIDE)
+        shards_ref[5 + half] = up_ref[:, lanes]
+        shards_ref[7 + half] = down_ref[:, lanes]
+
+    def frame_sum(use):
+        def one(f, carry):
+            return carry + use(f)
+
+        total = lax.fori_loop(0, frames, one, jnp.zeros((width, pixels), jnp.float32))
+        return jnp.sum(total, axis=1, keepdims=True)
+
+    def values(f):
+        return latent_ref[0, f].astype(jnp.float32)
+
+    centre = group_total(frame_sum(values)) / cells
+    spread_sum = group_total(frame_sum(lambda f: (values(f) - centre) * (values(f) - centre)))
+    inverse = lax.rsqrt(spread_sum / cells + 1e-06)
+    centre_ref[...] = centre
+    inverse_ref[...] = inverse
+    flag = (flag_ref[0] > 0).astype(jnp.float32)
+
+    def masked(f):
+        return cot_ref[0, f].astype(jnp.float32) * flag
+
+    bias_ref[...] = frame_sum(masked)
+    own = pixels // 4 * frames
+
+    def rows_of(use, target):
+        def one(f, carry):
+            block = use(f)
+            for part in range(3):
+                rows_buf[part, pl.ds(f, pixels, stride=frames), :] = block[
+                    part * 128 : part * 128 + 128, :
+                ].T
+            return carry
+
+        lax.fori_loop(0, frames, one, 0)
+
+        def cast(step, carry):
+            rows = pl.ds(pl.multiple_of(step * 128, 128), 128)
+            t, inside = step // (own // 128), step % (own // 128)
+            inner = pl.ds(pl.multiple_of(inside * 128, 128), 128)
+            for part in range(3):
+                low, high = part * 128, min(part * 128 + 128, width)
+                target[t, inner, low:high] = rows_buf[part, rows, 0 : high - low].astype(
+                    jnp.bfloat16
+                )
+            return carry
+
+        lax.fori_loop(0, 4 * own // 128, cast, 0)
+
+    def padded(block):
+        return jnp.concatenate([block, jnp.zeros((384 - width, pixels), jnp.float32)], 0)
+
+    gain, shift = gain_ref[...], shift_ref[...]
+    rows_of(lambda f: padded((values(f) - centre) * inverse * gain + shift), sent_ref)
+    rows_of(lambda f: padded(masked(f)), moved_ref)
+
+
+def enter(latent, cotangent, flags, gain, shift, w_in, w_qkv, w_out, w_up, w_down, w_proj):
+    slots, frames, width, pixels = latent.shape
+    share, rows = w_in.shape[0], pixels // 4 * frames
+    near = pl.BlockSpec(memory_space=pltpu.VMEM)
+    column = jax.ShapeDtypeStruct((width, 1), jnp.float32)
+    low = jnp.bfloat16
+    return pl.pallas_call(
+        enter_kernel,
+        in_specs=[near, near, pl.BlockSpec(memory_space=pltpu.SMEM)] + [near] * 8,
+        out_specs=[near] * 6,
+        out_shape=[
+            jax.ShapeDtypeStruct((4, rows, width), low),
+            jax.ShapeDtypeStruct((4, rows, width), low),
+            jax.ShapeDtypeStruct((UNITS, share, WIDE), low),
+            column,
+            column,
+            column,
+        ],
+        scratch_shapes=[pltpu.VMEM((3, 4 * rows, 128), jnp.float32)],
+        compiler_params=pltpu.CompilerParams(vmem_limit_bytes=48 << 20),
+    )(
+        latent,
+        cotangent,
+        flags,
+        gain.reshape(width, 1),
+        shift.reshape(width, 1),
+        w_in,
+        jnp.transpose(w_qkv, (0, 2, 1, 3)),
+        jnp.transpose(w_out, (0, 2, 1)),
+        w_up,
+        w_down.T,
+        w_proj,
+    )
+
+
+def leave_kernel(
+    grad_ref,
+    moved_ref,
+    latent_ref,
+    cot_ref,
+    flag_ref,
+    gain_ref,
+    centre_ref,
+    inverse_ref,
+    reduced_ref,
+    output_ref,
+    latent_grad_ref,
+    gain_grad_ref,
+    shift_grad_ref,
+    in_ref,
+    qkv_ref,
+    out_ref,
+    up_ref,
+    down_ref,
+    proj_ref,
+    rows_buf,
+    turned,
+):
+    frames, width, pixels = latent_ref.shape[1:]
+    cells = frames * pixels * (C // GROUPS)
+    for block in range(2):
+        for part in range(2):
+            qkv_ref[block, part] = reduced_ref[7 - 2 * block, :, part * width : (part + 1) * width]
+        qkv_ref[block, 2] = reduced_ref[8 - 2 * block, :, 0:width]
+    in_ref[...] = reduced_ref[8, :, width:]
+    out_ref[0] = reduced_ref[6, :, width:]
+    out_ref[1] = reduced_ref[4, :, 0:width]
+    proj_ref[...] = reduced_ref[4, :, width:]
+    for half in range(2):
+        lanes = slice(half * WIDE, (half + 1) * WIDE)
+        up_ref[:, lanes] = reduced_ref[3 - half]
+        down_ref[:, lanes] = reduced_ref[1 - half]
+
+    own = pixels // 4 * frames
+
+    def spread_rows(source):
+        def cast(step, carry):
+            rows = pl.ds(pl.multiple_of(step * 128, 128), 128)
+            t, inside = step // (own // 128), step % (own // 128)
+            inner = pl.ds(pl.multiple_of(inside * 128, 128), 128)
+            for part in range(3):
+                low, high = part * 128, min(part * 128 + 128, width)
+                rows_buf[part, rows, 0 : high - low] = source[t, inner, low:high].astype(
+                    jnp.float32
+                )
+            return carry
+
+        lax.fori_loop(0, 4 * own // 128, cast, 0)
+
+    def frame(f):
+        rows = pl.ds(f, pixels, stride=frames)
+        turned_parts = [rows_buf[part, rows, :].T for part in range(3)]
+        return jnp.concatenate(turned_parts, 0)[0:width, :]
+
+    def hat(f):
+        return (latent_ref[0, f].astype(jnp.float32) - centre_ref[...]) * inverse_ref[...]
+
+    flag = (flag_ref[0] > 0).astype(jnp.float32)
+    rows_buf[...] = jnp.zeros_like(rows_buf)
+    spread_rows(moved_ref)
+
+    def finish(f, carry):
+        start = latent_ref[0, f].astype(jnp.float32)
+        output_ref[0, f] = (start + flag * frame(f)).astype(jnp.bfloat16)
+        return carry
+
+    lax.fori_loop(0, frames, finish, 0)
+    spread_rows(grad_ref)
+    zero = jnp.zeros((width, pixels), jnp.float32)
+
+    def gather(f, carry):
+        grad = frame(f)
+        turned[f] = grad
+        return carry[0] + grad * hat(f), carry[1] + grad
+
+    by_gain, by_shift = lax.fori_loop(0, frames, gather, (zero, zero))
+    gain_sum = jnp.sum(by_gain, axis=1, keepdims=True)
+    shift_sum = jnp.sum(by_shift, axis=1, keepdims=True)
+    gain_grad_ref[...] = gain_sum
+    shift_grad_ref[...] = shift_sum
+    gain = gain_ref[...]
+    first = group_total(gain * shift_sum) / cells
+    second = group_total(gain * gain_sum) / cells
+
+    def back(f, carry):
+        grad = inverse_ref[...] * (turned[f] * gain - first - hat(f) * second)
+        latent_grad_ref[0, f] = cot_ref[0, f].astype(jnp.float32) + grad
+        return carry
+
+    lax.fori_loop(0, frames, back, 0)
+
+
+def leave(grad, moved, latent, cotangent, flags, gain, centre, inverse, reduced):
+    slots, frames, width, pixels = latent.shape
+    rows, share = pixels // 4 * frames, reduced.shape[1]
+    near = pl.BlockSpec(memory_space=pltpu.VMEM)
+    real = jnp.float32
+    column = jax.ShapeDtypeStruct((width, 1), real)
+    made = pl.pallas_call(
+        leave_kernel,
+        in_specs=[near] * 4 + [pl.BlockSpec(memory_space=pltpu.SMEM)] + [near] * 4,
+        out_specs=[near] * 10,
+        out_shape=[
+            jax.ShapeDtypeStruct(latent.shape, jnp.bfloat16),
+            jax.ShapeDtypeStruct(latent.shape, real),
+            column,
+            column,
+            jax.ShapeDtypeStruct((share, width), real),
+            jax.ShapeDtypeStruct((2, 3, share, width), real),
+            jax.ShapeDtypeStruct((2, share, width), real),
+            jax.ShapeDtypeStruct((share, 2 * WIDE), real),
+            jax.ShapeDtypeStruct((share, 2 * WIDE), real),
+            jax.ShapeDtypeStruct((share, width), real),
+        ],
+        scratch_shapes=[
+            pltpu.VMEM((3, 4 * rows, 128), real),
+            pltpu.VMEM((frames, width, pixels), real),
+        ],
+        compiler_params=pltpu.CompilerParams(vmem_limit_bytes=56 << 20),
+    )(
+        grad,
+        moved,
+        latent,
+        cotangent,
+        flags,
+        gain.reshape(width, 1),
+        centre,
+        inverse,
+        reduced,
+    )
+    output, latent_grad, gain_grad, shift_grad, g_in, g_qkv, g_out, g_up, g_down, g_proj = made
+    weights = (
+        g_in,
+        jnp.transpose(g_qkv, (0, 2, 1, 3)),
+        jnp.transpose(g_out, (0, 2, 1)),
+        g_up,
+        g_down.T,
+        g_proj,
+    )
+    return output, latent_grad, gain_grad.reshape(width), shift_grad.reshape(width), weights
+
+
+def kernel_body(
+    latent,
+    clip_flags,
+    cotangent,
+    norm_gain,
+    norm_shift,
+    channel_bias,
+    hidden_bias,
+    weight_in,
+    weight_qkv,
+    weight_out,
+    weight_up,
+    weight_down,
+    weight_proj,
+):
+    width = latent.shape[2]
+    side = jnp.concatenate
+    params = side([norm_gain, norm_shift, channel_bias, jnp.zeros((3, width), jnp.float32)], 0)
+    params = side([params, hidden_bias.reshape(4, width), jnp.zeros((4, width), jnp.float32)], 0)
+    sent, moved_sent, shards, centre, inverse, bias_moved = enter(
+        latent,
+        cotangent,
+        clip_flags,
+        norm_gain[0],
+        norm_shift[0],
+        weight_in,
+        weight_qkv,
+        weight_out,
+        weight_up,
+        weight_down,
+        weight_proj,
+    )
+    grad_moved = exchange(moved_sent)
+    moved_part = jnp.pad(grad_moved, ((0, 0), (0, 0), (width, 0)))
+    whole, q_all, pt_all, streams, qk_all, v_all, slopes, moved, joined = forward_all(
+        shards, sent, params, make_positions()
+    )
+    moved_back = exchange(moved)
+    reduced, q_all, pt_all, unused, unused, grad_back, sums, hidden_sums = backward_all(
+        whole, q_all, pt_all, streams, qk_all, v_all, slopes, moved_part, joined
+    )
+    output, latent_grad, group_gain, group_shift, weights = leave(
+        grad_back,
+        moved_back,
+        latent,
+        cotangent,
+        clip_flags,
+        norm_gain[0],
+        centre,
+        inverse,
+        reduced,
+    )
+    vectors = jnp.transpose(sums[:10].reshape(10, 4, width), (1, 0, 2)).reshape(4, 10 * width)
+    vectors = side([vectors, hidden_sums[:, :2].reshape(4, 2 * WIDE)], 1)
+    vectors = jnp.sum(exchange(vectors), 0)
+    local = side([vectors, group_gain, group_shift, bias_moved.reshape(width)])
+    total = local
+    count = lax.axis_size("dp")
+    for bit in range(count.bit_length() - 1):
+        total = total + lax.ppermute(total, "dp", [(i, i ^ (1 << bit)) for i in range(count)])
+    channel, hidden_grad = total[: 10 * width].reshape(10, width), total[10 * width : 14 * width]
+    group = total[14 * width :].reshape(3, width)
+    return (
+        output,
+        latent_grad,
+        side([group[0:1], channel[0:3]], 0),
+        side([group[1:2], channel[3:6]], 0),
+        side([channel[6:10], group[2:3]], 0),
+        hidden_grad,
+    ) + weights
+
+
 def body(
-    by_kernel,
     latent,
     clip_flags,
     cotangent,
@@ -1612,115 +2004,104 @@
 
     empty = jnp.zeros((tensor_size, rows, width), jnp.bfloat16)
     moved_part = side([empty, grad_moved], 2)
-    if by_kernel:
-        whole, q_all, pt_all, streams, qk_all, v_all, slopes, moved, joined = forward_all(
-            shards, sent, params, make_positions()
-        )
-        gains = joined[:4]
-        reduced, q_all, pt_all, unused, unused, arrived_grad, sums, hidden_sums = backward_all(
-            whole, q_all, pt_all, streams, qk_all, v_all, slopes, moved_part, joined
-        )
-        vectors = sums[:10]
-        hidden_grad = hidden_sums[:, :2].reshape(tensor_size, 2 * wide)
-    else:
-        arrived = exchange(sent)
-        inputs_in = jnp.transpose(arrived, (1, 0, 2)).reshape(rows, C)
-        packed = lax.all_gather(params, "tensor", axis=0, tiled=False)
-        joined = jnp.transpose(packed[:, :13], (1, 0, 2)).reshape(13, C)
-        gains, shifts, biases = joined[:4], joined[4:8], joined[8:]
-        hidden_full = packed[:, 16:20].reshape(tensor_size, 2 * wide)
-        whole = gather_plain(shards)
-        full_qk = (whole[0], whole[2])
-        full_v = (whole[1, :, :, :width], whole[3, :, :, :width])
-        full_in = whole[1, :, :, width:]
-        full_out = (whole[3, :, :, width:], whole[4, :, :, :width])
-        full_proj = whole[4, :, :, width:]
-        full_up = (whole[5], whole[6])
-        full_down = (whole[7], whole[8])
-
-        def join(parts):
-            return jnp.transpose(parts, (1, 0, 2)).reshape(rows, parts.shape[0] * parts.shape[2])
-
-        stream = join(spread(inputs_in, full_in)) + biases[0]
-        position = jnp.tile(make_positions(), (rows // FRAMES, 1))
-        kept = []
-        for block in range(2):
-            hat, inverse = layer_stats(stream)
-            lifted = (hat * gains[1 + block] + shifts[1 + block] + position).astype(jnp.bfloat16)
-            qk = spread(lifted, full_qk[block]).astype(jnp.bfloat16)
-            values = spread(lifted, full_v[block]).astype(jnp.bfloat16)
-            attended = attend(qk, values)
-            stream = stream + collapse(attended, full_out[block]) + biases[1 + block]
-            kept.append((hat, inverse, lifted.T, qk, values, attended))
-        hat_feed, inverse_feed = layer_stats(stream)
-        inputs_up = (hat_feed * gains[3] + shifts[3]).astype(jnp.bfloat16)
-        pre_act = [
-            spread(inputs_up, full_up[half])
-            + hidden_full[:, None, half * wide : half * wide + wide]
-            for half in range(2)
-        ]
-        slopes = [
-            jax.vjp(partial(jax.nn.gelu, approximate=False), pre)[1](jnp.ones_like(pre))[0]
-            for pre in pre_act
-        ]
-        hidden = [jax.nn.gelu(pre, approximate=False).astype(jnp.bfloat16) for pre in pre_act]
-        stream = stream + collapse(hidden[0], full_down[0]) + collapse(hidden[1], full_down[1])
-        stream = stream + biases[3]
-        inputs_proj = stream.astype(jnp.bfloat16)
-        moved = spread(inputs_proj, full_proj) + biases[4].reshape(tensor_size, 1, width)
-        moved = moved.astype(jnp.bfloat16)
-
-        bias_grads = [None] * 4
-        gain_grads = [None] * 3
-        shift_grads = [None] * 3
-        turned, parts = [None] * 8, [None] * 12
-        turned[1], turned[5], turned[7] = inputs_up.T, inputs_proj.T, inputs_in.T
-        parts[0], parts[1] = hidden[1], hidden[0]
-        parts[9] = moved_part
-        grad_stream = collapse(grad_moved, full_proj)
-        bias_grads[3] = jnp.sum(grad_stream, 0)
+    arrived = exchange(sent)
+    inputs_in = jnp.transpose(arrived, (1, 0, 2)).reshape(rows, C)
+    packed = lax.all_gather(params, "tensor", axis=0, tiled=False)
+    joined = jnp.transpose(packed[:, :13], (1, 0, 2)).reshape(13, C)
+    gains, shifts, biases = joined[:4], joined[4:8], joined[8:]
+    hidden_full = packed[:, 16:20].reshape(tensor_size, 2 * wide)
+    whole = gather_plain(shards)
+    full_qk = (whole[0], whole[2])
+    full_v = (whole[1, :, :, :width], whole[3, :, :, :width])
+    full_in = whole[1, :, :, width:]
+    full_out = (whole[3, :, :, width:], whole[4, :, :, :width])
+    full_proj = whole[4, :, :, width:]
+    full_up = (whole[5], whole[6])
+    full_down = (whole[7], whole[8])
+
+    def join(parts):
+        return jnp.transpose(parts, (1, 0, 2)).reshape(rows, parts.shape[0] * parts.shape[2])
+
+    stream = join(spread(inputs_in, full_in)) + biases[0]
+    position = jnp.tile(make_positions(), (rows // FRAMES, 1))
+    kept = []
+    for block in range(2):
+        hat, inverse = layer_stats(stream)
+        lifted = (hat * gains[1 + block] + shifts[1 + block] + position).astype(jnp.bfloat16)
+        qk = spread(lifted, full_qk[block]).astype(jnp.bfloat16)
+        values = spread(lifted, full_v[block]).astype(jnp.bfloat16)
+        attended = attend(qk, values)
+        stream = stream + collapse(attended, full_out[block]) + biases[1 + block]
+        kept.append((hat, inverse, lifted.T, qk, values, attended))
+    hat_feed, inverse_feed = layer_stats(stream)
+    inputs_up = (hat_feed * gains[3] + shifts[3]).astype(jnp.bfloat16)
+    pre_act = [
+        spread(inputs_up, full_up[half])
+        + hidden_full[:, None, half * wide : half * wide + wide]
+        for half in range(2)
+    ]
+    slopes = [
+        jax.vjp(partial(jax.nn.gelu, approximate=False), pre)[1](jnp.ones_like(pre))[0]
+        for pre in pre_act
+    ]
+    hidden = [jax.nn.gelu(pre, approximate=False).astype(jnp.bfloat16) for pre in pre_act]
+    stream = stream + collapse(hidden[0], full_down[0]) + collapse(hidden[1], full_down[1])
+    stream = stream + biases[3]
+    inputs_proj = stream.astype(jnp.bfloat16)
+    moved = spread(inputs_proj, full_proj) + biases[4].reshape(tensor_size, 1, width)
+    moved = moved.astype(jnp.bfloat16)
+
+    bias_grads = [None] * 4
+    gain_grads = [None] * 3
+    shift_grads = [None] * 3
+    turned, parts = [None] * 8, [None] * 12
+    turned[1], turned[5], turned[7] = inputs_up.T, inputs_proj.T, inputs_in.T
+    parts[0], parts[1] = hidden[1], hidden[0]
+    parts[9] = moved_part
+    grad_stream = collapse(grad_moved, full_proj)
+    bias_grads[3] = jnp.sum(grad_stream, 0)
+    grad_low = grad_stream.astype(jnp.bfloat16)
+    turned[0] = grad_low.T
+    hidden_grads = [None, None]
+    grad_normed = 0.0
+    for half in (1, 0):
+        grad_hidden = spread(grad_low, full_down[half])
+        grad_pre = grad_hidden * slopes[half]
+        hidden_grads[half] = jnp.sum(grad_pre, 1)
+        parts[3 - half] = grad_pre.astype(jnp.bfloat16)
+        grad_normed = grad_normed + collapse(parts[3 - half], full_up[half])
+    hidden_grad = side(hidden_grads, 1)
+    grad_layer, gain_grads[2], shift_grads[2] = layer_back(
+        grad_normed, hat_feed, inverse_feed, gains[3]
+    )
+    grad_stream = grad_stream + grad_layer
+    for block in (1, 0):
+        hat, inverse, lifted_turned, qk, values, attended = kept[block]
+        bias_grads[1 + block] = jnp.sum(grad_stream, 0)
         grad_low = grad_stream.astype(jnp.bfloat16)
-        turned[0] = grad_low.T
-        hidden_grads = [None, None]
-        grad_normed = 0.0
-        for half in (1, 0):
-            grad_hidden = spread(grad_low, full_down[half])
-            grad_pre = grad_hidden * slopes[half]
-            hidden_grads[half] = jnp.sum(grad_pre, 1)
-            parts[3 - half] = grad_pre.astype(jnp.bfloat16)
-            grad_normed = grad_normed + collapse(parts[3 - half], full_up[half])
-        hidden_grad = side(hidden_grads, 1)
-        grad_layer, gain_grads[2], shift_grads[2] = layer_back(
-            grad_normed, hat_feed, inverse_feed, gains[3]
+        turned[2 if block == 1 else 6] = grad_low.T
+        pair = [attended, empty] if block == 1 else [empty, attended]
+        parts[4 if block == 1 else 10] = side(pair, 2)
+        grad_attended = spread(grad_low, full_out[block]).astype(jnp.bfloat16)
+        grad_qk, grad_values = attend_back(qk, values, grad_attended)
+        turned[3 if block == 1 else 4] = lifted_turned
+        parts[6 if block == 1 else 8] = side([grad_values, empty], 2)
+        parts[5 if block == 1 else 7] = grad_qk
+        grad_lifted = collapse(grad_qk, full_qk[block]) + collapse(grad_values, full_v[block])
+        grad_layer, gain_grads[block], shift_grads[block] = layer_back(
+            grad_lifted, hat, inverse, gains[1 + block]
         )
         grad_stream = grad_stream + grad_layer
-        for block in (1, 0):
-            hat, inverse, lifted_turned, qk, values, attended = kept[block]
-            bias_grads[1 + block] = jnp.sum(grad_stream, 0)
-            grad_low = grad_stream.astype(jnp.bfloat16)
-            turned[2 if block == 1 else 6] = grad_low.T
-            pair = [attended, empty] if block == 1 else [empty, attended]
-            parts[4 if block == 1 else 10] = side(pair, 2)
-            grad_attended = spread(grad_low, full_out[block]).astype(jnp.bfloat16)
-            grad_qk, grad_values = attend_back(qk, values, grad_attended)
-            turned[3 if block == 1 else 4] = lifted_turned
-            parts[6 if block == 1 else 8] = side([grad_values, empty], 2)
-            parts[5 if block == 1 else 7] = grad_qk
-            grad_lifted = collapse(grad_qk, full_qk[block]) + collapse(grad_values, full_v[block])
-            grad_layer, gain_grads[block], shift_grads[block] = layer_back(
-                grad_lifted, hat, inverse, gains[1 + block]
-            )
-            grad_stream = grad_stream + grad_layer
-        bias_grads[0] = jnp.sum(grad_stream, 0)
-        grad_low = grad_stream.astype(jnp.bfloat16)
-        grad_low_parts = jnp.transpose(grad_low.reshape(rows, tensor_size, width), (1, 0, 2))
-        parts[11] = side([empty, grad_low_parts], 2)
-        turned, parts = jnp.stack(turned, 0), jnp.stack(parts, 0)
-        reduced = reduce_plain(turned, parts)
-        grad_normed = collapse(grad_low_parts, full_in).astype(jnp.bfloat16)
-        grad_normed = jnp.transpose(grad_normed.reshape(rows, tensor_size, width), (1, 0, 2))
-        arrived_grad = exchange(grad_normed)
-        vectors = jnp.stack(gain_grads + shift_grads + bias_grads, 0)
+    bias_grads[0] = jnp.sum(grad_stream, 0)
+    grad_low = grad_stream.astype(jnp.bfloat16)
+    grad_low_parts = jnp.transpose(grad_low.reshape(rows, tensor_size, width), (1, 0, 2))
+    parts[11] = side([empty, grad_low_parts], 2)
+    turned, parts = jnp.stack(turned, 0), jnp.stack(parts, 0)
+    reduced = reduce_plain(turned, parts)
+    grad_normed = collapse(grad_low_parts, full_in).astype(jnp.bfloat16)
+    grad_normed = jnp.transpose(grad_normed.reshape(rows, tensor_size, width), (1, 0, 2))
+    arrived_grad = exchange(grad_normed)
+    vectors = jnp.stack(gain_grads + shift_grads + bias_grads, 0)
 
     moved_local = back_to_channels(exchange(moved), slots, pixels).astype(jnp.float32)
     output = jnp.where(flags, start + moved_local, start).astype(jnp.bfloat16)
@@ -1788,8 +2169,9 @@
         P("tensor", "dp"),
         P("dp", "tensor"),
     )
+    kernels_fit = (mesh.shape["dp"], mesh.shape["tensor"]) == (8, 4)
     return jax.shard_map(
-        partial(body, tuple(mesh.shape[name] for name in ("dp", "tensor")) == (8, 4)),
+        kernel_body if kernels_fit else body,
         mesh=mesh,
         in_specs=placed,
         out_specs=(

time: 826 us -> 752 us (0.910)
  blocking collectives: 35 us -> 0 us
  local copies, waits for them, and re-layouts: 62.8 us -> 30 us
  other arithmetic: 32.7 us -> 4.61 us
  Pallas kernels: 670 us -> 690 us
  between operations: 15 us -> 1.47 us
  starting transfers between devices: 8.57 us -> 17.4 us
    pallas_call x1 -> x3, Pallas kernels: 294 us -> 330 us  [the longest x1 298 us: forward_all(): pl.pallas_call(forward_kernel, in_specs=[near, anywhere, near, near], out...]
    psum x1 -> x0, blocking collectives: 35 us -> none  [body(): lax.psum(jnp.concatenate([vectors, group_gain_grad, group_shift_grad, bia...]
    pallas_call x1, Pallas kernels: 376 us -> 361 us  [backward_all(): pl.pallas_call(backward_kernel, in_specs=[anywhere] * 8 + [near], out_spe...]
    reduce_sum x9 -> x1, other arithmetic: 13 us -> 0.07 us  [kernel_body(): vectors = jnp.sum(exchange(vectors), 0)]
    unnamed x69 -> x34, local copies, waits for them, and re-layouts: 21.4 us -> 11.8 us
  transfers between devices with their start and end apart: 3 -> 6, of which waited for: 0 -> 3; matrix products, arithmetic and copies ran while one was open for 10% -> 2% of each run, Pallas kernels for 81% -> 90%
where the time goes in v6:
time: 752 us; the launch traced here: 751 us
  Pallas kernels  690 us (92%)
  local copies, waits for them, and re-layouts  30 us (4%)
  starting transfers between devices  17.4 us (2%)
    pallas_call x1, Pallas kernels, backward_all(): pl.pallas_call(backward_kernel, in_specs=[anywhere] * 8 + [near], out_spe...  361 us
    pallas_call x1, Pallas kernels, forward_all(): pl.pallas_call(forward_kernel, in_specs=[near, anywhere, near, near], out...  298 us
    pallas_call x1, Pallas kernels, leave(): pl.pallas_call(leave_kernel, in_specs=[near] * 4 + [pl.BlockSpec(memory_s...  19.5 us
  transfers between devices with their start and end apart: 6, of which 3 were waited for; matrix products, arithmetic and copies ran while one was open for 2% of the time, Pallas kernels for 90%

profile of v6, /device:TPU:0, one launch (start us, length us, event | category | flops | bytes accessed | tf_op | source)
XLA Modules:
  0.0 750.9 jit_solution(12742690966038374940)
XLA Ops:
  3.0 1.3 copy-done
  4.3 1.3 copy-done.1
  5.6 1.1 copy-done.3
  11.5 12.5 %shard_map.220 = (bf16[4,512,320]{2,1,0:T(8,128)(2,1)}, bf16[4,512,320]{2,1,0:T(8,128)(2,1)}, bf16[9,160,640]{2,1,0:T(8,128)(2,1)}, f32[320,1]{1,0:T(8,128)S(1)}...) custom-call(bf16[1,16,320,128]{3,2,1,0:T(8,128)(2,1)S(1)} %copy-done, bf16[1,16,320,128]{3,2,1,0:T(8,128)(2,1)S(1)} %copy-done.1, ...), custom_call_target="tpu_custom_call" | custom-call | tf_op jit(solution)/shard_map/pallas_call | solution.py:1703
  25.3 2.5 copy.33
  27.8 4.4 all-to-all-start
  32.3 1.8 concatenate.18.params_ref
  35.2 298.0 %shard_map.221 = (bf16[9,2,2,4,2,160,640]{6,5,4,3,2,1,0:T(8,128)(2,1)}, bf16[12,4,512,640]{3,2,1,0:T(8,128)(2,1)}, bf16[8,1280,512]{2,1,0:T(8,128)(2,1)}, f32[3,...) custom-call(bf16[9,160,640]{2,1,0:T(8,128)(2,1)} %get-tuple-element., ...), custom_call_target="tpu_custom_call" | custom-call | tf_op jit(solution)/shard_map/pallas_call | solution.py:736
  333.2 2.5 copy.35
  336.7 4.3 all-to-all-start.1
  341.0 1.8 copy.34
  342.9 2.3 pad.4.moved_ref
  345.2 360.6 %shard_map.222 = (f32[9,160,640]{2,1,0:T(8,128)}, bf16[12,4,512,640]{3,2,1,0:T(8,128)(2,1)}, bf16[8,1280,512]{2,1,0:T(8,128)(2,1)}, bf16[8,1280,512]{2,1,0:T(8,1...) custom-call(bf16[9,2,2,4,2,160,640]{6,5,4,3,2,1,0:T(8,128)(2,1)} %ge, ...), custom_call_target="tpu_custom_call", output_to_operand_aliasing={{1}: (1, {}), {2}: (2, {})} | custom-call | tf_op jit(solution)/shard_map/pallas_call | solution.py:1500
  708.5 3.3 all-to-all-start.2
  712.0 2.6 copy.36.moved_ref
  714.5 19.5 %shard_map.223 = (bf16[1,16,320,128]{3,2,1,0:T(8,128)(2,1)}, f32[1,16,320,128]{3,2,1,0:T(8,128)}, f32[320,1]{1,0:T(8,128)}, f32[320,1]{1,0:T(8,128)}, f32[160,32...) custom-call(bf16[4,512,320]{2,1,0:T(8,128)(2,1)} %get-tuple-element., ...), custom_call_target="tpu_custom_call" | custom-call | tf_op jit(solution)/shard_map/pallas_call | solution.py:1835
  734.0 1.1 reduce.1
  735.0 1.1 reduce.2
  736.3 1.1 collective-permute-start
  737.3 2.8 collective-permute-done
  740.1 1.7 collective-permute-start.1
  741.8 2.1 collective-permute-done.1
  743.9 2.6 collective-permute-start.2
  746.6 2.1 collective-permute-done.2
  (67 shorter events, 15.2 us)
Async XLA Ops:
  2.8 21.1 %copy-start.2 = (f32[320,1]{1,0:T(8,128)}, f32[320,1]{1,0:T(8,128)S(1)}, u32[]{:S(2)}) copy-start(f32[320,1]{1,0:T(8,128)S(1)} %copy.31.gain_ref) | copy-start | bytes 3844
  3.0 1.3 copy-start
  4.3 1.3 copy-start.1
  5.6 1.1 copy-start.3
  6.7 1.0 copy-start.4
  7.7 1.0 copy-start.5
  8.7 0.9 copy-start.6
  9.7 0.9 copy-start.9
  10.6 0.9 copy-start.10
  24.0 0.7 copy-start.7
  24.6 0.7 copy-start.8
  27.8 4.4 copy-start.15
  27.8 4.5 copy-start.12
  27.8 4.5 copy-start.13
  27.8 4.5 copy-start.14
  27.8 307.8 %all-to-all-start = ((bf16[4,512,320]{1,2,0:T(8,128)(2,1)}), bf16[4,512,320]{1,2,0:T(8,128)(2,1)S(1)}, u32[]{:S(2)}, u32[]{:S(2)}) async-start(bf16[4,512,320]{1,2,0:T(8,128)(2,1)} %copy.33), calls=%async_computation | async-start | bytes 2621440 | tf_op jit(solution)/shard_map/all_to_all | solution.py:1589
  335.7 1.1 copy-start.11
  336.7 371.8 %all-to-all-start.1 = ((bf16[4,512,320]{1,2,0:T(8,128)(2,1)}), bf16[4,512,320]{1,2,0:T(8,128)(2,1)}, u32[]{:S(2)}, u32[]{:S(2)}) async-start(bf16[4,512,320]{1,2,0:T(8,128)(2,1)} %copy.35), calls=%async_computation.1 | async-start | bytes 2621440 | tf_op jit(solution)/shard_map/all_to_all | solution.py:1589
  708.5 27.6 %all-to-all-start.2 = ((f32[4,1,4480]{2,1,0:T(1,128)}), f32[4,1,4480]{2,1,0:T(1,128)S(1)}, u32[]{:S(2)}, u32[]{:S(2)}) async-start(f32[4,1,4480]{2,1,0:T(1,128)} %copy.39), calls=%async_computation.2 | async-start | bytes 143360 | tf_op jit(solution)/shard_map/all_to_all | solution.py:1589
  736.3 3.8 collective-permute-start
  740.1 3.8 collective-permute-start.1
  743.9 4.7 collective-permute-start.2

commit v7 on v6

--- a/solution.py
+++ b/solution.py
@@ -239,6 +239,7 @@
     x_ref,
     params_ref,
     position_ref,
+    grad_ref,
     whole_ref,
     q_ref,
     pt_ref,
@@ -246,6 +247,7 @@
     qk_ref,
     v_ref,
     slope_ref,
+    grad_got,
     moved_ref,
     joined_ref,
     stream,
@@ -454,11 +456,19 @@
                 recv_sem=peer_recv.at[1, index],
                 **target,
             ),
+            pltpu.make_async_remote_copy(
+                src_ref=grad_ref.at[t],
+                dst_ref=grad_got.at[own_t],
+                send_sem=peer_send.at[2, index],
+                recv_sem=peer_recv.at[2, index],
+                **target,
+            ),
         )
 
     own_peer = (
         pltpu.make_async_copy(params_ref, params_got.at[own_t], peer_send.at[0, 3]),
         pltpu.make_async_copy(x_ref.at[own_t], x_got.at[own_t], peer_send.at[1, 3]),
+        pltpu.make_async_copy(grad_ref.at[own_t], grad_got.at[own_t], peer_send.at[2, 3]),
     )
     for index in range(3):
         for copy in peer_copies(index):
@@ -629,9 +639,9 @@
 
     def do_join(op):
         for index in range(3):
-            for copy in peer_copies(index):
+            for copy in peer_copies(index)[:2]:
                 copy.wait_recv()
-        for copy in own_peer:
+        for copy in own_peer[:2]:
             copy.wait()
         for t in range(4):
             lanes = slice(t * width, (t + 1) * width)
@@ -726,17 +736,19 @@
     for index in range(3):
         for copy in peer_copies(index):
             copy.wait_send()
-
-
-def forward_all(shards, rows_in, params, position):
+        peer_copies(index)[2].wait_recv()
+    own_peer[2].wait()
+
+
+def forward_all(shards, rows_in, params, position, grad):
     units, share, wide = shards.shape
     rows, width = rows_in.shape[1], rows_in.shape[2]
     low = jnp.bfloat16
     anywhere, near = pl.BlockSpec(memory_space=pl.ANY), pl.BlockSpec(memory_space=pltpu.VMEM)
     return pl.pallas_call(
         forward_kernel,
-        in_specs=[near, anywhere, near, near],
-        out_specs=[anywhere] * 7 + [near] * 2,
+        in_specs=[near, anywhere, near, near, near],
+        out_specs=[anywhere] * 8 + [near] * 2,
         out_shape=[
             jax.ShapeDtypeStruct((units, 2, 2, 4, 2, share, wide), low),
             jax.ShapeDtypeStruct((12, 4, rows, wide), low),
@@ -745,6 +757,7 @@
             jax.ShapeDtypeStruct((2, 4, rows, wide), low),
             jax.ShapeDtypeStruct((2, 4, rows, width), low),
             jax.ShapeDtypeStruct((2, 4, rows, wide), low),
+            jax.ShapeDtypeStruct((4, rows, width), low),
             jax.ShapeDtypeStruct((4, rows, width), low),
             jax.ShapeDtypeStruct((16, C), jnp.float32),
         ],
@@ -765,8 +778,8 @@
             pltpu.SemaphoreType.DMA((2,)),
             pltpu.SemaphoreType.DMA((1,)),
             pltpu.SemaphoreType.DMA((4, 4, 3)),
-            pltpu.SemaphoreType.DMA((2, 4)),
-            pltpu.SemaphoreType.DMA((2, 3)),
+            pltpu.SemaphoreType.DMA((3, 4)),
+            pltpu.SemaphoreType.DMA((3, 3)),
             pltpu.SemaphoreType.DMA((units,)),
             pltpu.SemaphoreType.DMA((units, 2, 5)),
             pltpu.SemaphoreType.DMA((units, 2, 2, 4, 2)),
@@ -775,7 +788,7 @@
         compiler_params=pltpu.CompilerParams(
             collective_id=0, has_side_effects=True, vmem_limit_bytes=60 << 20
         ),
-    )(shards, rows_in, params, position)
+    )(shards, rows_in, params, position, grad)
 
 
 def backward_kernel(
@@ -786,6 +799,7 @@
     qk_ref,
     v_ref,
     slope_ref,
+    grad_ref,
     moved_ref,
     joined_ref,
     out_ref,
@@ -794,6 +808,7 @@
     ptx_ref,
     qx_ref,
     got_ref,
+    moved_got,
     vec_ref,
     hidden_ref,
     p_buf,
@@ -865,10 +880,9 @@
         )
 
     def known_q(index, yy):
-        source = moved_ref if index == 9 else q_ref.at[index]
-        return give_q(index, yy, source.at[2 * yy + 1 - c])
-
-    known = (0, 1, 4, 9, 10)
+        return give_q(index, yy, q_ref.at[index, 2 * yy + 1 - c])
+
+    known = (0, 1, 4, 10)
     known_p = (1, 5, 3, 4, 7)
     for index in known[:2]:
         for yy in range(2):
@@ -967,25 +981,14 @@
 
                     each(4, quarter, use)
 
-    def moved_own(t):
-        return pltpu.make_async_copy(cb.at[4], q_ref.at[9, t], misc_sem.at[0])
-
     def do_collapse(op):
         which, routed, t = op["aux"] % 5, op["aux"] // 5, op["t"]
 
-        @pl.when(which == 4)
-        def _():
-            load = aux_load(moved_ref.at[t], cb.at[4], 0)
-            load.start()
-            load.wait()
-            pl.when(c == t % 2)(lambda: moved_own(t).start())
-
         def multiply(rows):
             gn[rows, :] += dot_rows(cb[which, rows, :], wb[op["slot"]].reshape(C, WIDE))
 
         each(2, half_rows, multiply)
         pl.when(routed > 0)(lambda: route(cb.at[which], routed - 1, t)[1]())
-        pl.when((which == 4) & (c == t % 2))(lambda: moved_own(t).wait())
 
     def do_attention(op):
         block, t = op["aux"], op["t"]
@@ -1077,11 +1080,24 @@
         each(rows_all // chunk, chunk, use)
 
     def do_place(op):
-        t = op["t"]
+        t, aux = op["t"], op["aux"]
         side = t % 2
+
+        @pl.when(aux == 1)
+        def _():
+            load = aux_load(grad_ref.at[t], datt, 0)
+            load.start()
+            load.wait()
+
+            def use(rows):
+                cb[side, rows, 0:width] = jnp.zeros((quarter, width), jnp.bfloat16)
+                cb[side, rows, width:] = datt[rows, :]
+
+            each(4, quarter, use)
+
         for block in range(4):
 
-            @pl.when(t == block)
+            @pl.when((aux == 0) & (t == block))
             def _(block=block):
                 def use(rows):
                     cb[side, rows, 0:width] = jnp.zeros((quarter, width), jnp.bfloat16)
@@ -1089,7 +1105,7 @@
 
                 each(4, quarter, use)
 
-        route(cb.at[side], 11, t)[0]()
+        route(cb.at[side], 11 - 2 * aux, t)[0]()
 
     peers = (("y", far_y * 2 + c), ("core", y * 2 + 1 - c), ("cross", far_y * 2 + 1 - c))
 
@@ -1098,13 +1114,30 @@
         return pltpu.make_async_remote_copy(
             src_ref=dn.at[t],
             dst_ref=got_ref.at[own_t],
-            send_sem=peer_send.at[index],
-            recv_sem=peer_recv.at[index],
+            send_sem=peer_send.at[0, index],
+            recv_sem=peer_recv.at[0, index],
             device_id=at.to[kind],
             device_id_type=MESH_ID,
         )
 
-    own_peer = pltpu.make_async_copy(dn.at[own_t], got_ref.at[own_t], peer_send.at[3])
+    def moved_copy(index):
+        kind, t = peers[index]
+        return pltpu.make_async_remote_copy(
+            src_ref=moved_ref.at[t],
+            dst_ref=moved_got.at[own_t],
+            send_sem=peer_send.at[1, index],
+            recv_sem=peer_recv.at[1, index],
+            device_id=at.to[kind],
+            device_id_type=MESH_ID,
+        )
+
+    own_peer = pltpu.make_async_copy(dn.at[own_t], got_ref.at[own_t], peer_send.at[0, 3])
+    own_moved = pltpu.make_async_copy(
+        moved_ref.at[own_t], moved_got.at[own_t], peer_send.at[1, 3]
+    )
+    for index in range(3):
+        moved_copy(index).start()
+    own_moved.start()
 
     def do_send(op):
         for t in range(4):
@@ -1148,10 +1181,13 @@
     def inputs(t):
         return [(7, None, t, 0), (2, 1, t, t % 2 + 5 * 12)]
 
+    def outputs(t):
+        return [(7, None, t, 1), (2, 4, t, t % 2 + 5 * 10)]
+
     stage_count = 6
     plan = Plan(2 * stage_count, True)
     for turn, steps in {
-        -1: [(2, 4, t, 4) for t in four] + [(6, None, 0, 0), (5, None, 0, 0), (9, None, 0, 0)],
+        -1: outputs(0) + outputs(1) + outputs(2) + outputs(3) + [(6, None, 0, 0), (5, None, 0, 0), (9, None, 0, 0)],
         0: feed(1),
         1: feed(0),
         2: [(4, None, 0, 2), (5, None, 0, 2)] + heads(1, 0) + [(9, None, 0, 2)],
@@ -1268,7 +1304,7 @@
             ]
         return loads
 
-    def products(slot, p_index, q_index, more):
+    def products(slot, p_index, q_index, mixed, more):
         for load in product_loads(p_index, q_index):
             load.wait()
 
@@ -1276,13 +1312,28 @@
             side, zz = step // 4, step % 4
             yy = jnp.where(side == 0, far_y, y)
             rows = pl.ds(pl.multiple_of(zz * 2 * share, 2 * share), 2 * share)
-            result = dot_plain(p_buf[0, rows, :], q_buf[0, yy]) + dot_plain(
-                p_buf[1, rows, :], q_buf[1, yy]
-            )
-            result = result.reshape(2, share, WIDE)
-            earlier = dw[slot.d, yy, zz].astype(jnp.float32)
-            result = result + jnp.where(more == 1, earlier, 0.0)
-            dw[slot.d, yy, zz] = result.astype(jnp.bfloat16)
+
+            def part(first, last):
+                result = dot_plain(p_buf[0, rows, :], q_buf[0, yy, :, first:last])
+                result = result + dot_plain(p_buf[1, rows, :], q_buf[1, yy, :, first:last])
+                return result.reshape(2, share, last - first)
+
+            @pl.when(mixed == 0)
+            def _():
+                dw[slot.d, yy, zz] = part(0, WIDE).astype(jnp.bfloat16)
+
+            @pl.when((mixed == 1) & (more == 0))
+            def _():
+                dw[slot.d, yy, zz, :, :, 0:384] = part(0, 384).astype(jnp.bfloat16)
+
+            @pl.when((mixed == 1) & (more == 1))
+            def _():
+                result = part(256, WIDE)
+                shared = dw[slot.d, yy, zz, :, :, 256:384].astype(jnp.float32)
+                shared = shared + result[:, :, 0:128]
+                dw[slot.d, yy, zz, :, :, 256:384] = shared.astype(jnp.bfloat16)
+                dw[slot.d, yy, zz, :, :, 384:] = result[:, :, 128:].astype(jnp.bfloat16)
+
             return carry
 
         lax.fori_loop(0, 8, one, 0)
@@ -1326,6 +1377,7 @@
                 slot,
                 jnp.where(more == 1, 5 + extra, p_index),
                 jnp.where(more == 1, UNITS + extra, turn),
+                mixed,
                 more,
             )
             return carry
@@ -1482,7 +1534,9 @@
     out_copy(UNITS - 1).wait()
     for index in range(3):
         peer_copy(index).wait()
+        moved_copy(index).wait()
     own_peer.wait()
+    own_moved.wait()
     for index in known:
         for yy in range(2):
             known_q(index, yy).wait_send()
@@ -1490,7 +1544,7 @@
         give_p(index).wait_send()
 
 
-def backward_all(whole, q_all, pt_all, streams, qk, values, slopes, moved_part, joined):
+def backward_all(whole, q_all, pt_all, streams, qk, values, slopes, grad, moved, joined):
     share = whole.shape[5]
     count_p, unused, rows = pt_all.shape
     width = values.shape[3]
@@ -1499,14 +1553,15 @@
     anywhere, near = pl.BlockSpec(memory_space=pl.ANY), pl.BlockSpec(memory_space=pltpu.VMEM)
     return pl.pallas_call(
         backward_kernel,
-        in_specs=[anywhere] * 8 + [near],
-        out_specs=[anywhere] * 6 + [near] * 2,
+        in_specs=[anywhere] * 9 + [near],
+        out_specs=[anywhere] * 7 + [near] * 2,
         out_shape=[
             jax.ShapeDtypeStruct((UNITS, share, WIDE), jnp.float32),
             jax.ShapeDtypeStruct(q_all.shape, low),
             jax.ShapeDtypeStruct(pt_all.shape, low),
             jax.ShapeDtypeStruct(pt_all.shape, low),
             jax.ShapeDtypeStruct((q_all.shape[0], 2, rows, WIDE), low),
+            jax.ShapeDtypeStruct((4, rows, width), low),
             jax.ShapeDtypeStruct((4, rows, width), low),
             jax.ShapeDtypeStruct((16, C), jnp.float32),
             jax.ShapeDtypeStruct((4, 8, WIDE), jnp.float32),
@@ -1546,13 +1601,13 @@
             pltpu.SemaphoreType.DMA((12, 2)),
             pltpu.SemaphoreType.DMA((5,)),
             pltpu.SemaphoreType.DMA((2,)),
-            pltpu.SemaphoreType.DMA((4,)),
-            pltpu.SemaphoreType.DMA((3,)),
+            pltpu.SemaphoreType.DMA((2, 4)),
+            pltpu.SemaphoreType.DMA((2, 3)),
         ],
         compiler_params=pltpu.CompilerParams(
             collective_id=1, has_side_effects=True, vmem_limit_bytes=63 << 20
         ),
-    )(whole, q_all, pt_all, streams, qk, values, slopes, moved_part, joined)
+    )(whole, q_all, pt_all, streams, qk, values, slopes, grad, moved, joined)
 
 
 def gather_plain(shards):
@@ -1908,14 +1963,11 @@
         weight_down,
         weight_proj,
     )
-    grad_moved = exchange(moved_sent)
-    moved_part = jnp.pad(grad_moved, ((0, 0), (0, 0), (width, 0)))
-    whole, q_all, pt_all, streams, qk_all, v_all, slopes, moved, joined = forward_all(
-        shards, sent, params, make_positions()
+    whole, q_all, pt_all, streams, qk_all, v_all, slopes, grad, moved, joined = forward_all(
+        shards, sent, params, make_positions(), moved_sent
     )
-    moved_back = exchange(moved)
-    reduced, q_all, pt_all, unused, unused, grad_back, sums, hidden_sums = backward_all(
-        whole, q_all, pt_all, streams, qk_all, v_all, slopes, moved_part, joined
+    reduced, q_all, pt_all, unused, unused, grad_back, moved_back, sums, hidden_sums = backward_all(
+        whole, q_all, pt_all, streams, qk_all, v_all, slopes, grad, moved, joined
     )
     output, latent_grad, group_gain, group_shift, weights = leave(
         grad_back,

time: 752 us -> 736 us (0.979)
  local copies, waits for them, and re-layouts: 30 us -> 19.3 us
  starting transfers between devices: 17.4 us -> 8.23 us
    all_to_all x3 -> x1, starting transfers between devices: 12 us -> 3.29 us  [exchange(): return lax.all_to_all(parts, 'tensor', 0, 0, tiled=True)]
  transfers between devices with their start and end apart: 6 -> 4, of which waited for: 3 -> 3; matrix products, arithmetic and copies ran while one was open for 2% -> 0% of each run, Pallas kernels for 90% -> 3%
where the time goes in v7:
time: 736 us; the launch traced here: 734 us
  Pallas kernels  693 us (94%)
  local copies, waits for them, and re-layouts  19.3 us (3%)
  starting transfers between devices  8.23 us (1%)
  waiting for transfers between devices  7.44 us (1%)
    pallas_call x1, Pallas kernels, backward_all(): pl.pallas_call(backward_kernel, in_specs=[anywhere] * 9 + [near], out_spe...  354 us
    pallas_call x1, Pallas kernels, forward_all(): pl.pallas_call(forward_kernel, in_specs=[near, anywhere, near, near, near...  308 us
    pallas_call x1, Pallas kernels, leave(): pl.pallas_call(leave_kernel, in_specs=[near] * 4 + [pl.BlockSpec(memory_s...  19.5 us
  transfers between devices with their start and end apart: 4, of which 3 were waited for; matrix products, arithmetic and copies ran while one was open for 0% of the time, Pallas kernels for 3%

profile of v7, /device:TPU:0, one launch (start us, length us, event | category | flops | bytes accessed | tf_op | source)
XLA Modules:
  0.0 734.3 jit_solution(11984661385074491455)
XLA Ops:
  3.8 1.0 fusion.position_ref
  4.8 3.2 concatenate.18.params_ref
  8.1 1.3 copy-done
  9.4 1.3 copy-done.1
  10.7 1.1 copy-done.3
  11.8 1.0 copy-done.4
  12.8 1.0 copy-done.5
  13.8 0.9 copy-done.6
  14.8 0.9 copy-done.9
  15.7 0.9 copy-done.10
  16.6 12.5 %shard_map.220 = (bf16[4,512,320]{2,1,0:T(8,128)(2,1)}, bf16[4,512,320]{2,1,0:T(8,128)(2,1)}, bf16[9,160,640]{2,1,0:T(8,128)(2,1)}, f32[320,1]{1,0:T(8,128)S(1)}...) custom-call(bf16[1,16,320,128]{3,2,1,0:T(8,128)(2,1)S(1)} %copy-done, bf16[1,16,320,128]{3,2,1,0:T(8,128)(2,1)S(1)} %copy-done.1, ...), custom_call_target="tpu_custom_call" | custom-call | tf_op jit(solution)/shard_map/pallas_call | solution.py:1758
  30.4 307.5 %shard_map.221 = (bf16[9,2,2,4,2,160,640]{6,5,4,3,2,1,0:T(8,128)(2,1)}, bf16[12,4,512,640]{3,2,1,0:T(8,128)(2,1)}, bf16[8,1280,512]{2,1,0:T(8,128)(2,1)}, f32[3,...) custom-call(bf16[9,160,640]{2,1,0:T(8,128)(2,1)} %get-tuple-element., ...), custom_call_target="tpu_custom_call" | custom-call | tf_op jit(solution)/shard_map/pallas_call | solution.py:748
  337.9 353.9 %shard_map.222 = (f32[9,160,640]{2,1,0:T(8,128)}, bf16[12,4,512,640]{3,2,1,0:T(8,128)(2,1)}, bf16[8,1280,512]{2,1,0:T(8,128)(2,1)}, bf16[8,1280,512]{2,1,0:T(8,1...) custom-call(bf16[9,2,2,4,2,160,640]{6,5,4,3,2,1,0:T(8,128)(2,1)} %ge, ...), custom_call_target="tpu_custom_call", output_to_operand_aliasing={{1}: (1, {}), {2}: (2, {})} | custom-call | tf_op jit(solution)/shard_map/pallas_call | solution.py:1554
  692.7 1.0 reshape.123
  694.5 3.3 all-to-all-start
  697.9 19.5 %shard_map.223 = (bf16[1,16,320,128]{3,2,1,0:T(8,128)(2,1)}, f32[1,16,320,128]{3,2,1,0:T(8,128)}, f32[320,1]{1,0:T(8,128)}, f32[320,1]{1,0:T(8,128)}, f32[160,32...) custom-call(bf16[4,512,320]{2,1,0:T(8,128)(2,1)} %get-tuple-element., ...), custom_call_target="tpu_custom_call" | custom-call | tf_op jit(solution)/shard_map/pallas_call | solution.py:1890
  717.4 1.1 reduce.1
  718.5 1.1 reduce.2
  719.7 1.1 collective-permute-start
  720.8 2.7 collective-permute-done
  723.5 1.5 collective-permute-start.1
  725.0 2.3 collective-permute-done.1
  727.4 2.3 collective-permute-start.2
  729.7 2.4 collective-permute-done.2
  (48 shorter events, 8.0 us)
Async XLA Ops:
  3.6 334.2 %copy-start.2 = (f32[320,1]{1,0:T(8,128)}, f32[320,1]{1,0:T(8,128)S(1)}, u32[]{:S(2)}) copy-start(f32[320,1]{1,0:T(8,128)S(1)} %copy.31.gain_ref) | copy-start | bytes 3844
  8.1 1.3 copy-start
  9.4 1.3 copy-start.1
  10.7 1.1 copy-start.3
  11.8 1.0 copy-start.4
  12.8 1.0 copy-start.5
  13.8 0.9 copy-start.6
  14.8 0.9 copy-start.9
  15.7 0.9 copy-start.10
  29.0 0.7 copy-start.7
  29.7 0.7 copy-start.8
  694.5 25.0 %all-to-all-start = ((f32[4,1,4480]{2,1,0:T(1,128)}), f32[4,1,4480]{2,1,0:T(1,128)S(1)}, u32[]{:S(2)}, u32[]{:S(2)}) async-start(f32[4,1,4480]{2,1,0:T(1,128)} %copy.35), calls=%async_computation | async-start | bytes 143360 | tf_op jit(solution)/shard_map/all_to_all | solution.py:1644
  719.7 3.8 collective-permute-start
  723.5 3.8 collective-permute-start.1
  727.4 4.7 collective-permute-start.2

commit v8 on v7

--- a/solution.py
+++ b/solution.py
@@ -142,6 +142,7 @@
 WIDE = 640
 SLOTS_IN_FLIGHT = 6
 SLOTS_RECEIVED = 4
+AHEAD = 4
 ROWS_A = 96
 MESH_ID = pl.DeviceIdType.MESH
 
@@ -713,10 +714,19 @@
 
     def advance(turn, carry):
         def inner(place, carry):
-            for number in range(count):
-                unit = turn - number
-
-                @pl.when((place == count - 1 - number) & (unit >= 0) & (unit < UNITS))
+            for spot, number in enumerate((count - 1, 0) + tuple(range(count - 2, 0, -1))):
+                unit = turn - number + (AHEAD if number == 0 else 0)
+                if number == 0:
+
+                    @pl.when((place == spot) & (turn == 0))
+                    def _():
+                        def begin(unit, carry):
+                            stage0(unit)
+                            return carry
+
+                        lax.fori_loop(0, AHEAD, begin, 0)
+
+                @pl.when((place == spot) & (unit >= 0) & (unit < UNITS))
                 def _(number=number, unit=unit):
                     stages[number](unit)
 

time: 736 us -> 716 us (0.973)
  Pallas kernels: 693 us -> 673 us
    pallas_call x1, Pallas kernels: 308 us -> 296 us  [forward_all(): pl.pallas_call(forward_kernel, in_specs=[near, anywhere, near, near, near...]
    pallas_call x1, Pallas kernels: 354 us -> 345 us  [backward_all(): pl.pallas_call(backward_kernel, in_specs=[anywhere] * 9 + [near], out_spe...]
where the time goes in v8:
time: 716 us; the launch traced here: 714 us
  Pallas kernels  673 us (94%)
  local copies, waits for them, and re-layouts  19.3 us (3%)
  starting transfers between devices  10.8 us (2%)
    pallas_call x1, Pallas kernels, backward_all(): pl.pallas_call(backward_kernel, in_specs=[anywhere] * 9 + [near], out_spe...  345 us
    pallas_call x1, Pallas kernels, forward_all(): pl.pallas_call(forward_kernel, in_specs=[near, anywhere, near, near, near...  296 us
    pallas_call x1, Pallas kernels, leave(): pl.pallas_call(leave_kernel, in_specs=[near] * 4 + [pl.BlockSpec(memory_s...  19.5 us
  transfers between devices with their start and end apart: 4, of which 3 were waited for; matrix products, arithmetic and copies ran while one was open for 0% of the time, Pallas kernels for 3%

profile of v8, /device:TPU:0, one launch (start us, length us, event | category | flops | bytes accessed | tf_op | source)
XLA Modules:
  0.0 714.4 jit_solution(7202911748873208930)
XLA Ops:
  3.8 1.0 fusion.position_ref
  4.8 3.2 concatenate.18.params_ref
  8.1 1.3 copy-done
  9.4 1.3 copy-done.1
  10.7 1.1 copy-done.3
  11.8 1.0 copy-done.4
  12.8 1.0 copy-done.5
  13.8 0.9 copy-done.6
  14.8 0.9 copy-done.9
  15.7 0.9 copy-done.10
  16.6 12.5 %shard_map.220 = (bf16[4,512,320]{2,1,0:T(8,128)(2,1)}, bf16[4,512,320]{2,1,0:T(8,128)(2,1)}, bf16[9,160,640]{2,1,0:T(8,128)(2,1)}, f32[320,1]{1,0:T(8,128)S(1)}...) custom-call(bf16[1,16,320,128]{3,2,1,0:T(8,128)(2,1)S(1)} %copy-done, bf16[1,16,320,128]{3,2,1,0:T(8,128)(2,1)S(1)} %copy-done.1, ...), custom_call_target="tpu_custom_call" | custom-call | tf_op jit(solution)/shard_map/pallas_call | solution.py:1768
  30.4 295.6 %shard_map.221 = (bf16[9,2,2,4,2,160,640]{6,5,4,3,2,1,0:T(8,128)(2,1)}, bf16[12,4,512,640]{3,2,1,0:T(8,128)(2,1)}, bf16[8,1280,512]{2,1,0:T(8,128)(2,1)}, f32[3,...) custom-call(bf16[9,160,640]{2,1,0:T(8,128)(2,1)} %get-tuple-element., ...), custom_call_target="tpu_custom_call" | custom-call | tf_op jit(solution)/shard_map/pallas_call | solution.py:758
  326.0 345.4 %shard_map.222 = (f32[9,160,640]{2,1,0:T(8,128)}, bf16[12,4,512,640]{3,2,1,0:T(8,128)(2,1)}, bf16[8,1280,512]{2,1,0:T(8,128)(2,1)}, bf16[8,1280,512]{2,1,0:T(8,1...) custom-call(bf16[9,2,2,4,2,160,640]{6,5,4,3,2,1,0:T(8,128)(2,1)} %ge, ...), custom_call_target="tpu_custom_call", output_to_operand_aliasing={{1}: (1, {}), {2}: (2, {})} | custom-call | tf_op jit(solution)/shard_map/pallas_call | solution.py:1564
  672.3 1.0 reshape.123
  674.1 3.3 all-to-all-start
  677.5 19.5 %shard_map.223 = (bf16[1,16,320,128]{3,2,1,0:T(8,128)(2,1)}, f32[1,16,320,128]{3,2,1,0:T(8,128)}, f32[320,1]{1,0:T(8,128)}, f32[320,1]{1,0:T(8,128)}, f32[160,32...) custom-call(bf16[4,512,320]{2,1,0:T(8,128)(2,1)} %get-tuple-element., ...), custom_call_target="tpu_custom_call" | custom-call | tf_op jit(solution)/shard_map/pallas_call | solution.py:1900
  697.0 1.1 reduce.1
  698.0 1.1 reduce.2
  699.3 2.0 collective-permute-start
  701.3 1.8 collective-permute-done
  703.2 2.4 collective-permute-start.1
  705.6 1.8 collective-permute-done.1
  707.4 3.0 collective-permute-start.2
  710.4 1.8 collective-permute-done.2
  (48 shorter events, 8.0 us)
Async XLA Ops:
  3.6 322.3 %copy-start.2 = (f32[320,1]{1,0:T(8,128)}, f32[320,1]{1,0:T(8,128)S(1)}, u32[]{:S(2)}) copy-start(f32[320,1]{1,0:T(8,128)S(1)} %copy.31.gain_ref) | copy-start | bytes 3844
  8.1 1.3 copy-start
  9.4 1.3 copy-start.1
  10.7 1.1 copy-start.3
  11.8 1.0 copy-start.4
  12.8 1.0 copy-start.5
  13.8 0.9 copy-start.6
  14.8 0.9 copy-start.9
  15.7 0.9 copy-start.10
  29.0 0.7 copy-start.7
  29.7 0.7 copy-start.8
  674.1 25.0 %all-to-all-start = ((f32[4,1,4480]{2,1,0:T(1,128)}), f32[4,1,4480]{2,1,0:T(1,128)S(1)}, u32[]{:S(2)}, u32[]{:S(2)}) async-start(f32[4,1,4480]{2,1,0:T(1,128)} %copy.35), calls=%async_computation | async-start | bytes 143360 | tf_op jit(solution)/shard_map/all_to_all | solution.py:1654
  699.3 3.9 collective-permute-start
  703.2 4.2 collective-permute-start.1
  707.4 4.8 collective-permute-start.2

commit v9 on v8

--- a/solution.py
+++ b/solution.py
@@ -898,11 +898,14 @@
         for yy in range(2):
             known_q(index, yy).start()
     give_p(1).start()
-    for index in known[2:]:
-        for yy in range(2):
-            known_q(index, yy).start()
-    for index in known_p[1:]:
-        give_p(index).start()
+
+    def give_rest():
+        for index in known[2:]:
+            for yy in range(2):
+                known_q(index, yy).start()
+        for index in known_p[1:]:
+            give_p(index).start()
+
     def each(count, size, use):
         def one(step, carry):
             use(pl.ds(pl.multiple_of(step * size, size), size))
@@ -1535,6 +1538,7 @@
 
             return lax.fori_loop(0, 2, two, carry)
 
+        pl.when(now == 1)(give_rest)
         lax.fori_loop(0, stage_count, inner, 0)
         pl.when(now < UNITS)(lambda: prepare(now))
         return carry

time: 716 us -> 713 us (level)
  no operation moved by 1% of the time
where the time goes in v9:
time: 713 us; the launch traced here: 711 us
  Pallas kernels  670 us (94%)
  local copies, waits for them, and re-layouts  19.3 us (3%)
  starting transfers between devices  10.4 us (1%)
    pallas_call x1, Pallas kernels, backward_all(): pl.pallas_call(backward_kernel, in_specs=[anywhere] * 9 + [near], out_spe...  342 us
    pallas_call x1, Pallas kernels, forward_all(): pl.pallas_call(forward_kernel, in_specs=[near, anywhere, near, near, near...  296 us
    pallas_call x1, Pallas kernels, leave(): pl.pallas_call(leave_kernel, in_specs=[near] * 4 + [pl.BlockSpec(memory_s...  19.5 us
  transfers between devices with their start and end apart: 4, of which 3 were waited for; matrix products, arithmetic and copies ran while one was open for 0% of the time, Pallas kernels for 3%

profile of v9, /device:TPU:0, one launch (start us, length us, event | category | flops | bytes accessed | tf_op | source)
XLA Modules:
  0.0 711.1 jit_solution(4522461126496462998)
XLA Ops:
  3.8 1.0 fusion.position_ref
  4.8 3.2 concatenate.18.params_ref
  8.1 1.3 copy-done
  9.4 1.3 copy-done.1
  10.7 1.1 copy-done.3
  11.8 1.0 copy-done.4
  12.8 1.0 copy-done.5
  13.8 0.9 copy-done.6
  14.8 0.9 copy-done.9
  15.7 0.9 copy-done.10
  16.6 12.5 %shard_map.220 = (bf16[4,512,320]{2,1,0:T(8,128)(2,1)}, bf16[4,512,320]{2,1,0:T(8,128)(2,1)}, bf16[9,160,640]{2,1,0:T(8,128)(2,1)}, f32[320,1]{1,0:T(8,128)S(1)}...) custom-call(bf16[1,16,320,128]{3,2,1,0:T(8,128)(2,1)S(1)} %copy-done, bf16[1,16,320,128]{3,2,1,0:T(8,128)(2,1)S(1)} %copy-done.1, ...), custom_call_target="tpu_custom_call" | custom-call | tf_op jit(solution)/shard_map/pallas_call | solution.py:1772
  30.4 295.6 %shard_map.221 = (bf16[9,2,2,4,2,160,640]{6,5,4,3,2,1,0:T(8,128)(2,1)}, bf16[12,4,512,640]{3,2,1,0:T(8,128)(2,1)}, bf16[8,1280,512]{2,1,0:T(8,128)(2,1)}, f32[3,...) custom-call(bf16[9,160,640]{2,1,0:T(8,128)(2,1)} %get-tuple-element., ...), custom_call_target="tpu_custom_call" | custom-call | tf_op jit(solution)/shard_map/pallas_call | solution.py:758
  326.0 342.1 %shard_map.222 = (f32[9,160,640]{2,1,0:T(8,128)}, bf16[12,4,512,640]{3,2,1,0:T(8,128)(2,1)}, bf16[8,1280,512]{2,1,0:T(8,128)(2,1)}, bf16[8,1280,512]{2,1,0:T(8,1...) custom-call(bf16[9,2,2,4,2,160,640]{6,5,4,3,2,1,0:T(8,128)(2,1)} %ge, ...), custom_call_target="tpu_custom_call", output_to_operand_aliasing={{1}: (1, {}), {2}: (2, {})} | custom-call | tf_op jit(solution)/shard_map/pallas_call | solution.py:1568
  668.9 1.0 reshape.123
  670.8 3.3 all-to-all-start
  674.2 19.5 %shard_map.223 = (bf16[1,16,320,128]{3,2,1,0:T(8,128)(2,1)}, f32[1,16,320,128]{3,2,1,0:T(8,128)}, f32[320,1]{1,0:T(8,128)}, f32[320,1]{1,0:T(8,128)}, f32[160,32...) custom-call(bf16[4,512,320]{2,1,0:T(8,128)(2,1)} %get-tuple-element., ...), custom_call_target="tpu_custom_call" | custom-call | tf_op jit(solution)/shard_map/pallas_call | solution.py:1904
  693.7 1.1 reduce.1
  694.7 1.1 reduce.2
  696.0 2.0 collective-permute-start
  697.9 1.9 collective-permute-done
  699.8 2.6 collective-permute-start.1
  702.4 1.8 collective-permute-done.1
  704.2 2.5 collective-permute-start.2
  706.8 2.2 collective-permute-done.2
  (48 shorter events, 8.0 us)
Async XLA Ops:
  3.6 322.3 %copy-start.2 = (f32[320,1]{1,0:T(8,128)}, f32[320,1]{1,0:T(8,128)S(1)}, u32[]{:S(2)}) copy-start(f32[320,1]{1,0:T(8,128)S(1)} %copy.31.gain_ref) | copy-start | bytes 3844
  8.1 1.3 copy-start
  9.4 1.3 copy-start.1
  10.7 1.1 copy-start.3
  11.8 1.0 copy-start.4
  12.8 1.0 copy-start.5
  13.8 0.9 copy-start.6
  14.8 0.9 copy-start.9
  15.7 0.9 copy-start.10
  29.0 0.7 copy-start.7
  29.7 0.7 copy-start.8
  670.8 25.0 %all-to-all-start = ((f32[4,1,4480]{2,1,0:T(1,128)}), f32[4,1,4480]{2,1,0:T(1,128)S(1)}, u32[]{:S(2)}, u32[]{:S(2)}) async-start(f32[4,1,4480]{2,1,0:T(1,128)} %copy.35), calls=%async_computation | async-start | bytes 143360 | tf_op jit(solution)/shard_map/all_to_all | solution.py:1658
  696.0 3.8 collective-permute-start
  699.8 4.4 collective-permute-start.1
  704.2 4.7 collective-permute-start.2
